TPU v7x, 32 devices: a whole 2x2x4 slice. The times are simulated.
32 devices in a mesh: rows: 16 (over z, y, core), heads: 2 (over x).
Axes of the slice: x: 2, y: 2, z: 4, core: 2. Of those that a mesh axis runs over, the one named last changes fastest.
Arguments:
- tokens: bfloat16 [4096, 2048], P('rows', 'heads'), may hold values from -6 to 6
- cotangent: bfloat16 [4, 4096, 2048], P(None, 'rows', 'heads'), may hold values from -6 to 6
- doc_lengths: int32 [16], replicated, may hold values from 1 to 3976, as said below
- input_gain: float32 [2048], replicated, may hold values from 0.1 to 1.9
- input_weight: bfloat16 [2048, 32, 256], P('rows', None, 'heads'), may hold values from -0.125 to 0.125
- step_weight: bfloat16 [2048, 2, 32], P('rows', 'heads'), may hold values from -0.125 to 0.125
- state_weight: bfloat16 [2048, 256], replicated, may hold values from -0.125 to 0.125
- conv_inner: float32 [4, 4096], replicated, may hold values from -3 to 3
- conv_inner_bias: float32 [4096], replicated, may hold values from -1.5 to 1.5
- conv_state: float32 [4, 256], replicated, may hold values from -3 to 3
- conv_state_bias: float32 [256], replicated, may hold values from -1.5 to 1.5
- step_bias: float32 [64], replicated, may hold values from -12 to -3, as said below
- decay_log: float32 [64], replicated, may hold values from -6 to 1, as said below
- skip_gain: float32 [64], replicated, may hold values from 0.5 to 1.5
- gated_gain: float32 [4096], replicated, may hold values from 0.1 to 1.9
- output_weight: bfloat16 [32, 128, 2048], P(None, 'heads', 'rows'), may hold values from -0.125 to 0.125
Outputs:
- mixed: bfloat16 [4, 4096, 2048], P(None, 'rows', 'heads')
- tokens_grad: float32 [4096, 2048], P('rows', 'heads')
- input_gain_grad: float32 [2048], replicated
- input_weight_grad: float32 [2048, 32, 256], P('rows', None, 'heads')
- step_weight_grad: float32 [2048, 2, 32], P('rows', 'heads')
- state_weight_grad: float32 [2048, 256], replicated
- conv_inner_grad: float32 [4, 4096], replicated
- conv_inner_bias_grad: float32 [4096], replicated
- conv_state_grad: float32 [4, 256], replicated
- conv_state_bias_grad: float32 [256], replicated
- step_bias_grad: float32 [64], replicated
- decay_log_grad: float32 [64], replicated
- skip_gain_grad: float32 [64], replicated
- gated_gain_grad: float32 [4096], replicated
- output_weight_grad: float32 [32, 128, 2048], P(None, 'heads', 'rows')
Inputs may be any that keep to these rules, and one draw needn't show every extreme that they name: `doc_lengths`: the lengths add up to 4096. One document, at a place drawn from the seed, is exactly as long as the stated most; it starts among the first 256 tokens and ends among the last 256. Every other document has at most 16 tokens, and one of them has exactly 1. `step_bias`: A value for each head. `decay_log`: A value for each head.
All inputs are finite; a program needn't handle non-finite values.
Results may differ from a plain program's by a relative error of at most 0.011.
The roundings to bfloat16 on the way count: a program that leaves them out, or rounds other values in their place, can miss the bound.
Values may be sent and summed in bfloat16 or wider, within the bound.
No kernel may reach another device: no remote copies, remote signals or barrier semaphores. Data moves between devices by JAX's collectives and lax.ppermute only.
A program may use at most 256 MiB of HBM per device.

v0:
```python
from functools import partial

import jax
import jax.numpy as jnp
from jax import lax
from jax.sharding import PartitionSpec as P

D = 2048
P_SIZE = 64
STATE = 128
KERNEL = 4
SPAN = 256
INNER = 4096


eps = 1e-05
highest = lax.Precision.HIGHEST


def shifted(block, axis, distance):
    devices = range(lax.axis_size(axis))
    route = [(i - distance, i) for i in devices if i - distance in devices]
    return lax.ppermute(block, axis, route)


def prefix(part, axis, combine, identity, reverse):
    count = lax.axis_size(axis)
    place = lax.axis_index(axis)
    ahead = count - 1 - place if reverse else place
    gathered = jax.tree.map(lambda a: lax.all_gather(a, axis), part)
    state = jax.tree.map(lambda a, e: jnp.zeros_like(a) + jnp.asarray(e, a.dtype), part, identity)

    def one(step, state):
        source = count - 1 - step if reverse else step
        return combine(
            state, jax.tree.map(lambda a: lax.dynamic_index_in_dim(a, source, 0, False), gathered)
        )

    return lax.fori_loop(0, ahead, one, state)


def doc_matches(positions, starts, tap_count):
    doc_index = jnp.sum((positions[:, None] >= starts[None, :]).astype(jnp.int32), axis=1)
    row_count = positions.shape[0] - tap_count + 1
    compared = [
        (doc_index[offset : offset + row_count] == doc_index[tap_count - 1 :]).astype(jnp.float32)
        for offset in range(tap_count)
    ]
    return jnp.stack(compared)


def conv_apply(extended, kernel, bias_row, matches):
    row_count = matches.shape[1]
    summed = bias_row[None, :] + jnp.zeros((row_count, kernel.shape[1]), jnp.float32)
    for offset in range(kernel.shape[0]):
        summed = (
            summed
            + kernel[offset][None, :]
            * extended[offset : offset + row_count]
            * matches[offset][:, None]
        )
    return jax.nn.silu(summed)


def span_terms(inner_block, in_block, step_block, decay_block, reset_block):
    cumulative = jnp.cumsum(decay_block, axis=0)
    segment = jnp.cumsum(reset_block)
    to_end = jnp.where(
        (segment == segment[-1])[:, None], jnp.exp(cumulative[-1][None, :] - cumulative), 0.0
    )
    local_state = jnp.einsum(
        "jh,jh,jhp,jn->hpn", to_end, step_block, inner_block, in_block, precision=highest
    )
    span_decay = jnp.where(segment[-1] == 0, jnp.exp(cumulative[-1]), 0.0)
    return (local_state, span_decay)


def span_output(inner_block, in_block, out_block, step_block, decay_block, reset_block, entering):
    cumulative = jnp.cumsum(decay_block, axis=0)
    segment = jnp.cumsum(reset_block)
    position = jnp.arange(inner_block.shape[0])
    allowed = (segment[:, None] == segment[None, :]) & (position[:, None] >= position[None, :])
    spread = cumulative[:, None, :] - cumulative[None, :, :]
    weights = jnp.where(
        allowed[:, :, None], jnp.exp(jnp.where(allowed[:, :, None], spread, 0.0)), 0.0
    )
    scores = jnp.dot(out_block, in_block.T, precision=highest)
    within = jnp.einsum(
        "ijh,ij,jh,jhp->ihp", weights, scores, step_block, inner_block, precision=highest
    )
    entry_weight = jnp.where((segment == 0)[:, None], jnp.exp(cumulative), 0.0)
    carried = (
        jnp.einsum("in,hpn->ihp", out_block, entering, precision=highest) * entry_weight[:, :, None]
    )
    return within + carried


def to_blocks(values):
    span_total = values.shape[0] // SPAN
    return values.reshape((span_total, SPAN) + values.shape[1:])


def step_values(step_raw, step_shift, rate_log):
    step_size = jax.nn.softplus(step_raw + step_shift[None, :])
    return (step_size, -step_size * jnp.exp(rate_log)[None, :])


def state_piece(resets, inner_round, state_in, step_raw, step_shift, rate_log):
    step_size, decay = step_values(step_raw, step_shift, rate_log)
    local_states, span_decays = jax.vmap(span_terms)(
        to_blocks(inner_round),
        to_blocks(state_in),
        to_blocks(step_size),
        to_blocks(decay),
        to_blocks(resets),
    )

    def absorb(running, element):
        state_acc, decay_acc = running
        state_new, decay_new = element
        return ((decay_new[:, None, None] * state_acc + state_new, decay_acc * decay_new), None)

    initial = (jnp.zeros_like(local_states[0]), jnp.ones_like(span_decays[0]))
    (dev_state, dev_decay), unused = lax.scan(absorb, initial, (local_states, span_decays))
    return (local_states, span_decays, dev_state, dev_decay)


def output_piece(
    resets,
    inner_round,
    state_in,
    state_out,
    step_raw,
    step_shift,
    rate_log,
    skip_local,
    gate_wide,
    local_states,
    span_decays,
    incoming,
):
    step_size, decay = step_values(step_raw, step_shift, rate_log)

    def enter(state, element):
        state_new, decay_new = element
        return (decay_new[:, None, None] * state + state_new, state)

    unused, entering = lax.scan(enter, incoming, (local_states, span_decays))
    scanned = jax.vmap(span_output)(
        to_blocks(inner_round),
        to_blocks(state_in),
        to_blocks(state_out),
        to_blocks(step_size),
        to_blocks(decay),
        to_blocks(resets),
        entering,
    )
    scanned = scanned.reshape(inner_round.shape)
    return (scanned + skip_local[None, :, None] * inner_round) * jax.nn.silu(gate_wide)


def conv_piece(matches, ext_inner, ext_state, kernel_inner, bias_inner, kernel_state, bias_state):
    return (
        conv_apply(ext_inner, kernel_inner, bias_inner, matches),
        conv_apply(ext_state, kernel_state, bias_state, matches),
    )


def link_states(earlier, latter):
    decay_first, state_first = earlier
    decay_second, state_second = latter
    return (decay_first * decay_second, decay_second[:, None, None] * state_first + state_second)


def pick_heads(values, groups, head_count, head_index):
    shaped = values.reshape(values.shape[:-1] + (groups, head_count, -1))
    return lax.dynamic_index_in_dim(shaped, head_index, shaped.ndim - 2, keepdims=False)


def place_heads(local_part, head_count, head_index):
    shaped = jnp.expand_dims(local_part, local_part.ndim - 1)
    zero_fill = jnp.zeros(
        local_part.shape[:-1] + (head_count, local_part.shape[-1]), local_part.dtype
    )
    placed = lax.dynamic_update_slice_in_dim(zero_fill, shaped, head_index, local_part.ndim - 1)
    return placed.reshape(local_part.shape[:-2] + (-1,))


def contract(left_side, right_side, left_dim, right_dim):
    return lax.dot_general(
        left_side,
        right_side,
        (((left_dim,), (right_dim,)), ((), ())),
        preferred_element_type=jnp.float32,
    )


def shards(
    tokens,
    cotangent,
    doc_lengths,
    input_gain,
    input_weight,
    step_weight,
    state_weight,
    conv_inner,
    conv_inner_bias,
    conv_state,
    conv_state_bias,
    step_bias,
    decay_log,
    skip_gain,
    gated_gain,
    output_weight,
):
    head_count = lax.axis_size("heads")
    head_index = lax.axis_index("heads")
    row_index = lax.axis_index("rows")
    tok_rows, share_width = tokens.shape
    groups = input_weight.shape[1]
    local_width = groups * P_SIZE
    pad_rows = KERNEL - 1
    starts = jnp.cumsum(doc_lengths) - doc_lengths
    positions = row_index * tok_rows + jnp.arange(-pad_rows, tok_rows, dtype=jnp.int32)
    matches = doc_matches(positions, starts, KERNEL)
    resets = jnp.any(positions[pad_rows:, None] == starts[None, :], axis=1).astype(jnp.int32)
    kernel_inner = pick_heads(conv_inner, groups, head_count, head_index).reshape(
        KERNEL, local_width
    )
    bias_inner = pick_heads(conv_inner_bias, groups, head_count, head_index).reshape(local_width)
    gain_local = pick_heads(gated_gain, groups, head_count, head_index)
    step_shift = pick_heads(step_bias, groups, head_count, head_index).reshape(groups)
    rate_log = pick_heads(decay_log, groups, head_count, head_index).reshape(groups)
    skip_local = pick_heads(skip_gain, groups, head_count, head_index).reshape(groups)
    weight_in, weight_step, weight_out = (
        lax.all_gather(input_weight, "rows", axis=0, tiled=True),
        lax.all_gather(step_weight, "rows", axis=0, tiled=True),
        lax.all_gather(output_weight, "rows", axis=2, tiled=True),
    )
    gathered = lax.all_gather(tokens, "heads", axis=1, tiled=True)
    gathered_wide = gathered.astype(jnp.float32)
    inverse_norm = lax.rsqrt(jnp.mean(gathered_wide * gathered_wide, axis=1, keepdims=True) + eps)
    normed = (gathered_wide * inverse_norm * input_gain[None, :]).astype(jnp.bfloat16)
    projected = jnp.dot(
        normed, weight_in.reshape(D, groups * 2 * P_SIZE), preferred_element_type=jnp.float32
    )
    projected = projected.astype(jnp.bfloat16).reshape(tok_rows, groups, 2, P_SIZE)
    gate_z = projected[:, :, 0, :]
    inner_pre = projected[:, :, 1, :].reshape(tok_rows, local_width)
    step_raw = jnp.dot(normed, weight_step.reshape(D, groups), preferred_element_type=jnp.float32)
    state_pre = jnp.dot(normed, state_weight, preferred_element_type=jnp.float32).astype(
        jnp.bfloat16
    )
    rim_inner, rim_state = shifted(
        (inner_pre[tok_rows - pad_rows :], state_pre[tok_rows - pad_rows :]), "rows", 1
    )
    ext_inner = jnp.concatenate([rim_inner, inner_pre], axis=0).astype(jnp.float32)
    ext_state = jnp.concatenate([rim_state, state_pre], axis=0).astype(jnp.float32)
    (inner_conv, state_conv), conv_back = jax.vjp(
        partial(conv_piece, matches),
        ext_inner,
        ext_state,
        kernel_inner,
        bias_inner,
        conv_state,
        conv_state_bias,
    )
    inner_round = (
        lax.optimization_barrier(inner_conv.astype(jnp.bfloat16))
        .astype(jnp.float32)
        .reshape(tok_rows, groups, P_SIZE)
    )
    state_round = lax.optimization_barrier(state_conv.astype(jnp.bfloat16)).astype(jnp.float32)
    state_in = state_round[:, :STATE]
    state_out = state_round[:, STATE:]
    (local_states, span_decays, dev_state, dev_decay), states_back = jax.vjp(
        partial(state_piece, resets), inner_round, state_in, step_raw, step_shift, rate_log
    )
    identity = (jnp.ones_like(dev_decay), jnp.zeros_like(dev_state))
    incoming = prefix((dev_decay, dev_state), "rows", link_states, identity, False)[1]
    gated, output_back = jax.vjp(
        partial(output_piece, resets),
        inner_round,
        state_in,
        state_out,
        step_raw,
        step_shift,
        rate_log,
        skip_local,
        gate_z.astype(jnp.float32),
        local_states,
        span_decays,
        incoming,
    )
    squares = jnp.sum(gated * gated, axis=2)
    prefix_sums = jnp.stack(
        [jnp.sum(squares[:, : groups >> level_index], axis=1) for level_index in range(4)], axis=1
    )
    scaled_u = (gated * gain_local[None]).astype(jnp.bfloat16).reshape(tok_rows, local_width)
    widths = jnp.array([INNER >> level_index for level_index in range(4)], jnp.float32)
    bounds = [0, groups >> 3, groups >> 2, groups >> 1, groups]
    pieces = []
    for block_index in range(4):
        lower_group = bounds[block_index]
        upper_group = bounds[block_index + 1]
        pieces.append(
            jnp.dot(
                scaled_u[:, lower_group * P_SIZE : upper_group * P_SIZE],
                weight_out[lower_group:upper_group].reshape(-1, D),
                preferred_element_type=jnp.float32,
            )
        )
    blocks = jnp.stack(pieces)
    stat_copies = jnp.broadcast_to(prefix_sums[None], (head_count, tok_rows, 4))
    block_share, stat_share = (
        lax.psum_scatter(blocks, "heads", scatter_dimension=2, tiled=True),
        lax.psum_scatter(stat_copies, "heads", scatter_dimension=0, tiled=True),
    )
    scales = lax.rsqrt(stat_share[0] / widths[None, :] + eps)
    running = jnp.cumsum(block_share, axis=0)
    products = running[::-1]
    tokens_wide = tokens.astype(jnp.float32)
    mixed = (tokens_wide[None] + jnp.transpose(scales)[:, :, None] * products).astype(jnp.bfloat16)
    cot_wide = cotangent.astype(jnp.float32)
    resid_grad = jnp.sum(cot_wide, axis=0)
    cot_whole = lax.all_gather(cotangent, "heads", axis=2, tiled=True)
    dots_part = jnp.sum(cot_wide * products, axis=2)
    dot_totals = lax.psum(dots_part, "heads")
    total_grad = jnp.transpose(dot_totals) * -0.5 * scales * scales * scales / widths[None, :]
    scaled_grad = jnp.zeros((tok_rows, local_width), jnp.float32)
    out_weight_grad = jnp.zeros((groups * P_SIZE, D), jnp.float32)
    for level_index in range(4):
        kept_groups = groups >> level_index
        kept_width = kept_groups * P_SIZE
        product_grad = (
            scales[:, level_index : level_index + 1] * cot_whole[level_index].astype(jnp.float32)
        ).astype(jnp.bfloat16)
        u_part = contract(product_grad, weight_out[:kept_groups].reshape(kept_width, D), 1, 1)
        scaled_grad = scaled_grad + jnp.pad(u_part, ((0, 0), (0, local_width - kept_width)))
        weight_part = contract(scaled_u[:, :kept_width], product_grad, 0, 0)
        out_weight_grad = out_weight_grad + jnp.pad(
            weight_part, ((0, local_width - kept_width), (0, 0))
        )
    scaled_grad = scaled_grad.reshape(tok_rows, groups, P_SIZE)
    gain_local_grad = jnp.sum(scaled_grad * gated, axis=0)
    group_number = jnp.arange(groups)
    stat_factor = jnp.zeros((tok_rows, groups), jnp.float32)
    for level_index in range(4):
        inside = (group_number < groups >> level_index).astype(jnp.float32)
        stat_factor = stat_factor + total_grad[:, level_index : level_index + 1] * inside[None, :]
    gated_grad = scaled_grad * gain_local[None] + 2.0 * gated * stat_factor[:, :, None]
    (
        inner_grad_a,
        in_grad_a,
        out_grad_a,
        step_grad_a,
        shift_grad_a,
        rate_grad_a,
        skip_grad,
        gate_grad,
        local_states_grad,
        span_decays_grad,
        incoming_grad,
    ) = output_back(gated_grad)
    outgoing_grad = prefix((dev_decay, incoming_grad), "rows", link_states, identity, True)[1]
    dev_decay_grad = jnp.sum(outgoing_grad * incoming, axis=(1, 2))
    inner_grad_b, in_grad_b, step_grad_b, shift_grad_b, rate_grad_b = states_back(
        (local_states_grad, span_decays_grad, outgoing_grad, dev_decay_grad)
    )
    inner_act_grad = (inner_grad_a + inner_grad_b).reshape(tok_rows, local_width)
    state_act_grad = jnp.concatenate([in_grad_a + in_grad_b, out_grad_a], axis=1)
    (
        ext_inner_grad,
        ext_state_grad,
        kernel_inner_grad,
        bias_inner_grad,
        conv_state_grad,
        conv_state_bias_grad,
    ) = conv_back((inner_act_grad, state_act_grad))
    sent_inner, sent_state = shifted(
        (ext_inner_grad[:pad_rows], ext_state_grad[:pad_rows]), "rows", -1
    )
    inner_pre_grad = ext_inner_grad[pad_rows:] + jnp.pad(
        sent_inner, ((tok_rows - pad_rows, 0), (0, 0))
    )
    state_pre_grad = ext_state_grad[pad_rows:] + jnp.pad(
        sent_state, ((tok_rows - pad_rows, 0), (0, 0))
    )
    projection_grad = (
        jnp.stack([gate_grad, inner_pre_grad.reshape(tok_rows, groups, P_SIZE)], axis=2)
        .astype(jnp.bfloat16)
        .reshape(tok_rows, groups * 2 * P_SIZE)
    )
    step_grad = (step_grad_a + step_grad_b).astype(jnp.bfloat16)
    state_grad = state_pre_grad.astype(jnp.bfloat16)
    normed_grad = contract(projection_grad, weight_in.reshape(D, groups * 2 * P_SIZE), 1, 1)
    normed_grad = normed_grad + contract(step_grad, weight_step.reshape(D, groups), 1, 1)
    normed_grad = normed_grad + contract(state_grad, state_weight, 1, 1)
    input_weight_part = contract(normed, projection_grad, 0, 0).reshape(D, groups, 2 * P_SIZE)
    step_weight_part = contract(normed, step_grad, 0, 0).reshape(D, 1, groups)
    state_weight_part = contract(normed, state_grad, 0, 0)
    full_grad = lax.psum(normed_grad, "heads")
    unit_rows = gathered_wide * inverse_norm
    weighted = full_grad * input_gain[None, :]
    row_mean = jnp.mean(weighted * unit_rows, axis=1, keepdims=True)
    full_input_grad = inverse_norm * (weighted - unit_rows * row_mean)
    norm_part = lax.dynamic_slice_in_dim(full_input_grad, head_index * share_width, share_width, 1)
    gain_full = jnp.sum(full_grad * unit_rows, axis=0)
    column_owner = jnp.arange(D) // share_width
    gain_part = jnp.where(column_owner == head_index, gain_full, 0.0)
    tokens_grad = resid_grad + norm_part
    input_weight_grad, step_weight_grad, output_weight_grad = (
        lax.psum_scatter(input_weight_part, "rows", scatter_dimension=0, tiled=True),
        lax.psum_scatter(step_weight_part, "rows", scatter_dimension=0, tiled=True),
        lax.psum_scatter(
            out_weight_grad.reshape(groups, P_SIZE, D), "rows", scatter_dimension=2, tiled=True
        ),
    )
    conv_inner_part = place_heads(
        kernel_inner_grad.reshape(KERNEL, groups, P_SIZE), head_count, head_index
    )
    conv_bias_part = place_heads(bias_inner_grad.reshape(groups, P_SIZE), head_count, head_index)
    gated_gain_part = place_heads(gain_local_grad, head_count, head_index)
    step_bias_part = place_heads(
        (shift_grad_a + shift_grad_b).reshape(groups, 1), head_count, head_index
    )
    decay_log_part = place_heads(
        (rate_grad_a + rate_grad_b).reshape(groups, 1), head_count, head_index
    )
    skip_gain_part = place_heads(skip_grad.reshape(groups, 1), head_count, head_index)
    summed = lax.psum(
        (
            state_weight_part,
            conv_state_grad,
            conv_state_bias_grad,
            conv_inner_part,
            conv_bias_part,
            gated_gain_part,
            step_bias_part,
            decay_log_part,
            skip_gain_part,
            gain_part,
        ),
        ("rows", "heads"),
    )
    (
        state_weight_grad,
        conv_state_total,
        conv_state_bias_total,
        conv_inner_total,
        conv_bias_total,
        gated_gain_total,
        step_bias_total,
        decay_log_total,
        skip_gain_total,
        input_gain_grad,
    ) = summed
    return (
        mixed,
        tokens_grad,
        input_gain_grad,
        input_weight_grad,
        step_weight_grad,
        state_weight_grad,
        conv_inner_total,
        conv_bias_total,
        conv_state_total,
        conv_state_bias_total,
        step_bias_total,
        decay_log_total,
        skip_gain_total,
        gated_gain_total,
        output_weight_grad,
    )


def solution(mesh):
    placed = (
        P("rows", "heads"),
        P(None, "rows", "heads"),
        P(),
        P(),
        P("rows", None, "heads"),
        P("rows", "heads", None),
        P(),
        P(),
        P(),
        P(),
        P(),
        P(),
        P(),
        P(),
        P(),
        P(None, "heads", "rows"),
    )
    return jax.shard_map(
        shards,
        mesh=mesh,
        in_specs=placed,
        out_specs=(
            P(None, "rows", "heads"),
            P("rows", "heads"),
            P(),
            P("rows", None, "heads"),
            P("rows", "heads", None),
            P(),
            P(),
            P(),
            P(),
            P(),
            P(),
            P(),
            P(),
            P(),
            P(None, "heads", "rows"),
        ),
        check_vma=False,
    )
```

profile of v0, /device:TPU:0, one launch (start us, length us, event | category | flops | bytes accessed | tf_op | source)
XLA Modules:
  0.0 1700.2 jit_solution(15980174388720962809)
XLA Ops:
  17.5 23.4 %all_gather.30 = bf16[2048,1,32]{0,2,1:T(8,128)(2,1)S(1)} all-gather(bf16[128,1,32]{0,2,1:T(8,128)(2,1)S(1)} %copy-done.107), channel_id=1, replica_groups=mesh['rows'=16,'heads'=2] {'rows'}, dimensions={0}, use_global_device_ids=true | all-gather | bytes 139264 | tf_op jit(solution)/shard_map/all_gather | solution.py:237
  52.4 110.4 %all-gather.12.cloned.1.call-done = bf16[2048,32,128]{2,1,0:T(8,128)(2,1)} async-done(((bf16[128,32,128]{2,1,0:T(8,128)(2,1)}), bf16[2048,32,128]{2,1,0:T(8,128)(2,1)}) %all-gather.12.cloned.1.call-update) | async-done | bytes 16777232 | tf_op jit(solution)/shard_map/all_gather | solution.py:236
  162.8 12.7 fusion.16
  175.6 3.3 copy.149
  181.3 3.1 collective-permute-start
  190.3 3.0 multiply_convert_fusion.1
  195.6 3.4 fusion.84
  207.6 18.4 %all-gather = f32[16,1,32]{2,1,0:T(1,128)} all-gather(f32[1,1,32]{2,1,0:T(1,128)S(1)} %copy.157), channel_id=2, replica_groups=mesh['rows'=16,'heads'=2] {'rows'}, dimensions={0}, use_global_device_ids=true | all-gather | bytes 2176 | tf_op jit(solution)/shard_map/all_gather | solution.py:30
  229.1 12.3 all-gather.14.cloned.1.call-done
  241.4 3.1 fusion.209
  244.5 5.2 fusion.208
  250.8 3.8 fusion.207
  260.0 109.0 %all-gather.18.cloned.1.call-done = f32[512,64,128]{2,1,0:T(8,128)} async-done(((f32[32,64,128]{2,1,0:T(8,128)}), f32[512,64,128]{2,1,0:T(8,128)}) %all-gather.18.cloned.1.call-update) | async-done | bytes 16777232 | tf_op jit(solution)/shard_map/all_gather | solution.py:30
  372.6 13.9 multiply_reduce_fusion.10
  389.4 4.8 multiply_convert_fusion
  398.6 3.5 pad_maximum_fusion
  405.9 144.0 %reduce-scatter.5.cloned.1.call-done = f32[4,256,1024]{2,1,0:T(8,128)} async-done(((f32[4,256,2048]{2,1,0:T(8,128)}), f32[4,256,1024]{2,1,0:T(8,128)}) %reduce-scatter.5.cloned.1.call-update) | async-done | bytes 4194320 | tf_op jit(solution)/shard_map/reduce_scatter | solution.py:316
  555.2 7.4 all-reduce.29
  566.2 2.9 copy.165
  570.5 37.7 %all-gather.16.cloned.1.call-done = bf16[4,256,2048]{2,1,0:T(8,128)(2,1)} async-done(((bf16[4,256,1024]{2,1,0:T(8,128)(2,1)}), bf16[4,256,2048]{2,1,0:T(8,128)(2,1)}) %all-gather.16.cloned.1.call-update) | async-done | bytes 4194320 | tf_op jit(solution)/shard_map/all_gather | solution.py:326
  611.1 3.0 fusion.100
  614.1 3.9 fusion.105
  618.1 7.6 multiply_reduce_fusion.1
  628.7 3.7 add_multiply_fusion
  636.1 5.4 fusion.88
  641.6 13.7 fusion.20
  657.0 8.5 fusion.12
  670.1 92.8 %all-gather.20.cloned.1.call-done = f32[512,64,128]{2,1,0:T(8,128)} async-done(((f32[32,64,128]{2,1,0:T(8,128)}), f32[512,64,128]{2,1,0:T(8,128)}) %all-gather.20.cloned.1.call-update) | async-done | bytes 16777232 | tf_op jit(solution)/shard_map/all_gather | solution.py:30
  764.0 50.6 %while.17 = (s32[]{:T(128)}, f32[32,64,128]{2,1,0:T(8,128)}, s32[]{:T(128)}, f32[16,32]{1,0:T(8,128)}, f32[16,32,64,128]{3,2,1,0:T(8,128)}, /*index=5*/s32[]{:T(128)}, s32[]{:T(128)}, s32[]{:T(128)}, s32[]{:T(128)}) while((s32[]{:T(128)}, f32[32,64,128]{2,1,0:T(8,128)}, s32[]{:T(128)}, f32[16,32]{1,0:T(8,128)}, ...), condition=%wide.region_22.24_spmd, body=%wide.region_21.23_spmd.sunk | while | flops 524294 | bytes 3146267 | solution.py:39
  814.7 6.1 fusion.72
  826.6 5.3 multiply_reduce_fusion.5
  837.8 3.4 fusion.91
  852.3 3.8 reduce-window.56
  865.6 3.8 reduce-window.54
  885.9 18.2 %fusion = f32[256,2048]{1,0:T(8,128)} fusion(bf16[256,4096]{0,1:T(8,128)(2,1)S(1)} %bitcast.482, bf16[256,8,32,128]{3,2,1,0:T(8,128)(2,1)} %bitcast.546), kind=kOutput, calls=%fused_computation.4 | convolution fusion | flops 4294967296 | bytes 20971520 | tf_op jit(solution)/shard_map/dot_general | solution.py:190
  910.0 15.1 fusion.112
  932.1 7.2 pad_add_fusion
  941.9 4.0 add_convert_fusion
  955.3 16.6 all-reduce.33.cloned.1.call-done
  971.9 4.2 multiply_reduce_fusion.6
  976.1 40.7 %all-reduce.27 = (f32[2048]{0:T(1024)}, f32[4096]{0:T(1024)}, f32[4,256]{1,0:T(4,128)}, f32[256]{0:T(256)}, f32[64]{0:T(128)}, /*index=5*/f32[64]{0:T(128)}, f32[64]{0:T(128)}, f32[4096]{0:T(1024)}) all-reduce(f32[2048]{0:T(1024)S(1)} %fusion.186, f32[4096]{0:T(1024)S(1)} %reshape.1265, ...), channel_id=1, replica_groups=mesh['rows'=16,'heads'=2] {'rows','heads'}, use_global_device_ids=true, to_apply=%region_37.39 | all-reduce | flops 11712 | bytes 93696 | tf_op jit(solution)/shard_map/psum | solution.py:431
  1016.8 3.1 fusion.111
  1020.0 288.9 %reduce-scatter.7.cloned.1.call-done = f32[128,32,128]{2,0,1:T(8,128)} async-done(((f32[2048,32,128]{2,0,1:T(8,128)}), f32[128,32,128]{2,0,1:T(8,128)}) %reduce-scatter.7.cloned.1.call-update) | async-done | bytes 2097168 | tf_op jit(solution)/shard_map/reduce_scatter | solution.py:413
  1308.8 4.1 copy.189
  1313.0 178.1 %reduce-scatter.11.cloned.1.call-done = f32[32,64,128]{2,1,0:T(8,128)} async-done(((f32[32,64,2048]{2,1,0:T(8,128)}), f32[32,64,128]{2,1,0:T(8,128)}) %reduce-scatter.11.cloned.1.call-update) | async-done | bytes 1048592 | tf_op jit(solution)/shard_map/reduce_scatter | solution.py:415
  1491.0 58.4 %reduce-scatter.9.cloned.1.call-done = f32[128,1,32]{0,2,1:T(8,128)} async-done(((f32[2048,1,32]{0,2,1:T(8,128)}), f32[128,1,32]{0,2,1:T(8,128)}) %reduce-scatter.9.cloned.1.call-update) | async-done | bytes 16400 | tf_op jit(solution)/shard_map/reduce_scatter | solution.py:414
  1549.5 139.9 %all-reduce.35.cloned.1.call-done = (f32[2048,256]{1,0:T(8,128)}, f32[4,4096]{1,0:T(4,128)}) async-done(((f32[2048,256]{1,0:T(8,128)}, f32[4,4096]{1,0:T(4,128)}), (f32[2048,256]{1,0:T(8,128)}, f32[4,4096]{1,0:T(4,128)})) %all-reduce.35.cloned.1.call-update) | async-done | bytes 2162704 | tf_op jit(solution)/shard_map/psum | solution.py:431
  1689.4 3.1 copy.280
  (521 shorter events, 214.5 us)
Async XLA Ops:
  7.2 39.3 %copy-start = (bf16[2048,256]{1,0:T(8,128)(2,1)S(1)}, bf16[2048,256]{1,0:T(8,128)(2,1)}, u32[]{:S(2)}) copy-start(bf16[2048,256]{1,0:T(8,128)(2,1)} %param.28) | copy-start | bytes 3145732
  7.2 10.2 copy-start.107
  7.3 33.9 %copy-start.127 = (f32[4,256]{1,0:T(4,128)S(1)}, f32[4,256]{1,0:T(4,128)}, u32[]{:S(2)}) copy-start(f32[4,256]{1,0:T(4,128)} %param.31) | copy-start | bytes 12292
  7.3 35.7 %copy-start.59 = (f32[2048]{0:T(1024)S(1)}, f32[2048]{0:T(1024)}, u32[]{:S(2)}) copy-start(f32[2048]{0:T(1024)} %param.25) | copy-start | bytes 24580
  7.3 34.0 %all-gather.10.cloned.1.call-start = ((), (), s32[]{:S(2)}) async-start(), calls=%async_computation.4 | async-start | bytes 1572864 | tf_op jit(solution)/shard_map/all_gather | solution.py:240
  8.0 154.8 %all-gather.12.cloned.1.call-start = ((), (), s32[]{:S(2)}) async-start(), calls=%async_computation.5 | async-start | bytes 17825792 | tf_op jit(solution)/shard_map/all_gather | solution.py:236
  8.8 232.6 %all-gather.14.cloned.1.call-start = ((), (), s32[]{:S(2)}) async-start(), calls=%async_computation.6 | async-start | bytes 8912896 | tf_op jit(solution)/shard_map/all_gather | solution.py:238
  9.5 359.5 %all-gather.18.cloned.1.call-start = ((), (), s32[]{:S(2)}) async-start(), calls=%async_computation.13 | async-start | bytes 17825792 | tf_op jit(solution)/shard_map/all_gather | solution.py:30
  14.7 26.5 %copy-start.54 = (f32[32,2,1]{1,0,2:T(8,128)}, f32[32,2,1]{1,0,2:T(8,128)S(1)}, u32[]{:S(2)}) copy-start(f32[32,2,1]{1,0,2:T(8,128)S(1)} %reshape.1210) | copy-start | bytes 772
  17.5 28.8 %copy-start.116 = (f32[32]{0:T(128)}, f32[32]{0:T(128)S(1)}, u32[]{:S(2)}) copy-start(f32[32]{0:T(128)S(1)} %get-tuple-element.434) | copy-start | bytes 388
  41.1 9.6 copy-start.112
  41.2 10.2 copy-start.72
  41.2 10.2 copy-start.75
  41.2 10.2 copy-start.78
  41.2 10.2 copy-start.96
  41.2 10.2 copy-start.98
  41.3 10.2 copy-start.100
  41.3 10.2 copy-start.102
  42.9 119.9 %copy-start.91 = (f32[256]{0:T(256)}, f32[256]{0:T(256)S(1)}, u32[]{:S(2)}) copy-start(f32[256]{0:T(256)S(1)} %add_rsqrt_fusion) | copy-start | bytes 3076
  47.0 4.3 collective-permute-start.1
  50.7 112.1 %copy-start.110 = (f32[32]{0:T(128)}, f32[32]{0:T(128)S(1)}, u32[]{:S(2)}) copy-start(f32[32]{0:T(128)S(1)} %get-tuple-element.414) | copy-start | bytes 388
  50.8 144.7 %copy-start.41 = (f32[256,32]{0,1:T(8,128)}, f32[256,32]{0,1:T(8,128)S(1)}, u32[]{:S(2)}) copy-start(f32[256,32]{0,1:T(8,128)S(1)} %bitcast_multiply_fusion.6) | copy-start | bytes 98308
  181.3 7.3 collective-permute-start
  199.0 351.0 %reduce-scatter.5.cloned.1.call-start = ((), (), s32[]{:S(2)}) async-start(), calls=%async_computation.7 | async-start | bytes 12582912 | tf_op jit(solution)/shard_map/reduce_scatter | solution.py:316
  204.5 39.9 %copy-start.104 = (f32[32]{0:T(128)}, f32[32]{0:T(128)S(1)}, u32[]{:S(2)}) copy-start(f32[32]{0:T(128)S(1)} %dynamic-slice_reduce_fusion.4) | copy-start | bytes 388
  372.5 13.9 copy-start.22
  402.2 206.0 %all-gather.16.cloned.1.call-start = ((), (), s32[]{:S(2)}) async-start(), calls=%async_computation.8 | async-start | bytes 6291456 | tf_op jit(solution)/shard_map/all_gather | solution.py:326
  402.8 360.2 %all-gather.20.cloned.1.call-start = ((), (), s32[]{:S(2)}) async-start(), calls=%async_computation.14 | async-start | bytes 17825792 | tf_op jit(solution)/shard_map/all_gather | solution.py:30
  552.8 9.8 copy-start.136
  608.2 9.8 slice-start
  635.8 336.1 %all-reduce.33.cloned.1.call-start = ((), (), s32[]{:S(2)}) async-start(), calls=%async_computation.9 | async-start | bytes 4194304 | tf_op jit(solution)/shard_map/psum | solution.py:402
  641.6 14.4 copy-start.33
  641.6 15.3 copy-start.53
  657.0 8.5 copy-start.23
  657.0 8.5 copy-start.36
  657.0 8.5 copy-start.52
  764.0 50.7 %copy-start.42 = (f32[256,32]{0,1:T(8,128)S(1)}, f32[256,32]{0,1:T(8,128)}, u32[]{:S(2)}) copy-start(f32[256,32]{0,1:T(8,128)} %copy-done.41) | copy-start | bytes 98308
  842.8 38.1 %copy-start.20 = (f32[259,2048]{1,0:T(8,128)S(1)}, f32[259,2048]{1,0:T(8,128)}, u32[]{:S(2)}) copy-start(f32[259,2048]{1,0:T(8,128)} %pad_add_fusion.1) | copy-start | bytes 6365188
  843.5 37.4 %collective-permute-start.2 = (f32[3,2048]{1,0:T(4,128)}, f32[3,2048]{1,0:T(4,128)}, u32[]{:S(2)}, u32[]{:S(2)}) collective-permute-start(f32[3,2048]{1,0:T(4,128)} %pad_add_fusion.3), channel_id=1, source_target_pairs={{2,0},{4,2},{6,4},{8,6},{10,8},{12,10},{14,12},{16,14},{18,16},{20... | collective-permute-start | bytes 73736 | tf_op jit(solution)/shard_map/ppermute | solution.py:23
  877.6 28.7 %collective-permute-start.3 = (f32[3,256]{1,0:T(4,128)}, f32[3,256]{1,0:T(4,128)}, u32[]{:S(2)}, u32[]{:S(2)}) collective-permute-start(f32[3,256]{1,0:T(4,128)} %pad_add_fusion.5), channel_id=1, source_target_pairs={{2,0},{4,2},{6,4},{8,6},{10,8},{12,10},{14,12},{16,14},{18,16},{20... | collective-permute-start | bytes 9224 | tf_op jit(solution)/shard_map/ppermute | solution.py:23
  885.9 18.2 %copy-start.19 = (bf16[256,32,2,64]{0,3,2,1:T(8,128)(2,1)}, bf16[256,32,2,64]{0,3,2,1:T(8,128)(2,1)S(1)}, u32[]{:S(2)}) copy-start(bf16[256,32,2,64]{0,3,2,1:T(8,128)(2,1)S(1)} %copy.171) | copy-start | bytes 6291460
  908.8 400.1 %reduce-scatter.7.cloned.1.call-start = ((), (), s32[]{:S(2)}) async-start(), calls=%async_computation.10 | async-start | bytes 35651584 | tf_op jit(solution)/shard_map/reduce_scatter | solution.py:413
  925.1 565.9 %reduce-scatter.11.cloned.1.call-start = ((), (), s32[]{:S(2)}) async-start(), calls=%async_computation.12 | async-start | bytes 17825792 | tf_op jit(solution)/shard_map/reduce_scatter | solution.py:415
  939.3 610.1 %reduce-scatter.9.cloned.1.call-start = ((), (), s32[]{:S(2)}) async-start(), calls=%async_computation.11 | async-start | bytes 278528 | tf_op jit(solution)/shard_map/reduce_scatter | solution.py:414
  952.5 736.9 %all-reduce.35.cloned.1.call-start = ((), (), s32[]{:S(2)}) async-start(), calls=%async_computation.15 | async-start | bytes 4325376 | tf_op jit(solution)/shard_map/psum | solution.py:431
  955.3 20.8 %copy-start.117 = (f32[256]{0:T(256)S(1)}, f32[256]{0:T(256)}, u32[]{:S(2)}) copy-start(f32[256]{0:T(256)} %get-tuple-element.322) | copy-start | bytes 3076
  955.3 20.8 %copy-start.128 = (f32[64]{0:T(128)S(1)}, f32[64]{0:T(128)}, u32[]{:S(2)}) copy-start(f32[64]{0:T(128)} %reshape.1272) | copy-start | bytes 772
  955.3 61.6 %copy-start.28 = (f32[256,1024]{1,0:T(8,128)S(1)}, f32[256,1024]{1,0:T(8,128)}, u32[]{:S(2)}) copy-start(f32[256,1024]{1,0:T(8,128)} %get-tuple-element.308) | copy-start | bytes 3145732
  (107 other events, 411.9 us)
Sparse Core Ops, SparseCore 0:
  9.7 23.9 all-gather.9
  35.9 126.9 all-gather.11
  165.0 76.3 all-gather.13
  244.0 124.9 all-gather.17
  402.3 147.6 reduce-scatter.4
  551.4 56.7 all-gather.15
  635.9 126.9 all-gather.19
  908.9 62.9 all-reduce.32
  976.2 332.6 reduce-scatter.6
  1313.4 177.5 reduce-scatter.10
  1495.1 54.2 reduce-scatter.8
  1555.5 133.8 all-reduce.34
where the time goes:
time: 1710 us; the launch traced here: 1700 us
  waiting for transfers between devices  1190 us (70%)
  matrix products  152 us (9%)
  other arithmetic  128 us (7%)
  local copies, waits for them, and re-layouts  113 us (7%)
  blocking collectives  89.9 us (5%)
  between operations  17.5 us (1%)
    reduce_scatter x1, waiting for transfers between devices, shards(): lax.psum_scatter(input_weight_part, 'rows', scatter_dimension=0, tiled=True)  289 us
    all_gather x2, waiting for transfers between devices, prefix(): gathered = jax.tree.map(lambda a: lax.all_gather(a, axis), part)  202 us
    reduce_scatter x1, waiting for transfers between devices, shards(): lax.psum_scatter(out_weight_grad.reshape(groups, P_SIZE, D), 'rows', scat...  178 us
    reduce_scatter x1, waiting for transfers between devices, shards(): lax.psum_scatter(blocks, 'heads', scatter_dimension=2, tiled=True)  144 us
    psum x1, waiting for transfers between devices, shards(): lax.psum((state_weight_part, conv_state_grad, conv_state_bias_grad, conv_...  140 us
    all_gather x1, waiting for transfers between devices, shards(): lax.all_gather(input_weight, 'rows', axis=0, tiled=True)  110 us
    dot_general x14, matrix products, contract(): lax.dot_general(left_side, right_side, (((left_dim,), (right_dim,)), ((),...  71.7 us
    reduce_scatter x1, waiting for transfers between devices, shards(): lax.psum_scatter(step_weight_part, 'rows', scatter_dimension=0, tiled=True)  58.4 us
  transfers between devices with their start and end apart: 16, of which 11 were waited for; matrix products, arithmetic and copies ran while one was open for 14% of the time, Pallas kernels for 0%

commit v1 on v0

v1 whole, which is shorter than its diff:
```python
from functools import partial

import jax
import jax.numpy as jnp
from jax import lax
from jax.experimental import pallas as pl
from jax.experimental.pallas import tpu as pltpu
from jax.sharding import Mesh
from jax.sharding import PartitionSpec as P

D = 2048
P_SIZE = 64
STATE = 128
KERNEL = 4
INNER = 4096
CHUNK = 128
PLANE = 4

HALF_TOP = 16384.0

eps = 1e-05
bf16 = jnp.bfloat16
f32 = jnp.float32
high = lax.Precision.HIGHEST
PARAMS = pltpu.CompilerParams(
    vmem_limit_bytes=48 * 1024 * 1024, dimension_semantics=("arbitrary",)
)


def swap(block, axis, bit):
    return lax.ppermute(block, axis, [(a, a ^ bit) for a in range(lax.axis_size(axis))])


def shifted(block, axis, distance):
    devices = range(lax.axis_size(axis))
    route = [(a - distance, a) for a in devices if a - distance in devices]
    return lax.ppermute(block, axis, route)


def bits_of(axis):
    count = lax.axis_size(axis)
    return [1 << b for b in range(count.bit_length() - 1)]


def take(values, index, axis=0):
    return lax.dynamic_index_in_dim(values, index, axis, keepdims=False)


def put(buffer, piece, index):
    return lax.dynamic_update_index_in_dim(buffer, piece, index, 0)


def add_all(value, axes):
    for axis in axes:
        for bit in bits_of(axis):
            value = value + swap(value, axis, bit)
    return value


def stack_all(value, axes):
    whole = value[None]
    for axis in reversed(axes):
        place = lax.axis_index(axis)
        for bit in bits_of(axis):
            other = swap(whole, axis, bit)
            upper = (place & bit) != 0
            whole = jnp.where(
                upper,
                jnp.concatenate([other, whole], axis=0),
                jnp.concatenate([whole, other], axis=0),
            )
    return whole


def gather_inner(block):
    place = lax.axis_index("i")
    core = swap(block, "i", 1)
    across = swap(block, "i", 2)
    both = swap(across, "i", 1)
    out = jnp.zeros((PLANE,) + block.shape, block.dtype)
    for bit, piece in ((0, block), (1, core), (2, across), (3, both)):
        out = put(out, piece, place ^ bit)
    return out


def exchange_inner(blocks):
    place = lax.axis_index("i")
    out = blocks
    for bit in range(1, PLANE):
        out = put(out, swap(take(blocks, place ^ bit), "i", bit), place ^ bit)
    return out


def scatter_inner(parts):
    place = lax.axis_index("i")
    core, row = place & 1, place >> 1
    shaped = parts.reshape((2, 2) + parts.shape[1:])
    got = swap(take(shaped, 1 - core, 1).astype(bf16), "i", 1)
    half = take(shaped, core, 1) + got.astype(f32)
    got = swap(take(half, 1 - row).astype(bf16), "i", 2)
    return take(half, row) + got.astype(f32)


def gather_heads(block, axis):
    if lax.axis_size("h") != 2:
        return lax.all_gather(block, "h", axis=axis, tiled=True)
    other = swap(block, "h", 1)
    upper = lax.axis_index("h") != 0
    return jnp.where(
        upper,
        jnp.concatenate([other, block], axis=axis),
        jnp.concatenate([block, other], axis=axis),
    )


def scatter_heads(values, axis):
    count = lax.axis_size("h")
    if count != 2:
        return lax.psum_scatter(values, "h", scatter_dimension=axis, tiled=True)
    place = lax.axis_index("h")
    width = values.shape[axis] // 2
    sent = lax.dynamic_slice_in_dim(values, (1 - place) * width, width, axis)
    kept = lax.dynamic_slice_in_dim(values, place * width, width, axis)
    return kept + swap(sent.astype(bf16), "h", 1).astype(f32)


def to_half(values, largest):
    safe = jnp.maximum(largest, 1e-30)
    return (values * (HALF_TOP / safe)).astype(jnp.float16)


def from_half(values, largest):
    return values.astype(f32) * (jnp.maximum(largest, 1e-30) / HALF_TOP)


def chain(state, decay_wide, direction):
    count = lax.axis_size("o")
    largest = jnp.max(jnp.abs(state), axis=0, keepdims=True)
    sent = to_half(state, largest)
    rows = jnp.concatenate([largest, decay_wide, jnp.zeros((6, state.shape[1]), f32)], axis=0)
    total = None
    for distance in range(count - 1, 0, -1):
        got = shifted(rows, "o", direction * distance)
        own = from_half(shifted(sent, "o", direction * distance), got[0:1])
        total = own if total is None else own + got[1:2] * total
    return total


def mm(a, b):
    return jnp.dot(a, b, preferred_element_type=f32)


def mm_two(a, b):
    upper, lower = split_two(b)
    return mm(a, upper) + mm(a, lower)


def mm_three(a, b):
    a_up, a_low = split_two(a)
    b_up, b_low = split_two(b)
    return mm_t(a_up, b_up) + mm_t(a_up, b_low) + mm_t(a_low, b_up)


def mm_t(a, b):
    return lax.dot_general(a, b, (((1,), (1,)), ((), ())), preferred_element_type=f32)


def t_mm(a, b):
    return lax.dot_general(a, b, (((0,), (0,)), ((), ())), preferred_element_type=f32)


def head_mask(groups, width):
    head = lax.broadcasted_iota(jnp.int32, (groups, width), 0)
    lane = lax.broadcasted_iota(jnp.int32, (groups, width), 1)
    return (lane // P_SIZE == head).astype(f32).astype(bf16)


def split_two(values):
    upper = values.astype(bf16)
    return upper, (values - upper.astype(f32)).astype(bf16)


def widen(values, mask):
    upper, lower = split_two(values)
    return mm(upper, mask) + mm(lower, mask)


def fold(values, mask):
    upper, lower = split_two(values)
    return mm_t(upper, mask) + mm_t(lower, mask)


def pair_masks():
    lane = lax.broadcasted_iota(jnp.int32, (1, 2 * P_SIZE), 1)
    lower = (lane < P_SIZE).astype(f32)
    return lower.astype(bf16), (1.0 - lower).astype(bf16)


def rows_cols():
    row = lax.broadcasted_iota(jnp.int32, (CHUNK, CHUNK), 0)
    col = lax.broadcasted_iota(jnp.int32, (CHUNK, CHUNK), 1)
    return row, col


def within_kernel(groups, x_ref, st_ref, col_ref, row_ref, y_ref):
    b_in = st_ref[:, :STATE]
    c_out = st_ref[:, STATE:]
    scores = mm_t(c_out, b_in)
    doc_col = col_ref[:, 3 * groups : 3 * groups + 1]
    doc_row = row_ref[2 * groups : 2 * groups + 1, :]
    row, col = rows_cols()
    bias = jnp.where((doc_col == doc_row) & (row >= col), 0.0, -1e30)
    masks = pair_masks()
    for pair in range(groups // 2):
        lanes = slice(pair * 2 * P_SIZE, (pair + 1) * 2 * P_SIZE)
        x_pair = x_ref[:, lanes]
        weights, values = [], []
        for side in range(2):
            h = 2 * pair + side
            spread = jnp.exp(col_ref[:, h : h + 1] - row_ref[h : h + 1, :] + bias)
            weights.append(split_two(scores * spread * row_ref[groups + h : groups + h + 1, :]))
            values.append(x_pair * masks[side])
        value = jnp.concatenate(values, axis=0)
        y_ref[:, lanes] = mm(
            jnp.concatenate([weights[0][0], weights[1][0]], axis=1), value
        ) + mm(jnp.concatenate([weights[0][1], weights[1][1]], axis=1), value)


def carry_kernel(
    groups,
    x_ref,
    st_ref,
    stt_ref,
    col_ref,
    yl_ref,
    gz_ref,
    inc_ref,
    wide_ref,
    level_ref,
    v_ref,
    u_ref,
    sq_ref,
    enter_ref,
    state,
):
    @pl.when(pl.program_id(0) == 0)
    def _():
        state[...] = inc_ref[...]

    width = x_ref.shape[1]
    mask = head_mask(groups, width)
    cum = col_ref[:, :groups]
    step = col_ref[:, groups : 2 * groups]
    from_start = col_ref[:, 3 * groups + 1 : 3 * groups + 2]
    to_end = col_ref[:, 3 * groups + 2 : 3 * groups + 3]
    cum_last = cum[CHUNK - 1 : CHUNK, :]
    entry = jnp.exp(cum) * from_start
    ending = jnp.exp(cum_last - cum) * to_end * step
    entry_wide = widen(entry, mask)
    ending_wide = widen(ending, mask)
    held = state[...]
    enter_ref[...] = held
    carried = mm_two(st_ref[:, STATE:], held)
    x_wide = x_ref[...].astype(f32)
    v = yl_ref[...] + entry_wide * carried + wide_ref[0:1, :] * x_wide
    v_ref[...] = v
    z = gz_ref[...].astype(f32)
    gated = v * (z * jax.nn.sigmoid(z))
    u_ref[...] = (gated * wide_ref[1:2, :]).astype(bf16)
    upper, lower = split_two(gated * gated)
    sq_ref[...] = mm_t(level_ref[...], upper) + mm_t(level_ref[...], lower)
    added = mm_two(stt_ref[:STATE, :], x_wide * ending_wide)
    state[...] = entry_wide[CHUNK - 1 : CHUNK, :] * held + added


def gate_back_kernel(
    groups,
    ug_ref,
    v_ref,
    gz_ref,
    x_ref,
    stt_ref,
    col_ref,
    stat_ref,
    wide_ref,
    level_ref,
    yg_ref,
    zg_ref,
    acc_ref,
    lam_ref,
):
    @pl.when(pl.program_id(0) == 0)
    def _():
        acc_ref[...] = jnp.zeros_like(acc_ref)
        lam_ref[...] = jnp.zeros_like(lam_ref)

    mask = head_mask(groups, x_ref.shape[1])
    v = v_ref[...]
    z = gz_ref[...].astype(f32)
    sig = jax.nn.sigmoid(z)
    silu = z * sig
    gated = v * silu
    ug = ug_ref[...]
    upper, lower = split_two(stat_ref[...])
    stat = t_mm(upper, level_ref[...]) + t_mm(lower, level_ref[...])
    gated_grad = ug * wide_ref[1:2, :] + 2.0 * gated * stat
    y_grad = gated_grad * silu
    yg_ref[...] = y_grad
    zg_ref[...] = (gated_grad * v * (sig * (1.0 + z * (1.0 - sig)))).astype(bf16)
    acc_ref[0:1, :] += jnp.sum(ug * gated, axis=0, keepdims=True)
    acc_ref[1:2, :] += jnp.sum(y_grad * x_ref[...].astype(f32), axis=0, keepdims=True)
    whole_entry = widen(col_ref[:, 2 * groups : 3 * groups], mask)
    lam_ref[...] += mm_two(stt_ref[STATE:, :], y_grad * whole_entry)


def within_back_kernel(groups, x_ref, st_ref, col_ref, row_ref, yg_ref, dx_ref, dbc_ref, ds_ref):
    b_in = st_ref[:, :STATE]
    c_out = st_ref[:, STATE:]
    scores = mm_t(b_in, c_out)
    doc_col = col_ref[:, 3 * groups : 3 * groups + 1]
    doc_row = row_ref[2 * groups : 2 * groups + 1, :]
    row, col = rows_cols()
    same = doc_col == doc_row
    bias = jnp.where(same & (row <= col), 0.0, -1e30)
    masks = pair_masks()
    total = jnp.zeros((CHUNK, CHUNK), f32)
    head_lane = lax.broadcasted_iota(jnp.int32, (CHUNK, groups), 1)
    head_row = lax.broadcasted_iota(jnp.int32, (groups, CHUNK), 0)
    size_part = jnp.zeros((CHUNK, groups), f32)
    out_part = jnp.zeros((groups, CHUNK), f32)
    for pair in range(groups // 2):
        lanes = slice(pair * 2 * P_SIZE, (pair + 1) * 2 * P_SIZE)
        x_pair = x_ref[:, lanes]
        y_pair, y_rest = split_two(yg_ref[:, lanes])
        weights, values = [], []
        for side in range(2):
            h = 2 * pair + side
            step = col_ref[:, groups + h : groups + h + 1]
            spread = jnp.exp(row_ref[h : h + 1, :] - col_ref[:, h : h + 1] + bias)
            y_side = y_pair * masks[side]
            paired = spread * (mm_t(x_pair, y_side) + mm_t(x_pair, y_rest * masks[side]))
            total = total + step * paired
            product = scores * paired
            size_part = jnp.where(
                head_lane == h, jnp.sum(product, axis=1, keepdims=True), size_part
            )
            out_part = jnp.where(
                head_row == h, jnp.sum(step * product, axis=0, keepdims=True), out_part
            )
            weights.append((scores * spread).astype(bf16))
            values.append(y_side)
        dx_ref[:, lanes] = mm(jnp.concatenate(weights, axis=1), jnp.concatenate(values, axis=0))
    upper, lower = split_two(total)
    dbc_ref[:, :STATE] = mm(upper, c_out) + mm(lower, c_out)
    dbc_ref[:, STATE:] = t_mm(upper, b_in) + t_mm(lower, b_in)
    later = (same & (row <= col)).astype(f32)
    step_all = col_ref[:, groups : 2 * groups]
    ds_ref[:, :groups] = size_part
    ds_ref[:, groups:] = lax.dot_general(
        later, out_part, (((1,), (1,)), ((), ())), precision=high, preferred_element_type=f32
    ) - jnp.dot(later, step_all * size_part, precision=high, preferred_element_type=f32)


def conv_back_step(act_grad, pre, value, taps_ref, match, next_ref, sum_ref):
    sig = jax.nn.sigmoid(pre)
    slope = act_grad * (sig * (1.0 + pre * (1.0 - sig)))
    sum_ref[4:5, :] += jnp.sum(slope, axis=0, keepdims=True)
    sum_ref[3:4, :] += jnp.sum(slope * value, axis=0, keepdims=True)
    grad = taps_ref[3:4, :] * slope
    row = lax.broadcasted_iota(jnp.int32, (8, pre.shape[1]), 0)
    for k in range(KERNEL - 1):
        reach = KERNEL - 1 - k
        rolled = pltpu.roll(slope * match[k], CHUNK - reach, 0)
        last = rolled[CHUNK - 8 :]
        keep = row < 8 - reach
        after = next_ref[k * 8 : k * 8 + 8, :]
        moved = jnp.concatenate([rolled[: CHUNK - 8], jnp.where(keep, last, after)], axis=0)
        next_ref[k * 8 : k * 8 + 8, :] = jnp.where(keep, 0.0, last)
        grad = grad + taps_ref[k : k + 1, :] * moved
        sum_ref[k : k + 1, :] += jnp.sum(value * moved, axis=0, keepdims=True)
    return grad


def conv_back_edge(halo_ref, taps_ref, next_ref, sum_ref, edge_ref):
    value = halo_ref[...].astype(f32)[8:]
    edge = 0.0
    for k in range(KERNEL - 1):
        after = next_ref[k * 8 : k * 8 + 8, :]
        edge = edge + taps_ref[k : k + 1, :] * after
        sum_ref[k : k + 1, :] += jnp.sum(value * after, axis=0, keepdims=True)
    edge_ref[...] = edge


def carry_back_kernel(
    groups,
    x_ref,
    st_ref,
    stt_ref,
    col_ref,
    row_ref,
    yg_ref,
    dxl_ref,
    dbcl_ref,
    dsl_ref,
    enter_ref,
    lam_ref,
    wide_ref,
    pre_ref,
    value_ref,
    halo_ref,
    taps_ref,
    pre_state_ref,
    value_state_ref,
    halo_state_ref,
    taps_state_ref,
    grad_ref,
    tail_ref,
    edge_ref,
    sum_ref,
    grad_state_ref,
    edge_state_ref,
    sum_state_ref,
    ds_ref,
    adjoint,
    next_ref,
    next_state_ref,
):
    step_index = pl.program_id(0)

    @pl.when(step_index == 0)
    def _():
        adjoint[...] = lam_ref[...]
        next_ref[...] = jnp.zeros_like(next_ref)
        next_state_ref[...] = jnp.zeros_like(next_state_ref)
        sum_ref[...] = jnp.zeros_like(sum_ref)
        sum_state_ref[...] = jnp.zeros_like(sum_state_ref)

    width = x_ref.shape[1]
    mask = head_mask(groups, width)
    cum = col_ref[:, :groups]
    step = col_ref[:, groups : 2 * groups]
    from_start = col_ref[:, 3 * groups + 1 : 3 * groups + 2]
    to_end = col_ref[:, 3 * groups + 2 : 3 * groups + 3]
    inside = col_ref[:, 3 * groups + 3 : 3 * groups + 4]
    match = [col_ref[:, 3 * groups + 4 + k : 3 * groups + 5 + k] for k in range(KERNEL - 1)]
    cum_last = cum[CHUNK - 1 : CHUNK, :]
    entry = jnp.exp(cum) * from_start
    ending = jnp.exp(cum_last - cum) * to_end
    entry_wide = widen(entry, mask)
    ending_wide = widen(ending, mask)
    step_wide = widen(step, mask)
    y_grad = yg_ref[...]
    entered = enter_ref[...]
    held = adjoint[...]
    y_entry = y_grad * entry_wide
    out_grad = dbcl_ref[:, STATE:] + mm_three(y_entry, entered)
    out_carry = fold(y_entry * mm_two(st_ref[:, STATE:], entered), mask)
    x_wide = x_ref[...].astype(f32)
    back = ending_wide * mm_two(st_ref[:, :STATE], held)
    act_grad = step_wide * (dxl_ref[...] + back) + wide_ref[0:1, :] * y_grad
    in_grad = dbcl_ref[:, :STATE] + mm_three(x_wide * ending_wide * step_wide, held)
    size_carry = fold(x_wide * back, mask)
    both = jnp.sum(held * entered, axis=0, keepdims=True)
    crossing = fold(jnp.broadcast_to(both, (8, width)), mask)[0:1, :] * entry[CHUNK - 1 : CHUNK, :]
    doc_col = col_ref[:, 3 * groups : 3 * groups + 1]
    doc_row = row_ref[2 * groups : 2 * groups + 1, :]
    row, col = rows_cols()
    same = doc_col == doc_row
    later = (same & (row <= col)).astype(f32)
    earlier = (same & (row > col)).astype(f32)
    decayed = (
        dsl_ref[:, groups:]
        + jnp.dot(later, out_carry, precision=high, preferred_element_type=f32)
        + jnp.dot(earlier, step * size_carry, precision=high, preferred_element_type=f32)
        + crossing
    )
    ds_ref[:, :groups] = dsl_ref[:, :groups] + size_carry
    ds_ref[:, groups:] = decayed * inside
    adjoint[...] = entry_wide[CHUNK - 1 : CHUNK, :] * held + mm_two(stt_ref[STATE:, :], y_entry)

    grad = conv_back_step(
        act_grad, pre_ref[...], value_ref[...].astype(f32), taps_ref, match, next_ref, sum_ref
    )
    grad_ref[...] = grad.astype(bf16)
    grad_state_ref[...] = conv_back_step(
        jnp.concatenate([in_grad, out_grad], axis=1),
        pre_state_ref[...],
        value_state_ref[...].astype(f32),
        taps_state_ref,
        match,
        next_state_ref,
        sum_state_ref,
    )

    @pl.when(step_index == 0)
    def _():
        tail_ref[...] = grad[CHUNK - 16 :]

    @pl.when(step_index == pl.num_programs(0) - 1)
    def _():
        conv_back_edge(halo_ref, taps_ref, next_ref, sum_ref, edge_ref)
        conv_back_edge(halo_state_ref, taps_state_ref, next_state_ref, sum_state_ref, edge_state_ref)


def norm_kernel(count, cols, planes_each, place_ref, gain_ref, *refs):
    pieces = refs[: PLANE * count]
    out_ref, share_ref = refs[PLANE * count :]
    place = place_ref[0]
    head = place_ref[1]
    share = pieces[0].shape[1]
    for r in range(PLANE):

        @pl.when(pl.program_id(0) == r)
        def _():
            wide = [pieces[r * count + q][...].astype(f32) for q in range(count)]
            total = 0.0
            for q in range(count):
                total = total + jnp.sum(wide[q] * wide[q], axis=1, keepdims=True)
            inverse = lax.rsqrt(total / D + eps)
            for q in range(count):
                lanes = pl.ds(pl.multiple_of((head ^ q) * share, 128), share)
                out_ref[:, lanes] = (wide[q] * inverse * gain_ref[:, lanes]).astype(bf16)
            for t in range(PLANE):

                @pl.when(place == t)
                def _():
                    for z in range(planes_each):
                        share_ref[0, :, z * cols : (z + 1) * cols] = pieces[r * count][
                            :, (z * PLANE + t) * cols : (z * PLANE + t + 1) * cols
                        ]


def project_kernel(
    groups,
    normed_ref,
    halo_ref,
    weight_ref,
    stt_ref,
    col_ref,
    taps_ref,
    value_ref,
    pre_ref,
    x_ref,
    state_ref,
    halo_out_ref,
    last_ref,
):
    @pl.when(pl.program_id(0) == 0)
    def _():
        halo = mm(halo_ref[...], weight_ref[...]).astype(bf16)
        halo_out_ref[...] = halo
        last_ref[...] = halo.astype(f32)[8:]
        state_ref[...] = jnp.zeros_like(state_ref)

    width = x_ref.shape[1]
    rows = x_ref.shape[0]
    value_low = mm(normed_ref[...], weight_ref[...]).astype(bf16)
    value_ref[...] = value_low
    value = value_low.astype(f32)
    row = lax.broadcasted_iota(jnp.int32, (8, width), 0)
    last = last_ref[...]
    pre = taps_ref[4:5, :] + taps_ref[3:4, :] * value
    for k in range(KERNEL - 1):
        reach = KERNEL - 1 - k
        rolled = pltpu.roll(value, reach, 0)
        top = jnp.where(row < reach, pltpu.roll(last, reach, 0), rolled[:8])
        moved = jnp.concatenate([top, rolled[8:]], axis=0)
        pre = pre + taps_ref[k : k + 1, :] * moved * col_ref[:, 3 * groups + 4 + k : 3 * groups + 5 + k]
    last_ref[...] = value[rows - 8 :]
    pre_ref[...] = pre
    x_low = (pre * jax.nn.sigmoid(pre)).astype(bf16)
    x_ref[...] = x_low
    ending = widen(col_ref[:, 3 * groups + 7 : 4 * groups + 7], head_mask(groups, width))
    state_ref[...] += mm_two(stt_ref[:STATE, :], x_low.astype(f32) * ending)


def normed_back_kernel(z_ref, inner_ref, step_ref, state_ref, wg_ref, wi_ref, ws_ref, wt_ref, *out_refs):
    total = (
        mm_t(z_ref[...], wg_ref[...])
        + mm_t(inner_ref[...], wi_ref[...])
        + mm_t(step_ref[...], ws_ref[...])
        + mm_t(state_ref[...], wt_ref[...])
    )
    for r in range(PLANE):

        @pl.when(pl.program_id(0) == r)
        def _():
            out_refs[r][...] = total.astype(out_refs[r].dtype)


def level_of(place, half):
    return jnp.where(place == 0, 3 - half, jnp.where(place == 1, 1, 0))


def split_kernel(count, cols, place_ref, whole_ref, *out_refs):
    place = place_ref[0]
    for r in range(PLANE):
        for t in range(PLANE):

            @pl.when(place == t ^ r)
            def _():
                for z in range(count):
                    out_refs[r][0, :, z * cols : (z + 1) * cols] = whole_ref[
                        0, :, (z * PLANE + t) * cols : (z * PLANE + t + 1) * cols
                    ]


def join_kernel(count, cols, place_ref, *refs):
    place = place_ref[0]
    out_ref = refs[PLANE]
    for r in range(PLANE):
        for t in range(PLANE):

            @pl.when(place == t ^ r)
            def _():
                for z in range(count):
                    out_ref[0, :, (z * PLANE + t) * cols : (z * PLANE + t + 1) * cols] = refs[r][
                        0, :, z * cols : (z + 1) * cols
                    ]


def out_back_kernel(count, place_ref, scale_ref, weight_ref, *refs):
    cot_refs = refs[:count]
    part_refs = refs[count : count + PLANE]
    sum_ref = refs[count + PLANE]
    top_ref = refs[count + PLANE + 1]
    low_ref = refs[count + PLANE + 2]
    place = place_ref[0]

    @pl.when(pl.program_id(0) == 0)
    def _():
        top_ref[...] = jnp.zeros_like(top_ref)

    half = cot_refs[0].shape[3]
    for q in range(count):
        lanes = slice(q * half, (q + 1) * half)
        total = None
        for m in range(4):
            grad = (scale_ref[:, m : m + 1] * cot_refs[q][0, m].astype(f32)).astype(bf16)
            total = grad.astype(f32) if m == 0 else total + grad.astype(f32)
            upper, lower = split_two(total)
            sum_ref[m, :, lanes] = upper
            low_ref[m, :, lanes] = lower
    rows = weight_ref.shape[2] // 2
    for r in range(PLANE):
        owner = place ^ r
        for side in range(2):
            level = level_of(owner, side)
            span = slice(side * rows, (side + 1) * rows)
            weight = weight_ref[owner, :, span]
            part = mm(sum_ref[level], weight)
            out_ref = part_refs[r]

            @pl.when(owner < 2)
            def _():
                out_ref[:, span] = (part + mm(low_ref[level], weight)).astype(out_ref.dtype)

            @pl.when(owner >= 2)
            def _():
                out_ref[:, span] = part.astype(out_ref.dtype)

        if r % 2 == 0 or r == 3:
            bound = jnp.max(jnp.abs(out_ref[...]), axis=0, keepdims=True)
            top_ref[r : r + 1, :] = jnp.maximum(top_ref[r : r + 1, :], bound)


def product_kernel(count, place_ref, weight_ref, *refs):
    u_refs = refs[:PLANE]
    cot_refs = refs[PLANE : PLANE + count]
    dot_ref, own_ref = refs[PLANE + count : PLANE + count + 2]
    send_refs = refs[PLANE + count + 2 : PLANE + 2 * count + 1]
    block_ref = refs[PLANE + 2 * count + 1]
    place = place_ref[0]
    half = cot_refs[0].shape[3]
    rows = weight_ref.shape[1] // 2
    block_ref[...] = jnp.zeros_like(block_ref)
    for r in range(PLANE):
        owner = place ^ r
        for side in range(2):
            span = slice(side * rows, (side + 1) * rows)
            block_ref[level_of(owner, side)] += mm(u_refs[r][:, span], weight_ref[owner, span, :])
    running = None
    ones = jnp.ones((8, half), bf16)
    dot_ref[4:8, :] = jnp.zeros((4, dot_ref.shape[1]), f32)
    for m in (3, 2, 1, 0):
        running = block_ref[m] if running is None else running + block_ref[m]
        dots = 0.0
        for q in range(count):
            part = running[:, q * half : (q + 1) * half]
            dots = dots + cot_refs[q][0, m].astype(f32) * part
            if q == 0:
                own_ref[0, m] = part
            else:
                send_refs[q - 1][0, m] = part.astype(bf16)
        upper, lower = split_two(dots)
        dot_ref[m : m + 1, :] = (mm_t(ones, upper) + mm_t(ones, lower))[0:1, :]


def mix_kernel(count, scale_ref, tok_ref, own_ref, *refs):
    got_refs = refs[: count - 1]
    out_refs = refs[count - 1 :]
    for r in range(PLANE):

        @pl.when(pl.program_id(0) == r)
        def _():
            for m in range(4):
                total = own_ref[0, m]
                for got in got_refs:
                    total = total + got[0, m].astype(f32)
                out_refs[r][m] = (
                    tok_ref[0].astype(f32) + scale_ref[:, m : m + 1] * total
                ).astype(bf16)


def out_weight_kernel(count, planes_each, cols, place_ref, sum_ref, *refs):
    u_refs = refs[:PLANE]
    out_ref = refs[PLANE]
    place = place_ref[0]
    head = place_ref[1]
    rows = u_refs[0].shape[1] // 2
    for r in range(PLANE):

        @pl.when(pl.program_id(0) == r)
        def _():
            owner = place ^ r
            for side in range(2):
                span = slice(side * rows, (side + 1) * rows)
                grad = t_mm(u_refs[r][:, span], sum_ref[level_of(owner, side)])
                for q in range(count):
                    for z in range(planes_each):
                        lanes = slice((q * planes_each + z) * cols, (q * planes_each + z + 1) * cols)
                        out_ref[(head ^ q) * planes_each + z, span, :] = grad[:, lanes].astype(bf16)


def per_chunk(width):
    return pl.BlockSpec((CHUNK, width), lambda c: (c, 0))


def across(height):
    return pl.BlockSpec((height, CHUNK), lambda c: (0, c))


def fixed(*shape):
    return pl.BlockSpec(shape, lambda c: (0,) * len(shape))


def back_chunk(width, steps):
    return pl.BlockSpec((CHUNK, width), lambda c: (steps - 1 - c, 0))


def back_across(height, steps):
    return pl.BlockSpec((height, CHUNK), lambda c: (0, steps - 1 - c))


def shaped(shape, kind=f32):
    return jax.ShapeDtypeStruct(shape, kind)


def contract(left_side, right_side, left_dim, right_dim):
    return lax.dot_general(
        left_side,
        right_side,
        (((left_dim,), (right_dim,)), ((), ())),
        preferred_element_type=f32,
    )


def own_heads(values, heads):
    shape = values.shape[:-1]
    shaped_values = values.reshape(shape + (PLANE, -1, lax.axis_size("h"), heads))
    mine = take(shaped_values, lax.axis_index("i"), len(shape))
    mine = take(mine, lax.axis_index("h"), len(shape) + 1)
    return mine.reshape(shape + (-1,))


def shards(
    tokens,
    cotangent,
    doc_lengths,
    input_gain,
    input_weight,
    step_weight,
    state_weight,
    conv_inner,
    conv_inner_bias,
    conv_state,
    conv_state_bias,
    step_bias,
    decay_log,
    skip_gain,
    gated_gain,
    output_weight,
):
    planes = lax.axis_size("o")
    head_count = lax.axis_size("h")
    plane = lax.axis_index("o")
    inner = lax.axis_index("i")
    head = lax.axis_index("h")
    here = jnp.stack([inner, head]).astype(jnp.int32)
    tok_rows, share = tokens.shape
    span = tok_rows * PLANE
    steps = span // CHUNK
    weight_rows, groups_all = input_weight.shape[:2]
    groups = groups_all // PLANE
    width = groups * P_SIZE
    wide_rows = groups_all * P_SIZE
    cols = output_weight.shape[2]
    own_planes = planes // head_count
    half = own_planes * cols
    pad = KERNEL - 1
    halo = 16
    fence = lax.optimization_barrier

    def token_block(*rest):
        return pl.BlockSpec((tok_rows,) + rest, lambda r, place: (r ^ place[0],) + (0,) * len(rest))

    def part_block(*rest):
        return pl.BlockSpec((1,) + rest, lambda r, place: (r,) + (0,) * len(rest))

    def whole_block(*shape):
        return pl.BlockSpec(shape, lambda r, place: (0,) * len(shape))

    def placed_call(kernel, in_specs, out_specs, out_shape, scratch, name):
        return pl.pallas_call(
            kernel,
            grid_spec=pltpu.PrefetchScalarGridSpec(
                num_scalar_prefetch=1,
                grid=(PLANE,),
                in_specs=in_specs,
                out_specs=out_specs,
                scratch_shapes=scratch,
            ),
            out_shape=out_shape,
            compiler_params=PARAMS,
            name=name,
        )

    def unplaced(kernel):
        return lambda place_ref, *refs: kernel(*refs)

    def chunk_call(kernel, in_specs, out_specs, out_shape, scratch, name):
        return pl.pallas_call(
            kernel,
            grid=(steps,),
            in_specs=in_specs,
            out_specs=out_specs,
            out_shape=out_shape,
            scratch_shapes=scratch,
            compiler_params=PARAMS,
            name=name,
        )

    pieces = input_weight.reshape(weight_rows, PLANE, groups, 2, P_SIZE)

    def head_pieces(side):
        return jnp.transpose(pieces[:, :, :, side, :], (1, 0, 2, 3)).reshape(
            PLANE, weight_rows, width
        )

    inner_pieces = exchange_inner(head_pieces(1))
    weight_inner = lax.all_gather(
        inner_pieces.reshape(PLANE * weight_rows, width), "o", axis=0, tiled=True
    )

    near = [swap(tokens, "h", q) if q else tokens for q in range(head_count)]
    far = swap(tokens, "i", 2)
    far = [swap(far, "h", q) if q else far for q in range(head_count)]
    blocks = [near, [swap(b, "i", 1) for b in near], far, [swap(b, "i", 1) for b in far]]
    normed, tok_share = placed_call(
        partial(norm_kernel, head_count, cols, own_planes),
        [whole_block(1, D)] + [whole_block(tok_rows, share)] * (PLANE * head_count),
        [token_block(D), part_block(tok_rows, half)],
        [shaped((span, D), bf16), shaped((PLANE, tok_rows, half), bf16)],
        [],
        "norm",
    )(here, input_gain[None], *[b for row in blocks for b in row])
    normed_halo = shifted(normed[span - halo :], "o", 1)

    gate_pieces, inner_pieces = fence((head_pieces(0), inner_pieces))
    weight_gate = lax.all_gather(
        exchange_inner(gate_pieces).reshape(PLANE * weight_rows, width), "o", axis=0, tiled=True
    )
    weight_out = lax.all_gather(output_weight.reshape(wide_rows, cols), "o")
    weight_out = jnp.concatenate(
        [
            take(weight_out, (head ^ q) * own_planes + z)
            for q in range(head_count)
            for z in range(own_planes)
        ],
        axis=1,
    ).reshape(PLANE, width, head_count * half)
    weight_out_t = jnp.transpose(weight_out, (0, 2, 1))
    weight_step = stack_all(step_weight.reshape(weight_rows, groups_all), ("o", "i")).reshape(
        D, groups_all
    )
    weight_step = lax.dynamic_slice_in_dim(weight_step, inner * groups, groups, 1)

    cot_parts = pl.pallas_call(
        partial(split_kernel, own_planes, cols),
        grid_spec=pltpu.PrefetchScalarGridSpec(
            num_scalar_prefetch=1,
            grid=(4,),
            in_specs=[pl.BlockSpec((1, tok_rows, share), lambda m, place: (m, 0, 0))],
            out_specs=[pl.BlockSpec((1, tok_rows, half), lambda m, place: (m, 0, 0))] * PLANE,
        ),
        out_shape=[shaped((4, tok_rows, half), bf16)] * PLANE,
        compiler_params=PARAMS,
        name="split",
    )(here, cotangent)
    cot_parts = [cot_parts[0]] + [swap(cot_parts[r], "i", r) for r in range(1, PLANE)]
    normed, normed_halo, cot_parts = fence((normed, normed_halo, cot_parts))
    cots = [
        [swap(part, "h", q) if q else part for part in cot_parts] for q in range(head_count)
    ]

    starts = jnp.cumsum(doc_lengths) - doc_lengths
    positions = plane * span + jnp.arange(-pad, span, dtype=jnp.int32)
    docs_ext = jnp.sum((positions[:, None] >= starts[None, :]).astype(jnp.int32), axis=1)
    docs = docs_ext[pad:]
    matches = [(docs_ext[k : k + span] == docs).astype(f32) for k in range(pad)]

    def taps_of(kernel, bias):
        return jnp.concatenate([kernel, bias[None], jnp.zeros((3, bias.shape[0]), f32)], axis=0)

    taps_inner = taps_of(own_heads(conv_inner, P_SIZE), own_heads(conv_inner_bias, P_SIZE))
    taps_state = taps_of(conv_state, conv_state_bias)
    gain_wide = own_heads(gated_gain, P_SIZE)
    step_shift = own_heads(step_bias, 1)
    rate_log = own_heads(decay_log, 1)
    skip_wide = jnp.repeat(own_heads(skip_gain, 1), P_SIZE)
    wide = jnp.concatenate([skip_wide[None], gain_wide[None], jnp.zeros((6, width), f32)], axis=0)
    group_number = inner * groups + jnp.arange(groups)
    level_limit = jnp.array([groups_all >> m for m in range(4)] + [0] * 4)
    level_mask = jnp.repeat(
        (group_number[None, :] < level_limit[:, None]).astype(bf16), P_SIZE, axis=1
    )

    state_halo, state_value = fence(
        (
            jnp.dot(normed_halo, state_weight, preferred_element_type=f32).astype(bf16),
            jnp.dot(normed, state_weight, preferred_element_type=f32).astype(bf16),
        )
    )
    extended = jnp.concatenate([state_halo[halo - pad :], state_value], axis=0).astype(f32)
    pre_state = conv_state_bias[None, :] + conv_state[pad][None, :] * extended[pad:]
    for k in range(pad):
        pre_state = pre_state + (
            conv_state[k][None, :] * extended[k : k + span] * matches[k][:, None]
        )
    state_act = jax.nn.silu(pre_state).astype(bf16)
    state_act_t = jnp.transpose(state_act)

    step_raw = jnp.dot(normed, weight_step, preferred_element_type=f32)
    step = jax.nn.softplus(step_raw + step_shift[None, :])
    rate = jnp.exp(rate_log)
    decay = -step * rate[None, :]
    lower = jnp.tril(jnp.ones((CHUNK, CHUNK), f32))
    cum = jnp.einsum("ts,csh->cth", lower, decay.reshape(steps, CHUNK, groups), precision=high)
    sums = cum[:, -1]
    before = jnp.cumsum(sums, axis=0) - sums
    cum_whole = (cum + before[:, None, :]).reshape(span, groups)
    cum = cum.reshape(span, groups)
    docs_f = docs.astype(f32)
    prior_doc = docs_ext[pad - 1 : pad - 1 + span]
    by_chunk = docs.reshape(steps, CHUNK)
    prior = prior_doc.reshape(steps, CHUNK)[:, :1]
    from_start = (by_chunk == prior).astype(f32).reshape(span)
    to_end = (by_chunk == by_chunk[:, -1:]).astype(f32).reshape(span)
    inside = (docs == prior_doc).astype(f32)
    whole_start = (docs == docs_ext[pad - 1]).astype(f32)
    whole_end = (docs == docs[-1]).astype(f32)
    entry_whole = jnp.exp(cum_whole) * whole_start[:, None]
    end_whole = jnp.exp(cum_whole[-1:] - cum_whole) * whole_end[:, None] * step
    decay_whole = jnp.repeat(entry_whole[-1:], P_SIZE, axis=1)
    col_pack = jnp.concatenate(
        [
            cum,
            step,
            entry_whole,
            jnp.stack([docs_f, from_start, to_end, inside] + matches, axis=1),
            end_whole,
        ],
        axis=1,
    )
    col_width = col_pack.shape[1]
    row_pack = jnp.concatenate([cum.T, step.T, docs_f[None]], axis=0)
    row_height = row_pack.shape[0]

    wide_out = shaped((span, width))
    value, pre_inner, x, own_state, inner_halo = chunk_call(
        partial(project_kernel, groups),
        [
            per_chunk(D),
            fixed(halo, D),
            fixed(D, width),
            across(2 * STATE),
            per_chunk(col_width),
            fixed(8, width),
        ],
        [per_chunk(width)] * 3 + [fixed(STATE, width), fixed(halo, width)],
        [
            shaped((span, width), bf16),
            wide_out,
            shaped((span, width), bf16),
            shaped((STATE, width)),
            shaped((halo, width), bf16),
        ],
        [pltpu.VMEM((8, width), f32)],
        "project",
    )(normed, normed_halo, weight_inner, state_act_t, col_pack, taps_inner)
    incoming = chain(own_state, decay_whole, 1)
    y_local = chunk_call(
        partial(within_kernel, groups),
        [per_chunk(width), per_chunk(2 * STATE), per_chunk(col_width), across(row_height)],
        per_chunk(width),
        wide_out,
        [],
        "within",
    )(x, state_act, col_pack, row_pack)
    y_local, cots = fence((y_local, cots))
    cots = [jnp.stack(parts) for parts in cots]
    gate_z = jnp.dot(normed, weight_gate, preferred_element_type=f32).astype(bf16)
    v, scaled_u, squares, entering = chunk_call(
        partial(carry_kernel, groups),
        [
            per_chunk(width),
            per_chunk(2 * STATE),
            across(2 * STATE),
            per_chunk(col_width),
            per_chunk(width),
            per_chunk(width),
            fixed(STATE, width),
            fixed(8, width),
            fixed(8, width),
        ],
        [per_chunk(width), per_chunk(width), across(8), per_chunk(width)],
        [
            wide_out,
            shaped((span, width), bf16),
            shaped((8, span)),
            shaped((steps * STATE, width)),
        ],
        [pltpu.VMEM((STATE, width), f32)],
        "carry",
    )(x, state_act, state_act_t, col_pack, y_local, gate_z, incoming, wide, level_mask)

    u_far = swap(scaled_u, "i", 2)
    u_parts = [scaled_u, swap(scaled_u, "i", 1), u_far, swap(u_far, "i", 1)]
    squares = add_all(squares[:4], ("i", "h"))
    widths = jnp.array([INNER >> m for m in range(4)], f32)
    scales_row = lax.rsqrt(squares / widths[:, None] + eps)
    scales = jnp.transpose(jnp.concatenate([scales_row, jnp.zeros_like(scales_row)], axis=0))
    cot_block = part_block(4, tok_rows, half)
    cot_shape = shaped((PLANE, 4, tok_rows, half), bf16)
    *parts, sums, tops = placed_call(
        partial(out_back_kernel, head_count),
        [token_block(8), whole_block(PLANE, head_count * half, width)] + [cot_block] * head_count,
        [token_block(width)] * PLANE
        + [
            pl.BlockSpec((4, tok_rows, head_count * half), lambda r, place: (0, r ^ place[0], 0)),
            whole_block(8, width),
        ],
        [wide_out] * PLANE + [shaped((4, span, head_count * half), bf16), shaped((8, width))],
        [pltpu.VMEM((4, tok_rows, head_count * half), bf16)],
        "out_back",
    )(here, scales, weight_out_t, *cots)
    top = tops[2:3] + swap(tops, "i", 1)[3:4]
    top_across = swap(jnp.broadcast_to(top, tops.shape), "i", 2)[:1]
    got_across = swap(to_half(parts[2] + swap(parts[3], "i", 1), top), "i", 2)
    got_near = swap(parts[1], "i", 1)
    u_grad = parts[0] + got_near + from_half(got_across, top_across)
    dots, own_product, *sent_products = placed_call(
        partial(product_kernel, head_count),
        [whole_block(PLANE, width, head_count * half)]
        + [token_block(width)] * PLANE
        + [cot_block] * head_count,
        [pl.BlockSpec((8, tok_rows), lambda r, place: (0, r ^ place[0]))]
        + [cot_block] * head_count,
        [shaped((8, span)), shaped(cot_shape.shape)] + [cot_shape] * (head_count - 1),
        [pltpu.VMEM((4, tok_rows, head_count * half), f32)],
        "products",
    )(here, weight_out, *u_parts, *cots)
    dots = add_all(dots[:4], ("i", "h"))
    out_grad = placed_call(
        partial(out_weight_kernel, head_count, own_planes, cols),
        [whole_block(4, span, head_count * half)] + [whole_block(span, width)] * PLANE,
        pl.BlockSpec((planes, width, cols), lambda r, place: (0, r ^ place[0], 0)),
        shaped((planes, wide_rows, cols), bf16),
        [],
        "out_weight_back",
    )(here, sums, *u_parts)
    out_grad = lax.psum_scatter(out_grad, "o", scatter_dimension=0, tiled=False)
    output_weight_grad = out_grad.astype(f32).reshape(groups_all, P_SIZE, cols)

    stat = dots * -0.5 * scales_row * scales_row * scales_row / widths[:, None]
    stat = jnp.concatenate([stat, jnp.zeros_like(stat)], axis=0)
    y_grad, z_grad, wide_sums, leaving = chunk_call(
        partial(gate_back_kernel, groups),
        [
            per_chunk(width),
            per_chunk(width),
            per_chunk(width),
            per_chunk(width),
            across(2 * STATE),
            per_chunk(col_width),
            across(8),
            fixed(8, width),
            fixed(8, width),
        ],
        [per_chunk(width), per_chunk(width), fixed(8, width), fixed(STATE, width)],
        [wide_out, shaped((span, width), bf16), shaped((8, width)), shaped((STATE, width))],
        [],
        "gate_back",
    )(u_grad, v, gate_z, x, state_act_t, col_pack, stat, wide, level_mask)
    lam = chain(leaving, decay_whole, -1)
    gate_grad = contract(normed, z_grad, 0, 0).astype(bf16)
    gate_grad, y_grad = fence((gate_grad, y_grad))
    gate_grad = lax.psum_scatter(gate_grad, "o", scatter_dimension=0, tiled=True)

    dx_local, dbc_local, ds_local = chunk_call(
        partial(within_back_kernel, groups),
        [
            per_chunk(width),
            per_chunk(2 * STATE),
            per_chunk(col_width),
            across(row_height),
            per_chunk(width),
        ],
        [per_chunk(width), per_chunk(2 * STATE), per_chunk(2 * groups)],
        [wide_out, shaped((span, 2 * STATE)), shaped((span, 2 * groups))],
        [],
        "within_back",
    )(x, state_act, col_pack, row_pack, y_grad)
    back_wide = back_chunk(width, steps)
    back_state = back_chunk(2 * STATE, steps)
    back_step = back_chunk(2 * groups, steps)
    (
        inner_grad,
        inner_tail,
        inner_edge,
        inner_sums,
        state_grad,
        state_edge,
        state_sums,
        step_pair,
    ) = chunk_call(
        partial(carry_back_kernel, groups),
        [
            back_wide,
            back_state,
            back_across(2 * STATE, steps),
            back_chunk(col_width, steps),
            back_across(row_height, steps),
            back_wide,
            back_wide,
            back_state,
            back_step,
            back_wide,
            fixed(STATE, width),
            fixed(8, width),
            back_wide,
            back_wide,
            fixed(halo, width),
            fixed(8, width),
            back_state,
            back_state,
            fixed(halo, 2 * STATE),
            fixed(8, 2 * STATE),
        ],
        [
            back_wide,
            fixed(16, width),
            fixed(8, width),
            fixed(8, width),
            back_state,
            fixed(8, 2 * STATE),
            fixed(8, 2 * STATE),
            back_step,
        ],
        [
            shaped((span, width), bf16),
            shaped((16, width)),
            shaped((8, width)),
            shaped((8, width)),
            shaped((span, 2 * STATE)),
            shaped((8, 2 * STATE)),
            shaped((8, 2 * STATE)),
            shaped((span, 2 * groups)),
        ],
        [
            pltpu.VMEM((STATE, width), f32),
            pltpu.VMEM((24, width), f32),
            pltpu.VMEM((24, 2 * STATE), f32),
        ],
        "carry_back",
    )(
        x,
        state_act,
        state_act_t,
        col_pack,
        row_pack,
        y_grad,
        dx_local,
        dbc_local,
        ds_local,
        entering,
        lam,
        wide,
        pre_inner,
        value,
        inner_halo,
        taps_inner,
        pre_state,
        state_value,
        state_halo,
        taps_state,
    )
    size_grad = step_pair[:, :groups]
    decay_grad = step_pair[:, groups:]
    step_raw_grad = (size_grad - rate[None, :] * decay_grad) * jax.nn.sigmoid(
        step_raw + step_shift[None, :]
    )
    edges = shifted(jnp.concatenate([inner_edge, state_edge], axis=1), "o", -1)
    tail = inner_tail + jnp.pad(edges[:, :width], ((8, 0), (0, 0)))
    inner_grad = lax.dynamic_update_slice_in_dim(inner_grad, tail.astype(bf16), span - 16, 0)
    state_grad = state_grad + jnp.pad(edges[:, width:], ((span - 8, 0), (0, 0)))

    inner_part = contract(normed, inner_grad, 0, 0).astype(bf16)
    inner_part, inner_grad = fence((inner_part, inner_grad))
    inner_part = lax.psum_scatter(inner_part, "o", scatter_dimension=0, tiled=True)
    step_grad_low = step_raw_grad.astype(bf16)
    state_grad_low = state_grad.astype(bf16)
    normed_parts = placed_call(
        unplaced(normed_back_kernel),
        [
            token_block(width),
            token_block(width),
            token_block(groups),
            token_block(2 * STATE),
            whole_block(D, width),
            whole_block(D, width),
            whole_block(D, groups),
            whole_block(D, 2 * STATE),
        ],
        [whole_block(tok_rows, D)] * PLANE,
        [shaped((tok_rows, D), f32 if r % 2 == 0 else bf16) for r in range(PLANE)],
        [],
        "normed_back",
    )(
        here,
        z_grad,
        inner_grad,
        step_grad_low,
        state_grad_low,
        weight_gate,
        weight_inner,
        weight_step,
        state_weight,
    )
    got_across = swap(
        (normed_parts[2] + swap(normed_parts[3], "i", 1).astype(f32)).astype(bf16), "i", 2
    )
    full_grad = scatter_heads(
        normed_parts[0] + swap(normed_parts[1], "i", 1).astype(f32) + got_across.astype(f32), 1
    )

    got_products = [swap(sent_products[q - 1], "h", q) for q in range(1, head_count)]
    mixed_parts = placed_call(
        unplaced(partial(mix_kernel, head_count)),
        [token_block(8), part_block(tok_rows, half)] + [cot_block] * head_count,
        [whole_block(4, tok_rows, half)] * PLANE,
        [shaped((4, tok_rows, half), bf16)] * PLANE,
        [],
        "mix",
    )(here, scales, tok_share, own_product, *got_products)
    mixed_parts = [mixed_parts[0]] + [swap(mixed_parts[r], "i", r) for r in range(1, PLANE)]
    mixed = placed_call(
        partial(join_kernel, own_planes, cols),
        [part_block(tok_rows, half)] * PLANE,
        part_block(tok_rows, share),
        shaped((4, tok_rows, share), bf16),
        [],
        "join",
    )(here, *mixed_parts)

    gate_back = exchange_inner(gate_grad.reshape(PLANE, weight_rows, width))
    inner_back = exchange_inner(inner_part.reshape(PLANE, weight_rows, width))

    def by_group(values):
        return jnp.transpose(
            values.reshape(PLANE, weight_rows, groups, P_SIZE), (1, 0, 2, 3)
        ).reshape(weight_rows, groups_all, P_SIZE)

    input_weight_grad = jnp.concatenate(
        [by_group(gate_back), by_group(inner_back)], axis=2
    ).astype(f32)
    step_part = add_all(contract(step_grad_low, normed, 0, 0), ("o",))
    step_part = lax.dynamic_slice_in_dim(
        stack_all(step_part, ("i",)).reshape(groups_all, planes * PLANE, weight_rows),
        plane * PLANE + inner,
        1,
        1,
    )
    step_weight_grad = jnp.transpose(step_part, (2, 1, 0))

    state_sum = state_grad
    for axis in ("i", "h"):
        for bit in bits_of(axis):
            kind = f32 if axis == "i" and bit == 1 else bf16
            state_sum = state_sum + swap(state_sum.astype(kind), axis, bit).astype(f32)
    part_rows = D // (PLANE * head_count)
    normed_part = lax.dynamic_slice_in_dim(
        normed, (inner * head_count + head) * part_rows, part_rows, 1
    )
    state_part = contract(normed_part, state_sum.astype(bf16), 0, 0)
    state_part = add_all(state_part, ("o",)).astype(bf16)
    state_weight_grad = stack_all(state_part, ("i", "h")).reshape(D, 2 * STATE).astype(f32)

    own_wide = [near[q].astype(f32) for q in range(head_count)]
    square = sum(jnp.sum(a * a, axis=1, keepdims=True) for a in own_wide)
    inverse = lax.rsqrt(square / D + eps)
    gain_share = lax.dynamic_slice_in_dim(input_gain, head * share, share, 0)
    unit = own_wide[0] * inverse
    weighted = full_grad * gain_share[None, :]
    row_sum = add_all(jnp.sum(weighted * unit, axis=1).reshape(-1, CHUNK), ("h",)).reshape(-1, 1)
    resid = jnp.sum(cotangent.astype(f32), axis=0)
    tokens_grad = resid + inverse * (weighted - unit * (row_sum / D))
    gain_part = add_all(jnp.sum(full_grad * unit, axis=0).reshape(-1, CHUNK), ("o", "i"))
    input_gain_grad = stack_all(gain_part, ("h",)).reshape(D)

    per_head = jnp.stack(
        [
            jnp.sum(step_raw_grad, axis=0),
            jnp.sum(decay_grad * decay, axis=0),
            jnp.sum(wide_sums[1].reshape(groups, P_SIZE), axis=1),
        ]
    )
    per_head = jnp.pad(per_head, ((0, 0), (0, width - groups)))
    flat = state_sums[: KERNEL + 1].reshape(-1)
    flat = jnp.pad(flat, (0, -flat.shape[0] % width)).reshape(-1, width)
    small = jnp.concatenate([inner_sums[: KERNEL + 1], wide_sums[:1], per_head, flat], axis=0)
    small = stack_all(add_all(small, ("o",)), ("i", "h"))
    small = small.reshape(PLANE, head_count, -1, width)
    shared = jnp.sum(small[:, :, 9:], axis=(0, 1)).reshape(-1)[: (KERNEL + 1) * 2 * STATE]
    shared = shared.reshape(KERNEL + 1, 2 * STATE)

    def all_heads(values, size):
        values = values.reshape(PLANE, head_count, -1, groups, size)
        return jnp.transpose(values, (2, 0, 3, 1, 4)).reshape(values.shape[2], -1)

    wide_total = all_heads(small[:, :, :6], P_SIZE)
    head_total = all_heads(small[:, :, 6:9, :groups], 1)
    return (
        mixed,
        tokens_grad,
        input_gain_grad,
        input_weight_grad,
        step_weight_grad,
        state_weight_grad,
        wide_total[:4],
        wide_total[4],
        shared[:4],
        shared[4],
        head_total[0],
        head_total[1],
        head_total[2],
        wide_total[5],
        output_weight_grad,
    )


def solution(mesh):
    rows, heads = mesh.devices.shape
    cut = Mesh(mesh.devices.reshape(rows // PLANE, PLANE, heads), ("o", "i", "h"))
    both = ("o", "i")
    placed = (
        P(both, "h"),
        P(None, both, "h"),
        P(),
        P(),
        P(both, None, "h"),
        P(both, "h", None),
        P(),
        P(),
        P(),
        P(),
        P(),
        P(),
        P(),
        P(),
        P(),
        P(None, "h", both),
    )
    return jax.shard_map(
        shards,
        mesh=cut,
        in_specs=placed,
        out_specs=(
            P(None, both, "h"),
            P(both, "h"),
            P(),
            P(both, None, "h"),
            P(both, "h", None),
            P(),
            P(),
            P(),
            P(),
            P(),
            P(),
            P(),
            P(),
            P(),
            P(None, "h", both),
        ),
        check_vma=False,
    )
```

time: 1710 us -> 616 us (0.36)
  waiting for transfers between devices: 1190 us -> 215 us
  matrix products: 152 us -> 25.5 us
  Pallas kernels: 0 us -> 124 us
  blocking collectives: 89.9 us -> 0 us
  starting transfers between devices: 9.1 us -> 85.9 us
  other arithmetic: 128 us -> 53.5 us
  local copies, waits for them, and re-layouts: 113 us -> 87.1 us
    reduce_scatter x4 -> x3, waiting for transfers between devices: 669 us -> 0.04 us  [the longest x1 0.02 us: shards(): lax.psum_scatter(inner_part, 'o', scatter_dimension=0, tiled=True)]
    all_gather x6 -> x3, waiting for transfers between devices: 362 us -> 0.04 us  [the longest x1 0.02 us: shards(): lax.all_gather(exchange_inner(gate_pieces).reshape(PLANE * weight_rows, w...]
    ppermute x0 -> x75, waiting for transfers between devices: none -> 184 us  [swap(): lax.ppermute(block, axis, [(a, a ^ bit) for a in range(lax.axis_size(axis...]
    psum x2 -> x0, waiting for transfers between devices: 157 us -> none  [the longest x1 140 us: shards(): lax.psum((state_weight_part, conv_state_grad, conv_state_bias_grad, conv_...]
    pallas_call x0 -> x14, Pallas kernels: none -> 124 us  [the longest x1 17.3 us: shards(): placed_call(partial(out_back_kernel, head_count), [token_block(8), whole_...]
    dot_general x19 -> x5, matrix products: 79.9 us -> 13.5 us  [the longest x1 5.19 us: shards(): jnp.dot(normed, weight_gate, preferred_element_type=f32).astype(bf16)]
    ppermute x0 -> x75, starting transfers between devices: none -> 61 us  [swap(): lax.ppermute(block, axis, [(a, a ^ bit) for a in range(lax.axis_size(axis...]
    dot_general x14 -> x4, matrix products: 71.7 us -> 11.9 us  [contract(): lax.dot_general(left_side, right_side, (((left_dim,), (right_dim,)), ((),...]
  transfers between devices with their start and end apart: 16 -> 95, of which waited for: 11 -> 41; matrix products, arithmetic and copies ran while one was open for 14% -> 22% of each run, Pallas kernels for 0% -> 18%
where the time goes in v1:
time: 616 us; the launch traced here: 607 us
  waiting for transfers between devices  215 us (35%)
  Pallas kernels  124 us (20%)
  local copies, waits for them, and re-layouts  87.1 us (14%)
  starting transfers between devices  85.9 us (14%)
  other arithmetic  53.5 us (9%)
  matrix products  25.5 us (4%)
  between operations  15.9 us (3%)
    ppermute x75, waiting for transfers between devices, swap(): lax.ppermute(block, axis, [(a, a ^ bit) for a in range(lax.axis_size(axis...  184 us
    ppermute x75, starting transfers between devices, swap(): lax.ppermute(block, axis, [(a, a ^ bit) for a in range(lax.axis_size(axis...  61 us
    ppermute x14, waiting for transfers between devices, shifted(): return lax.ppermute(block, axis, route)  31 us
    unnamed x184, local copies, waits for them, and re-layouts  27.1 us
    ppermute x14, starting transfers between devices, shifted(): return lax.ppermute(block, axis, route)  24.3 us
    pallas_call x1, Pallas kernels, shards(): placed_call(partial(out_back_kernel, head_count), [token_block(8), whole_...  17.3 us
    pallas_call x1, Pallas kernels, shards(): chunk_call(partial(carry_back_kernel, groups), [back_wide, back_state, ba...  16 us
    pallas_call x1, Pallas kernels, shards(): placed_call(unplaced(normed_back_kernel), [token_block(width), token_bloc...  13.5 us
  transfers between devices with their start and end apart: 95, of which 41 were waited for; matrix products, arithmetic and copies ran while one was open for 22% of the time, Pallas kernels for 18%

profile of v1, /device:TPU:0, one launch (start us, length us, event | category | flops | bytes accessed | tf_op | source)
XLA Modules:
  0.0 607.4 jit_solution(6293456639194184059)
XLA Ops:
  13.8 4.3 collective-permute-done.12
  24.4 4.6 collective-permute-done.23
  38.7 9.3 %collective-permute-done.3.refs_4_ = bf16[256,1024]{1,0:T(8,128)(2,1)} collective-permute-done((bf16[256,1024]{1,0:T(8,128)(2,1)S(1)}, bf16[256,1024]{1,0:T(8,128)(2,1)}, u32[]{:S(2)}, u32[]{:S(2)}) %collective-permute-start.3) | collective-permute-done | bytes 524320 | tf_op jit(solution)/shard_map/ppermute | solution.py:31
  73.2 5.9 norm.1
  82.8 3.2 collective-permute-done.9
  86.0 10.3 %collective-permute-done.10 = bf16[4,256,256]{2,1,0:T(8,128)(2,1)S(1)} collective-permute-done((bf16[4,256,256]{2,1,0:T(8,128)(2,1)}, bf16[4,256,256]{2,1,0:T(8,128)(2,1)S(1)}, u32[]{:S(2)}, u32[]{:S(2)}) %collective-permute-start.10) | collective-permute-done | bytes 524320 | tf_op jit(solution)/shard_map/ppermute | solution.py:31
  97.1 3.7 negate_multiply_fusion
  102.2 3.4 convolution_convert_fusion.3.value_state_ref
  117.5 4.1 concatenate.138.col_ref
  121.6 10.0 %project.1 = (bf16[1024,512]{1,0:T(8,128)(2,1)S(1)}, f32[1024,512]{1,0:T(8,128)S(1)}, bf16[1024,512]{1,0:T(8,128)(2,1)S(1)}, f32[128,512]{1,0:T(8,128)S(1)}, bf16[16,512]{1,0:T(8,128)(2,1)S(1)}) custom-call(bf16[1024,2048]{1,0:T(8,128)(2,1)} %get-tuple-element.89.normed_ref, bf16[16,2048]{1,0:T(8,128)(2,1)S(1)} %collective-permute-done.7.halo_ref, ...), custom_call_target="tpu_custom_call" | custom-call | tf_op jit(solution)/shard_map/project/pallas_call | solution.py:990
  135.0 3.8 within.1.yl_ref
  144.2 3.6 collective-permute-done.20
  149.7 9.0 %collective-permute-done.21 = bf16[4,256,256]{2,1,0:T(8,128)(2,1)} collective-permute-done((bf16[4,256,256]{2,1,0:T(8,128)(2,1)}, bf16[4,256,256]{2,1,0:T(8,128)(2,1)}, u32[]{:S(2)}, u32[]{:S(2)}) %collective-permute-start.21) | collective-permute-done | bytes 524320 | tf_op jit(solution)/shard_map/ppermute | solution.py:31
  158.7 3.3 collective-permute-start.30
  165.0 5.2 convolution_convert_fusion.2.gz_ref
  170.2 8.4 %carry.1 = (f32[1024,512]{1,0:T(8,128)}, bf16[1024,512]{1,0:T(8,128)(2,1)}, f32[8,1024]{1,0:T(8,128)S(1)}, f32[1024,512]{1,0:T(8,128)}) custom-call(bf16[1024,512]{1,0:T(8,128)(2,1)S(1)} %get-tuple-element.93.x_ref, bf16[1024,256]{1,0:T(8,128)(2,1)S(1)} %get-tuple-element.165.st_ref, bf16[256,1024]{1,0:T(8,128)(2,1)S(1)} %copy.261.stt_ref, ...), custom_call_target="tpu_custom_call" | custom-call | tf_op jit(solution)/shard_map/carry/pallas_call | solution.py:1023
  180.7 22.7 %collective-permute-done.35.refs_2_ = bf16[1024,512]{1,0:T(8,128)(2,1)} collective-permute-done((bf16[1024,512]{1,0:T(8,128)(2,1)}, bf16[1024,512]{1,0:T(8,128)(2,1)}, u32[]{:S(2)}, u32[]{:S(2)}) %collective-permute-start.35) | collective-permute-done | bytes 1048608 | tf_op jit(solution)/shard_map/ppermute | solution.py:31
  214.5 3.9 fusion.56
  218.4 4.1 copy.270.weight_ref
  222.5 3.1 pad_maximum_fusion.1.refs_4_.refs_0_
  229.3 10.4 %products.1 = (f32[8,1024]{1,0:T(8,128)S(1)}, f32[4,4,256,256]{3,2,1,0:T(8,128)}, bf16[4,4,256,256]{3,2,1,0:T(8,128)(2,1)}) custom-call(s32[2]{0:T(128)S(1)} %copy-done.37, bf16[4,512,512]{2,1,0:T(8,128)(2,1)} %copy.270.weight_ref, bf16[1024,512]{1,0:T(8,128)(2,1)} %get-tuple-element.103.refs_0_, bf16[1024,512]{1,0:T(8,128)(2,1)} %collective-permute-done.34.refs_1_, ...), custom_call_target="tpu_custom_call" | custom-call | tf_op jit(solution)/shard_map/products/pallas_call | solution.py:1072
  251.2 17.3 %out_back.1 = (f32[1024,512]{1,0:T(8,128)S(1)}, f32[1024,512]{1,0:T(8,128)S(1)}, f32[1024,512]{1,0:T(8,128)}, f32[1024,512]{1,0:T(8,128)}, bf16[4,1024,512]{2,1,0:T(8,128)(2,1)}, /*index=5*/f32[8,512]{1,0:T(8,128)S(1)}) custom-call(s32[2]{0:T(128)S(1)} %copy-done.37, f32[1024,8]{1,0:T(8,128)S(1)} %copy-done.4, ...), custom_call_target="tpu_custom_call" | custom-call | tf_op jit(solution)/shard_map/out_back/pallas_call | solution.py:1055
  271.2 7.9 %out_weight_back.1 = bf16[4,2048,128]{2,1,0:T(8,128)(2,1)} custom-call(s32[2]{0:T(128)S(1)} %copy-done.37, bf16[4,1024,512]{2,1,0:T(8,128)(2,1)} %get-tuple-element.152.sum_ref, bf16[1024,512]{1,0:T(8,128)(2,1)} %get-tuple-element.103.refs_0_, bf16[1024,512]{1,0:T(8,128)(2,1)} %collective-permute-done.34.refs_1_, ...), custom_call_target="tpu_custom_call" | custom-call | tf_op jit(solution)/shard_map/out_weight_back/pallas_call | solution.py:1084
  281.6 3.3 collective-permute-done.43
  284.9 3.8 multiply_convert_fusion
  290.5 3.2 convert_reduce_fusion
  295.1 19.5 %collective-permute-done.45 = f32[8,512]{1,0:T(8,128)S(1)} collective-permute-done((f32[8,512]{1,0:T(8,128)S(1)}, f32[8,512]{1,0:T(8,128)S(1)}, u32[]{:S(2)}, u32[]{:S(2)}) %collective-permute-start.45) | collective-permute-done | bytes 16416 | tf_op jit(solution)/shard_map/ppermute | solution.py:31
  314.7 13.3 %collective-permute-done.37.refs_3_ = bf16[4,4,256,256]{3,2,1,0:T(8,128)(2,1)} collective-permute-done((bf16[4,4,256,256]{3,2,1,0:T(8,128)(2,1)}, bf16[4,4,256,256]{3,2,1,0:T(8,128)(2,1)}, u32[]{:S(2)}, u32[]{:S(2)}) %collective-permute-start.37) | collective-permute-done | bytes 2097184 | tf_op jit(solution)/shard_map/ppermute | solution.py:31
  328.0 5.4 mix.1
  334.8 3.9 multiply_add_fusion.ug_ref
  338.7 8.0 %gate_back.1 = (f32[1024,512]{1,0:T(8,128)}, bf16[1024,512]{1,0:T(8,128)(2,1)S(1)}, f32[8,512]{1,0:T(8,128)S(1)}, f32[128,512]{1,0:T(8,128)S(1)}) custom-call(f32[1024,512]{1,0:T(8,128)} %multiply_add_fusion.ug_ref, f32[1024,512]{1,0:T(8,128)} %get-tuple-element.123.v_ref, bf16[1024,512]{1,0:T(8,128)(2,1)S(1)} %copy-done.7, ...), custom_call_target="tpu_custom_call" | custom-call | tf_op jit(solution)/shard_map/gate_back/pallas_call | solution.py:1097
  350.0 3.8 convolution_convert_fusion.1
  356.9 10.9 %within_back.1 = (f32[1024,512]{1,0:T(8,128)S(1)}, f32[1024,256]{1,0:T(8,128)S(1)}, f32[1024,16]{1,0:T(8,128)S(1)}) custom-call(bf16[1024,512]{1,0:T(8,128)(2,1)S(1)} %get-tuple-element.93.x_ref, bf16[1024,256]{1,0:T(8,128)(2,1)S(1)} %get-tuple-element.165.st_ref, f32[1024,39]{1,0:T(8,128)S(1)} %concatenate.138.col_ref, ...), custom_call_target="tpu_custom_call" | custom-call | tf_op jit(solution)/shard_map/within_back/pallas_call | solution.py:1120
  372.5 9.2 %collective-permute-done.50 = f32[8,512]{1,0:T(8,128)S(1)} collective-permute-done((f32[8,512]{1,0:T(8,128)S(1)}, f32[8,512]{1,0:T(8,128)S(1)}, u32[]{:S(2)}, u32[]{:S(2)}) %collective-permute-start.50) | collective-permute-done | bytes 16416 | tf_op jit(solution)/shard_map/ppermute | solution.py:37
  382.9 6.8 %collective-permute-done.54 = f32[8,512]{1,0:T(8,128)S(1)} collective-permute-done((f32[8,512]{1,0:T(8,128)S(1)}, f32[8,512]{1,0:T(8,128)S(1)}, u32[]{:S(2)}, u32[]{:S(2)}) %collective-permute-start.54) | collective-permute-done | bytes 16416 | tf_op jit(solution)/shard_map/ppermute | solution.py:37
  391.1 13.6 %collective-permute-done.49 = f16[128,512]{1,0:T(8,128)(2,1)S(1)} collective-permute-done((f16[128,512]{1,0:T(8,128)(2,1)}, f16[128,512]{1,0:T(8,128)(2,1)S(1)}, u32[]{:S(2)}, u32[]{:S(2)}) %collective-permute-start.49) | collective-permute-done | bytes 131104 | tf_op jit(solution)/shard_map/ppermute | solution.py:37
  407.9 16.0 %carry_back.1 = (bf16[1024,512]{1,0:T(8,128)(2,1)S(1)}, f32[16,512]{1,0:T(8,128)S(1)}, f32[8,512]{1,0:T(8,128)S(1)}, f32[8,512]{1,0:T(8,128)S(1)}, f32[1024,256]...) custom-call(bf16[1024,512]{1,0:T(8,128)(2,1)} %copy-done, ...), custom_call_target="tpu_custom_call" | custom-call | tf_op jit(solution)/shard_map/carry_back/pallas_call | solution.py:1146
  433.3 6.0 convolution_convert_fusion
  442.4 13.5 %normed_back.1 = (f32[256,2048]{1,0:T(8,128)}, bf16[256,2048]{1,0:T(8,128)(2,1)S(1)}, f32[256,2048]{1,0:T(8,128)}, bf16[256,2048]{1,0:T(8,128)(2,1)}) custom-call(s32[2]{0:T(128)S(1)} %copy-done.37, bf16[1024,512]{1,0:T(8,128)(2,1)S(1)} %copy-done.19, bf16[1024,512]{1,0:T(8,128)(2,1)S(1)} %copy-done.23, bf16[1024,8]{1,0:T(8,128)(2,1)S(1)} %get-tuple-element.156.refs_2_, ...), custom_call_target="tpu_custom_call" | custom-call | tf_op jit(solution)/shard_map/normed_back/pallas_call | solution.py:1233
  462.5 4.5 join.1
  469.1 4.8 collective-permute-done.73
  494.6 19.7 %collective-permute-done.77 = bf16[1024,256]{1,0:T(8,128)(2,1)S(1)} collective-permute-done((bf16[1024,256]{1,0:T(8,128)(2,1)}, bf16[1024,256]{1,0:T(8,128)(2,1)S(1)}, u32[]{:S(2)}, u32[]{:S(2)}) %collective-permute-start.77) | collective-permute-done | bytes 524320 | tf_op jit(solution)/shard_map/ppermute | solution.py:31
  519.6 9.8 %collective-permute-done.78 = bf16[1024,256]{1,0:T(8,128)(2,1)S(1)} collective-permute-done((bf16[1024,256]{1,0:T(8,128)(2,1)S(1)}, bf16[1024,256]{1,0:T(8,128)(2,1)S(1)}, u32[]{:S(2)}, u32[]{:S(2)}) %collective-permute-start.78) | collective-permute-done | bytes 524320 | tf_op jit(solution)/shard_map/ppermute | solution.py:31
  547.2 4.7 collective-permute-done.80
  554.3 3.6 collective-permute-done.81
  567.8 7.4 %collective-permute-done.83 = bf16[4,256,256]{2,1,0:T(8,128)(2,1)S(1)} collective-permute-done((bf16[4,256,256]{2,1,0:T(8,128)(2,1)S(1)}, bf16[4,256,256]{2,1,0:T(8,128)(2,1)S(1)}, u32[]{:S(2)}, u32[]{:S(2)}) %collective-permute-start.83) | collective-permute-done | bytes 524320 | tf_op jit(solution)/shard_map/ppermute | solution.py:31
  580.8 4.2 collective-permute-done.67
  591.0 4.5 collective-permute-done.70
  (563 shorter events, 226.8 us)
Async XLA Ops:
  7.2 114.4 %all-gather.4.cloned.1.call-start = ((), (), s32[]{:S(2)}) async-start(), calls=%async_computation.3 | async-start | bytes 2621440 | tf_op jit(solution)/shard_map/all_gather | solution.py:861
  21.0 143.9 %all-gather.6.cloned.1.call-start = ((), (), s32[]{:S(2)}) async-start(), calls=%async_computation.4 | async-start | bytes 2621440 | tf_op jit(solution)/shard_map/all_gather | solution.py:880
  31.6 171.8 %all-gather.8.cloned.1.call-start = ((), (), s32[]{:S(2)}) async-start(), calls=%async_computation.5 | async-start | bytes 2621440 | tf_op jit(solution)/shard_map/all_gather | solution.py:883
  31.7 18.5 %collective-permute-start = (bf16[256,1024]{1,0:T(8,128)(2,1)S(1)}, bf16[256,1024]{1,0:T(8,128)(2,1)S(1)}, u32[]{:S(2)}, u32[]{:S(2)}) collective-permute-start(bf16[256,1024]{1,0:T(8,128)(2,1)S(1)} %copy-done.2), channel_id=1, source_target_pairs={{0,1},{1,0},{2,3},{3,2},{4,5},{5,4},{6,7},{7,6},{8,9},{9,8},{10,11... | collective-permute-start | bytes 1572872 | tf_op jit(solution)/shard_map/ppermute | solution.py:31
  33.6 37.5 %collective-permute-start.1 = (bf16[256,1024]{1,0:T(8,128)(2,1)S(1)}, bf16[256,1024]{1,0:T(8,128)(2,1)}, u32[]{:S(2)}, u32[]{:S(2)}) collective-permute-start(bf16[256,1024]{1,0:T(8,128)(2,1)S(1)} %copy-done.2), channel_id=1, source_target_pairs={{0,2},{2,0},{4,6},{6,4},{1,3},{3,1},{5,7},{7,5},{8,10},{10,8},{12,... | collective-permute-start | bytes 1572872 | tf_op jit(solution)/shard_map/ppermute | solution.py:31
  33.7 14.4 %collective-permute-start.3 = (bf16[256,1024]{1,0:T(8,128)(2,1)S(1)}, bf16[256,1024]{1,0:T(8,128)(2,1)}, u32[]{:S(2)}, u32[]{:S(2)}) collective-permute-start(bf16[256,1024]{1,0:T(8,128)(2,1)S(1)} %copy-done.2), channel_id=1, source_target_pairs={{0,4},{2,6},{4,0},{6,2},{1,5},{3,7},{5,1},{7,3},{8,12},{10,14},{12... | collective-permute-start | bytes 1572872 | tf_op jit(solution)/shard_map/ppermute | solution.py:31
  35.4 507.5 %reduce-scatter.8.cloned.1.call-start = ((), (), s32[]{:S(2)}) async-start(), calls=%async_computation.8 | async-start | bytes 2621440 | tf_op jit(solution)/shard_map/reduce_scatter | solution.py:1092
  48.0 14.3 %collective-permute-start.4 = (bf16[256,1024]{1,0:T(8,128)(2,1)}, bf16[256,1024]{1,0:T(8,128)(2,1)}, u32[]{:S(2)}, u32[]{:S(2)}) collective-permute-start(bf16[256,1024]{1,0:T(8,128)(2,1)} %collective-permute-done.3.refs_4_), channel_id=1, source_target_pairs={{0,1},{1,0},{2,3},{3,2},{4,5},{5,4},{6,7},{7,6},{8,9},{9,8},{10,11... | collective-permute-start | bytes 1572872 | tf_op jit(solution)/shard_map/ppermute | solution.py:31
  50.2 22.3 %collective-permute-start.2 = (bf16[256,1024]{1,0:T(8,128)(2,1)S(1)}, bf16[256,1024]{1,0:T(8,128)(2,1)}, u32[]{:S(2)}, u32[]{:S(2)}) collective-permute-start(bf16[256,1024]{1,0:T(8,128)(2,1)S(1)} %collective-permute-done.refs_1_), channel_id=1, source_target_pairs={{0,2},{2,0},{4,6},{6,4},{1,3},{3,1},{5,7},{7,5},{8,10},{10,8},{12,... | collective-permute-start | bytes 1572872 | tf_op jit(solution)/shard_map/ppermute | solution.py:31
  71.0 14.9 %collective-permute-start.9 = (bf16[4,256,256]{2,1,0:T(8,128)(2,1)}, bf16[4,256,256]{2,1,0:T(8,128)(2,1)S(1)}, u32[]{:S(2)}, u32[]{:S(2)}) collective-permute-start(bf16[4,256,256]{2,1,0:T(8,128)(2,1)} %copy-done.45), channel_id=1, source_target_pairs={{0,4},{2,6},{4,0},{6,2},{1,5},{3,7},{5,1},{7,3},{8,12},{10,14},{12... | collective-permute-start | bytes 1572872 | tf_op jit(solution)/shard_map/ppermute | solution.py:31
  72.5 23.8 %collective-permute-start.10 = (bf16[4,256,256]{2,1,0:T(8,128)(2,1)}, bf16[4,256,256]{2,1,0:T(8,128)(2,1)S(1)}, u32[]{:S(2)}, u32[]{:S(2)}) collective-permute-start(bf16[4,256,256]{2,1,0:T(8,128)(2,1)} %copy-done.44), channel_id=1, source_target_pairs={{0,6},{2,4},{4,2},{6,0},{1,7},{3,5},{5,3},{7,1},{8,14},{10,12},{12... | collective-permute-start | bytes 1572872 | tf_op jit(solution)/shard_map/ppermute | solution.py:31
  80.0 16.3 %collective-permute-start.7 = (bf16[16,2048]{1,0:T(8,128)(2,1)S(1)}, bf16[16,2048]{1,0:T(8,128)(2,1)S(1)}, u32[]{:S(2)}, u32[]{:S(2)}) collective-permute-start(bf16[16,2048]{1,0:T(8,128)(2,1)S(1)} %slice.193), channel_id=1, source_target_pairs={{0,8},{8,16},{16,24},{1,9},{9,17},{17,25},{2,10},{10,18},{18,26},{... | collective-permute-start | bytes 196616 | tf_op jit(solution)/shard_map/ppermute | solution.py:37
  110.1 30.0 %collective-permute-start.18 = (bf16[4,256,256]{2,1,0:T(8,128)(2,1)}, bf16[4,256,256]{2,1,0:T(8,128)(2,1)}, u32[]{:S(2)}, u32[]{:S(2)}) collective-permute-start(bf16[4,256,256]{2,1,0:T(8,128)(2,1)} %get-tuple-element.104), channel_id=1, source_target_pairs={{0,1},{1,0},{2,3},{3,2},{4,5},{5,4},{6,7},{7,6},{8,9},{9,8},{10,11... | collective-permute-start | bytes 1572872 | tf_op jit(solution)/shard_map/ppermute | solution.py:31
  111.6 31.2 %collective-permute-start.19 = (bf16[4,256,256]{2,1,0:T(8,128)(2,1)}, bf16[4,256,256]{2,1,0:T(8,128)(2,1)}, u32[]{:S(2)}, u32[]{:S(2)}) collective-permute-start(bf16[4,256,256]{2,1,0:T(8,128)(2,1)} %copy-done.62), channel_id=1, source_target_pairs={{0,1},{1,0},{2,3},{3,2},{4,5},{5,4},{6,7},{7,6},{8,9},{9,8},{10,11... | collective-permute-start | bytes 1572872 | tf_op jit(solution)/shard_map/ppermute | solution.py:31
  112.2 35.5 %collective-permute-start.20 = (bf16[4,256,256]{2,1,0:T(8,128)(2,1)}, bf16[4,256,256]{2,1,0:T(8,128)(2,1)}, u32[]{:S(2)}, u32[]{:S(2)}) collective-permute-start(bf16[4,256,256]{2,1,0:T(8,128)(2,1)} %copy-done.63), channel_id=1, source_target_pairs={{0,1},{1,0},{2,3},{3,2},{4,5},{5,4},{6,7},{7,6},{8,9},{9,8},{10,11... | collective-permute-start | bytes 1572872 | tf_op jit(solution)/shard_map/ppermute | solution.py:31
  113.7 45.0 %collective-permute-start.21 = (bf16[4,256,256]{2,1,0:T(8,128)(2,1)}, bf16[4,256,256]{2,1,0:T(8,128)(2,1)}, u32[]{:S(2)}, u32[]{:S(2)}) collective-permute-start(bf16[4,256,256]{2,1,0:T(8,128)(2,1)} %copy-done.64), channel_id=1, source_target_pairs={{0,1},{1,0},{2,3},{3,2},{4,5},{5,4},{6,7},{7,6},{8,9},{9,8},{10,11... | collective-permute-start | bytes 1572872 | tf_op jit(solution)/shard_map/ppermute | solution.py:31
  133.1 28.8 %collective-permute-start.28 = (f32[8,512]{1,0:T(8,128)S(1)}, f32[8,512]{1,0:T(8,128)S(1)}, u32[]{:S(2)}, u32[]{:S(2)}) collective-permute-start(f32[8,512]{1,0:T(8,128)S(1)} %get-tuple-element.224), channel_id=1, source_target_pairs={{0,16},{8,24},{1,17},{9,25},{2,18},{10,26},{3,19},{11,27},{4,20},{... | collective-permute-start | bytes 49160 | tf_op jit(solution)/shard_map/ppermute | solution.py:37
  140.2 24.7 %collective-permute-start.29 = (f16[128,512]{1,0:T(8,128)(2,1)S(1)}, f16[128,512]{1,0:T(8,128)(2,1)S(1)}, u32[]{:S(2)}, u32[]{:S(2)}) collective-permute-start(f16[128,512]{1,0:T(8,128)(2,1)S(1)} %multiply_convert_fusion.3), channel_id=1, source_target_pairs={{0,24},{1,25},{2,26},{3,27},{4,28},{5,29},{6,30},{7,31}} | collective-permute-start | bytes 393224 | tf_op jit(solution)/shard_map/ppermute | solution.py:37
  142.9 22.0 %collective-permute-start.27 = (f16[128,512]{1,0:T(8,128)(2,1)S(1)}, f16[128,512]{1,0:T(8,128)(2,1)S(1)}, u32[]{:S(2)}, u32[]{:S(2)}) collective-permute-start(f16[128,512]{1,0:T(8,128)(2,1)S(1)} %multiply_convert_fusion.3), channel_id=1, source_target_pairs={{0,16},{8,24},{1,17},{9,25},{2,18},{10,26},{3,19},{11,27},{4,20},{... | collective-permute-start | bytes 393224 | tf_op jit(solution)/shard_map/ppermute | solution.py:37
  147.7 17.1 %collective-permute-start.25 = (f16[128,512]{1,0:T(8,128)(2,1)S(1)}, f16[128,512]{1,0:T(8,128)(2,1)S(1)}, u32[]{:S(2)}, u32[]{:S(2)}) collective-permute-start(f16[128,512]{1,0:T(8,128)(2,1)S(1)} %multiply_convert_fusion.3), channel_id=1, source_target_pairs={{0,8},{8,16},{16,24},{1,9},{9,17},{17,25},{2,10},{10,18},{18,26},{... | collective-permute-start | bytes 393224 | tf_op jit(solution)/shard_map/ppermute | solution.py:37
  179.2 24.2 %collective-permute-start.35 = (bf16[1024,512]{1,0:T(8,128)(2,1)}, bf16[1024,512]{1,0:T(8,128)(2,1)}, u32[]{:S(2)}, u32[]{:S(2)}) collective-permute-start(bf16[1024,512]{1,0:T(8,128)(2,1)} %get-tuple-element.103.refs_0_), channel_id=1, source_target_pairs={{0,4},{2,6},{4,0},{6,2},{1,5},{3,7},{5,1},{7,3},{8,12},{10,14},{12... | collective-permute-start | bytes 3145736 | tf_op jit(solution)/shard_map/ppermute | solution.py:31
  180.7 48.6 %collective-permute-start.34 = (bf16[1024,512]{1,0:T(8,128)(2,1)}, bf16[1024,512]{1,0:T(8,128)(2,1)}, u32[]{:S(2)}, u32[]{:S(2)}) collective-permute-start(bf16[1024,512]{1,0:T(8,128)(2,1)} %get-tuple-element.103.refs_0_), channel_id=1, source_target_pairs={{0,2},{2,0},{4,6},{6,4},{1,3},{3,1},{5,7},{7,5},{8,10},{10,8},{12,... | collective-permute-start | bytes 3145736 | tf_op jit(solution)/shard_map/ppermute | solution.py:31
  203.4 25.9 %collective-permute-start.36 = (bf16[1024,512]{1,0:T(8,128)(2,1)}, bf16[1024,512]{1,0:T(8,128)(2,1)}, u32[]{:S(2)}, u32[]{:S(2)}) collective-permute-start(bf16[1024,512]{1,0:T(8,128)(2,1)} %collective-permute-done.35.refs_2_), channel_id=1, source_target_pairs={{0,2},{2,0},{4,6},{6,4},{1,3},{3,1},{5,7},{7,5},{8,10},{10,8},{12,... | collective-permute-start | bytes 3145736 | tf_op jit(solution)/shard_map/ppermute | solution.py:31
  225.6 14.2 %collective-permute-start.31 = (f32[4,1024]{1,0:T(4,128)S(1)}, f32[4,1024]{1,0:T(4,128)S(1)}, u32[]{:S(2)}, u32[]{:S(2)}) collective-permute-start(f32[4,1024]{1,0:T(4,128)S(1)} %slice.222), channel_id=1, source_target_pairs={{0,2},{2,0},{4,6},{6,4},{1,3},{3,1},{5,7},{7,5},{8,10},{10,8},{12,... | collective-permute-start | bytes 49160 | tf_op jit(solution)/shard_map/ppermute | solution.py:31
  271.2 13.6 %collective-permute-start.42 = (f32[1024,512]{1,0:T(8,128)}, f32[1024,512]{1,0:T(8,128)}, u32[]{:S(2)}, u32[]{:S(2)}) collective-permute-start(f32[1024,512]{1,0:T(8,128)} %get-tuple-element.121), channel_id=1, source_target_pairs={{0,2},{2,0},{4,6},{6,4},{1,3},{3,1},{5,7},{7,5},{8,10},{10,8},{12,... | collective-permute-start | bytes 6291464 | tf_op jit(solution)/shard_map/ppermute | solution.py:31
  279.1 296.3 %reduce-scatter.4.cloned.1.call-start = ((), (), s32[]{:S(2)}) async-start(), calls=%async_computation.6 | async-start | bytes 2621440 | tf_op jit(solution)/shard_map/reduce_scatter | solution.py:1118
  279.5 48.4 %collective-permute-start.37 = (bf16[4,4,256,256]{3,2,1,0:T(8,128)(2,1)}, bf16[4,4,256,256]{3,2,1,0:T(8,128)(2,1)}, u32[]{:S(2)}, u32[]{:S(2)}) collective-permute-start(bf16[4,4,256,256]{3,2,1,0:T(8,128)(2,1)} %get-tuple-element.113), channel_id=1, source_target_pairs={{0,1},{1,0},{2,3},{3,2},{4,5},{5,4},{6,7},{7,6},{8,9},{9,8},{10,11... | collective-permute-start | bytes 6291464 | tf_op jit(solution)/shard_map/ppermute | solution.py:31
  281.1 53.7 %collective-permute-start.41 = (f32[1024,512]{1,0:T(8,128)}, f32[1024,512]{1,0:T(8,128)}, u32[]{:S(2)}, u32[]{:S(2)}) collective-permute-start(f32[1024,512]{1,0:T(8,128)} %copy-done.42), channel_id=1, source_target_pairs={{0,2},{2,0},{4,6},{6,4},{1,3},{3,1},{5,7},{7,5},{8,10},{10,8},{12,... | collective-permute-start | bytes 6291464 | tf_op jit(solution)/shard_map/ppermute | solution.py:31
  288.7 46.1 %collective-permute-start.44 = (f16[1024,512]{1,0:T(8,128)(2,1)}, f16[1024,512]{1,0:T(8,128)(2,1)}, u32[]{:S(2)}, u32[]{:S(2)}) collective-permute-start(f16[1024,512]{1,0:T(8,128)(2,1)} %multiply_convert_fusion), channel_id=1, source_target_pairs={{0,4},{2,6},{4,0},{6,2},{1,5},{3,7},{5,1},{7,3},{8,12},{10,14},{12... | collective-permute-start | bytes 3145736 | tf_op jit(solution)/shard_map/ppermute | solution.py:31
  293.8 20.9 %collective-permute-start.45 = (f32[8,512]{1,0:T(8,128)S(1)}, f32[8,512]{1,0:T(8,128)S(1)}, u32[]{:S(2)}, u32[]{:S(2)}) collective-permute-start(f32[8,512]{1,0:T(8,128)S(1)} %broadcast_in_dim.134), channel_id=1, source_target_pairs={{0,4},{2,6},{4,0},{6,2},{1,5},{3,7},{5,1},{7,3},{8,12},{10,14},{12... | collective-permute-start | bytes 49160 | tf_op jit(solution)/shard_map/ppermute | solution.py:31
  333.4 128.4 %collective-permute-start.38 = (bf16[4,256,256]{2,1,0:T(8,128)(2,1)}, bf16[4,256,256]{2,1,0:T(8,128)(2,1)}, u32[]{:S(2)}, u32[]{:S(2)}) collective-permute-start(bf16[4,256,256]{2,1,0:T(8,128)(2,1)} %get-tuple-element.115), channel_id=1, source_target_pairs={{0,2},{2,0},{4,6},{6,4},{1,3},{3,1},{5,7},{7,5},{8,10},{10,8},{12,... | collective-permute-start | bytes 1572872 | tf_op jit(solution)/shard_map/ppermute | solution.py:31
  333.4 129.1 %collective-permute-start.39 = (bf16[4,256,256]{2,1,0:T(8,128)(2,1)}, bf16[4,256,256]{2,1,0:T(8,128)(2,1)}, u32[]{:S(2)}, u32[]{:S(2)}) collective-permute-start(bf16[4,256,256]{2,1,0:T(8,128)(2,1)} %get-tuple-element.116), channel_id=1, source_target_pairs={{0,4},{2,6},{4,0},{6,2},{1,5},{3,7},{5,1},{7,3},{8,12},{10,14},{12... | collective-permute-start | bytes 1572872 | tf_op jit(solution)/shard_map/ppermute | solution.py:31
  347.4 43.6 %collective-permute-start.53 = (f16[128,512]{1,0:T(8,128)(2,1)}, f16[128,512]{1,0:T(8,128)(2,1)}, u32[]{:S(2)}, u32[]{:S(2)}) collective-permute-start(f16[128,512]{1,0:T(8,128)(2,1)} %multiply_convert_fusion.2), channel_id=1, source_target_pairs={{24,0},{25,1},{26,2},{27,3},{28,4},{29,5},{30,6},{31,7}} | collective-permute-start | bytes 393224 | tf_op jit(solution)/shard_map/ppermute | solution.py:37
  348.7 42.4 %collective-permute-start.51 = (f16[128,512]{1,0:T(8,128)(2,1)}, f16[128,512]{1,0:T(8,128)(2,1)}, u32[]{:S(2)}, u32[]{:S(2)}) collective-permute-start(f16[128,512]{1,0:T(8,128)(2,1)} %multiply_convert_fusion.2), channel_id=1, source_target_pairs={{16,0},{24,8},{17,1},{25,9},{18,2},{26,10},{19,3},{27,11},{20,4},{... | collective-permute-start | bytes 393224 | tf_op jit(solution)/shard_map/ppermute | solution.py:37
  354.8 230.3 %reduce-scatter.6.cloned.1.call-start = ((), (), s32[]{:S(2)}) async-start(), calls=%async_computation.7 | async-start | bytes 2621440 | tf_op jit(solution)/shard_map/reduce_scatter | solution.py:1230
  355.5 15.6 %collective-permute-start.52 = (f32[8,512]{1,0:T(8,128)S(1)}, f32[8,512]{1,0:T(8,128)S(1)}, u32[]{:S(2)}, u32[]{:S(2)}) collective-permute-start(f32[8,512]{1,0:T(8,128)S(1)} %fusion.31), channel_id=1, source_target_pairs={{16,0},{24,8},{17,1},{25,9},{18,2},{26,10},{19,3},{27,11},{20,4},{... | collective-permute-start | bytes 49160 | tf_op jit(solution)/shard_map/ppermute | solution.py:37
  389.7 15.0 %collective-permute-start.49 = (f16[128,512]{1,0:T(8,128)(2,1)}, f16[128,512]{1,0:T(8,128)(2,1)S(1)}, u32[]{:S(2)}, u32[]{:S(2)}) collective-permute-start(f16[128,512]{1,0:T(8,128)(2,1)} %multiply_convert_fusion.2), channel_id=1, source_target_pairs={{8,0},{16,8},{24,16},{9,1},{17,9},{25,17},{10,2},{18,10},{26,18},{... | collective-permute-start | bytes 393224 | tf_op jit(solution)/shard_map/ppermute | solution.py:37
  391.0 71.5 %collective-permute-start.40 = (bf16[4,256,256]{2,1,0:T(8,128)(2,1)}, bf16[4,256,256]{2,1,0:T(8,128)(2,1)}, u32[]{:S(2)}, u32[]{:S(2)}) collective-permute-start(bf16[4,256,256]{2,1,0:T(8,128)(2,1)} %copy-done.43), channel_id=1, source_target_pairs={{0,6},{2,4},{4,2},{6,0},{1,7},{3,5},{5,3},{7,1},{8,14},{10,12},{12... | collective-permute-start | bytes 1572872 | tf_op jit(solution)/shard_map/ppermute | solution.py:31
  431.5 24.4 %collective-permute-start.85 = (f32[12,512]{1,0:T(8,128)S(1)}, f32[12,512]{1,0:T(8,128)S(1)}, u32[]{:S(2)}, u32[]{:S(2)}) collective-permute-start(f32[12,512]{1,0:T(8,128)S(1)} %fusion.85), channel_id=1, source_target_pairs={{0,16},{8,24},{16,0},{24,8},{1,17},{9,25},{17,1},{25,9},{2,18},{10... | collective-permute-start | bytes 73736 | tf_op jit(solution)/shard_map/ppermute | solution.py:31
  455.8 18.2 %collective-permute-start.57 = (bf16[256,2048]{1,0:T(8,128)(2,1)}, bf16[256,2048]{1,0:T(8,128)(2,1)S(1)}, u32[]{:S(2)}, u32[]{:S(2)}) collective-permute-start(bf16[256,2048]{1,0:T(8,128)(2,1)} %get-tuple-element.146), channel_id=1, source_target_pairs={{0,2},{2,0},{4,6},{6,4},{1,3},{3,1},{5,7},{7,5},{8,10},{10,8},{12,... | collective-permute-start | bytes 3145736 | tf_op jit(solution)/shard_map/ppermute | solution.py:31
  467.0 48.9 %collective-permute-start.56 = (bf16[256,2048]{1,0:T(8,128)(2,1)S(1)}, bf16[256,2048]{1,0:T(8,128)(2,1)}, u32[]{:S(2)}, u32[]{:S(2)}) collective-permute-start(bf16[256,2048]{1,0:T(8,128)(2,1)S(1)} %get-tuple-element.144), channel_id=1, source_target_pairs={{0,2},{2,0},{4,6},{6,4},{1,3},{3,1},{5,7},{7,5},{8,10},{10,8},{12,... | collective-permute-start | bytes 3145736 | tf_op jit(solution)/shard_map/ppermute | solution.py:31
  467.7 15.2 %collective-permute-start.88 = (f32[4,12,512]{2,1,0:T(8,128)S(1)}, f32[4,12,512]{2,1,0:T(8,128)S(1)}, u32[]{:S(2)}, u32[]{:S(2)}) collective-permute-start(f32[4,12,512]{2,1,0:T(8,128)S(1)} %maximum_select_fusion.7), channel_id=1, source_target_pairs={{0,4},{2,6},{4,0},{6,2},{1,5},{3,7},{5,1},{7,3},{8,12},{10,14},{12... | collective-permute-start | bytes 294920 | tf_op jit(solution)/shard_map/ppermute | solution.py:31
  476.9 39.0 %collective-permute-start.58 = (bf16[256,2048]{1,0:T(8,128)(2,1)}, bf16[256,2048]{1,0:T(8,128)(2,1)}, u32[]{:S(2)}, u32[]{:S(2)}) collective-permute-start(bf16[256,2048]{1,0:T(8,128)(2,1)} %add_convert_fusion), channel_id=1, source_target_pairs={{0,4},{2,6},{4,0},{6,2},{1,5},{3,7},{5,1},{7,3},{8,12},{10,14},{12... | collective-permute-start | bytes 3145736 | tf_op jit(solution)/shard_map/ppermute | solution.py:31
  480.8 33.5 %collective-permute-start.77 = (bf16[1024,256]{1,0:T(8,128)(2,1)}, bf16[1024,256]{1,0:T(8,128)(2,1)S(1)}, u32[]{:S(2)}, u32[]{:S(2)}) collective-permute-start(bf16[1024,256]{1,0:T(8,128)(2,1)} %get-tuple-element.157), channel_id=1, source_target_pairs={{0,4},{2,6},{4,0},{6,2},{1,5},{3,7},{5,1},{7,3},{8,12},{10,14},{12... | collective-permute-start | bytes 1572872 | tf_op jit(solution)/shard_map/ppermute | solution.py:31
  481.5 56.2 %collective-permute-start.75 = (f32[2,8,2048]{2,1,0:T(8,128)S(1)}, f32[2,8,2048]{2,1,0:T(8,128)}, u32[]{:S(2)}, u32[]{:S(2)}) collective-permute-start(f32[2,8,2048]{2,1,0:T(8,128)S(1)} %maximum_select_fusion.6), channel_id=1, source_target_pairs={{0,4},{2,6},{4,0},{6,2},{1,5},{3,7},{5,1},{7,3},{8,12},{10,14},{12... | collective-permute-start | bytes 393224 | tf_op jit(solution)/shard_map/ppermute | solution.py:31
  514.5 14.9 %collective-permute-start.78 = (bf16[1024,256]{1,0:T(8,128)(2,1)S(1)}, bf16[1024,256]{1,0:T(8,128)(2,1)S(1)}, u32[]{:S(2)}, u32[]{:S(2)}) collective-permute-start(bf16[1024,256]{1,0:T(8,128)(2,1)S(1)} %fusion.16), channel_id=1, source_target_pairs={{0,1},{1,0},{2,3},{3,2},{4,5},{5,4},{6,7},{7,6},{8,9},{9,8},{10,11... | collective-permute-start | bytes 1572872 | tf_op jit(solution)/shard_map/ppermute | solution.py:31
  519.0 26.0 %collective-permute-start.59 = (bf16[256,1024]{1,0:T(8,128)(2,1)}, bf16[256,1024]{1,0:T(8,128)(2,1)S(1)}, u32[]{:S(2)}, u32[]{:S(2)}) collective-permute-start(bf16[256,1024]{1,0:T(8,128)(2,1)} %dynamic-slice_convert_fusion), channel_id=1, source_target_pairs={{0,1},{1,0},{2,3},{3,2},{4,5},{5,4},{6,7},{7,6},{8,9},{9,8},{10,11... | collective-permute-start | bytes 1572872 | tf_op jit(solution)/shard_map/ppermute | solution.py:31
  561.4 13.8 %collective-permute-start.83 = (bf16[4,256,256]{2,1,0:T(8,128)(2,1)S(1)}, bf16[4,256,256]{2,1,0:T(8,128)(2,1)S(1)}, u32[]{:S(2)}, u32[]{:S(2)}) collective-permute-start(bf16[4,256,256]{2,1,0:T(8,128)(2,1)S(1)} %maximum_select_fusion.1), channel_id=1, source_target_pairs={{0,4},{2,6},{4,0},{6,2},{1,5},{3,7},{5,1},{7,3},{8,12},{10,14},{12... | collective-permute-start | bytes 1572872 | tf_op jit(solution)/shard_map/ppermute | solution.py:31
  (137 other events, 1497.1 us)
Sparse Core Ops, SparseCore 0:
  21.2 49.2 all-gather.3
  72.0 44.7 all-gather.5
  118.4 51.8 all-gather.7
  279.2 48.5 reduce-scatter.7
  354.9 53.1 reduce-scatter.3
  467.7 42.0 reduce-scatter.5

commit v2 on v1

v2 whole, which is shorter than its diff:
```python
from functools import partial

import jax
import jax.numpy as jnp
from jax import lax
from jax.experimental import pallas as pl
from jax.experimental.pallas import tpu as pltpu
from jax.sharding import Mesh
from jax.sharding import PartitionSpec as P

D = 2048
P_SIZE = 64
STATE = 128
KERNEL = 4
INNER = 4096
CHUNK = 128
SUB = 2
PLANE = 4

HALF_TOP = 16384.0

eps = 1e-05
bf16 = jnp.bfloat16
f32 = jnp.float32
high = lax.Precision.HIGHEST
PARAMS = pltpu.CompilerParams(
    vmem_limit_bytes=58 * 1024 * 1024, dimension_semantics=("arbitrary",)
)


def swap(block, axis, bit):
    return lax.ppermute(block, axis, [(a, a ^ bit) for a in range(lax.axis_size(axis))])


def shifted(block, axis, distance):
    devices = range(lax.axis_size(axis))
    route = [(a - distance, a) for a in devices if a - distance in devices]
    return lax.ppermute(block, axis, route)


def scattered_inner(blocks):
    place = lax.axis_index("i")
    got = {0: take(blocks, place)}
    for bit in (2, 3, 1):
        got[bit] = swap(take(blocks, place ^ bit), "i", bit)
    return [got[r] for r in range(PLANE)]


def bits_of(axis):
    count = lax.axis_size(axis)
    return [1 << b for b in range(count.bit_length() - 1)]


def take(values, index, axis=0):
    return lax.dynamic_index_in_dim(values, index, axis, keepdims=False)


def put(buffer, piece, index):
    return lax.dynamic_update_index_in_dim(buffer, piece, index, 0)


def add_all(value, axes):
    for axis in axes:
        for bit in bits_of(axis):
            value = value + swap(value, axis, bit)
    return value


def add_inner(value, bit):
    return value + swap(value, "i", bit)


def stack_over(value, axis, bit, at):
    other = swap(value, axis, bit)
    upper = (lax.axis_index(axis) & bit) != 0
    return jnp.where(
        upper, jnp.stack([other, value], axis=at), jnp.stack([value, other], axis=at)
    )


def stack_plane(value):
    shape = value.shape
    count = lax.axis_size("h")
    for bit in bits_of("h"):
        value = stack_over(value, "h", bit, 0)
        value = value.reshape((-1,) + shape) if bit > 1 else value
    value = value.reshape((count,) + shape)
    value = stack_over(value, "i", 2, 0)
    value = stack_over(value, "i", 1, 1)
    return value.reshape((PLANE, count) + shape)


def stack_planes(value):
    shape = value.shape
    for bit in bits_of("o"):
        value = stack_over(value, "o", bit, 0)
        value = value.reshape((-1,) + shape)
    return value


def stack_inner(value):
    shape = value.shape
    value = stack_over(value, "i", 2, 0)
    return stack_over(value, "i", 1, 1).reshape((PLANE,) + shape)


def exchange_inner(blocks):
    place = lax.axis_index("i")
    out = blocks
    for bit in (2, 3, 1):
        out = put(out, swap(take(blocks, place ^ bit), "i", bit), place ^ bit)
    return out


def scatter_heads(values, axis):
    count = lax.axis_size("h")
    if count != 2:
        return lax.psum_scatter(values, "h", scatter_dimension=axis, tiled=True)
    place = lax.axis_index("h")
    width = values.shape[axis] // 2
    sent = lax.dynamic_slice_in_dim(values, (1 - place) * width, width, axis)
    kept = lax.dynamic_slice_in_dim(values, place * width, width, axis)
    return kept + swap(sent.astype(bf16), "h", 1).astype(f32)


def column_power(values):
    largest = jnp.max(jnp.abs(values), axis=0, keepdims=True)
    exponent = jnp.ceil(jnp.log2(jnp.clip(largest, 1e-30, 1e30)))
    return jnp.exp2(exponent), exponent


def split_rows(values):
    upper = lax.reduce_precision(values, 8, 7)
    return upper.astype(bf16), (values - upper).astype(bf16)


def pack_half(values, extra=()):
    power, exponent = column_power(values)
    rows = [exponent]
    for row in extra:
        first = lax.reduce_precision(row, 5, 10)
        rows += [first, (row - first) * 2048.0]
    rows.append(jnp.zeros((16 - len(rows), values.shape[1]), f32))
    return jnp.concatenate([values * (HALF_TOP / power)] + rows, axis=0).astype(jnp.float16)


def unpack_half(packed):
    rows = packed.shape[0] - 16
    tail = packed[rows:].astype(f32)
    values = packed[:rows].astype(f32) * (jnp.exp2(tail[0:1]) / HALF_TOP)
    return values, tail[1:2] + tail[2:3] / 2048.0


def chain(state, decay_wide, direction):
    packed = pack_half(state, (decay_wide,))
    total = None
    for distance in range(lax.axis_size("o") - 1, 0, -1):
        own, decay = unpack_half(shifted(packed, "o", direction * distance))
        total = own if total is None else own + decay * total
    return total


def mm(a, b):
    return jnp.dot(a, b, preferred_element_type=f32)


def mm_two(a, b):
    upper, lower = split_two(b)
    return mm(a, upper) + mm(a, lower)


def mm_three(a, b):
    a_up, a_low = split_two(a)
    b_up, b_low = split_two(b)
    return mm_t(a_up, b_up) + mm_t(a_up, b_low) + mm_t(a_low, b_up)


def mm_t(a, b):
    return lax.dot_general(a, b, (((1,), (1,)), ((), ())), preferred_element_type=f32)


def t_mm(a, b):
    return lax.dot_general(a, b, (((0,), (0,)), ((), ())), preferred_element_type=f32)


def head_mask(groups, width):
    head = lax.broadcasted_iota(jnp.int32, (groups, width), 0)
    lane = lax.broadcasted_iota(jnp.int32, (groups, width), 1)
    return (lane // P_SIZE == head).astype(f32).astype(bf16)


def split_two(values):
    upper = values.astype(bf16)
    return upper, (values - upper.astype(f32)).astype(bf16)


def widen(values, mask):
    upper, lower = split_two(values)
    return mm(upper, mask) + mm(lower, mask)


def fold(values, mask):
    upper, lower = split_two(values)
    return mm_t(upper, mask) + mm_t(lower, mask)


def pair_masks():
    lane = lax.broadcasted_iota(jnp.int32, (1, 2 * P_SIZE), 1)
    lower = (lane < P_SIZE).astype(f32)
    return lower.astype(bf16), (1.0 - lower).astype(bf16)


def rows_cols():
    row = lax.broadcasted_iota(jnp.int32, (CHUNK, CHUNK), 0)
    col = lax.broadcasted_iota(jnp.int32, (CHUNK, CHUNK), 1)
    return row, col


def within_kernel(groups, turn, x_ref, st_ref, col_ref, row_ref, y_ref):
    b_in = st_ref[:, :STATE]
    c_out = st_ref[:, STATE:]
    scores = mm_t(c_out, b_in)
    doc_col = col_ref[:, 3 * groups : 3 * groups + 1]
    doc_row = row_ref[2 * groups : 2 * groups + 1, :]
    row, col = rows_cols()
    bias = jnp.where((doc_col == doc_row) & (row >= col), 0.0, -1e30)
    masks = pair_masks()
    for pair in range(groups // 2):
        lanes = slice(pair * 2 * P_SIZE, (pair + 1) * 2 * P_SIZE)
        x_pair = x_ref[:, lanes]
        weights, values = [], []
        for side in range(2):
            h = 2 * pair + side
            spread = jnp.exp(col_ref[:, h : h + 1] - row_ref[h : h + 1, :] + bias)
            weights.append(split_two(scores * spread * row_ref[groups + h : groups + h + 1, :]))
            values.append(x_pair * masks[side])
        value = jnp.concatenate(values, axis=0)
        y_ref[:, lanes] = mm(
            jnp.concatenate([weights[0][0], weights[1][0]], axis=1), value
        ) + mm(jnp.concatenate([weights[0][1], weights[1][1]], axis=1), value)


def carry_kernel(
    groups, turn,
    x_ref,
    st_ref,
    stt_ref,
    col_ref,
    yl_ref,
    gz_ref,
    inc_ref,
    wide_ref,
    level_ref,
    v_ref,
    u_ref,
    sq_ref,
    enter_ref,
    state,
):
    @pl.when(turn == 0)
    def _():
        state[...] = inc_ref[...]

    width = x_ref.shape[1]
    mask = head_mask(groups, width)
    cum = col_ref[:, :groups]
    step = col_ref[:, groups : 2 * groups]
    from_start = col_ref[:, 3 * groups + 1 : 3 * groups + 2]
    to_end = col_ref[:, 3 * groups + 2 : 3 * groups + 3]
    cum_last = cum[CHUNK - 1 : CHUNK, :]
    entry = jnp.exp(cum) * from_start
    ending = jnp.exp(cum_last - cum) * to_end * step
    entry_wide = widen(entry, mask)
    ending_wide = widen(ending, mask)
    held = state[...]
    enter_ref[...] = held
    carried = mm_two(st_ref[:, STATE:], held)
    x_wide = x_ref[...].astype(f32)
    v = yl_ref[...] + entry_wide * carried + wide_ref[0:1, :] * x_wide
    v_ref[...] = v
    z = gz_ref[...].astype(f32)
    gated = v * (z * jax.nn.sigmoid(z))
    u_ref[...] = (gated * wide_ref[1:2, :]).astype(bf16)
    upper, lower = split_two(gated * gated)
    sq_ref[...] = mm_t(level_ref[...], upper) + mm_t(level_ref[...], lower)
    added = mm_two(stt_ref[:STATE, :], x_wide * ending_wide)
    state[...] = entry_wide[CHUNK - 1 : CHUNK, :] * held + added


def gate_back_kernel(
    groups, turn,
    ug_ref,
    v_ref,
    gz_ref,
    x_ref,
    stt_ref,
    col_ref,
    dot_ref,
    scale_ref,
    wide_ref,
    level_ref,
    yg_ref,
    zg_ref,
    acc_ref,
    lam_ref,
):
    @pl.when(turn == 0)
    def _():
        acc_ref[...] = jnp.zeros_like(acc_ref)
        lam_ref[...] = jnp.zeros_like(lam_ref)

    mask = head_mask(groups, x_ref.shape[1])
    v = v_ref[...]
    z = gz_ref[...].astype(f32)
    sig = jax.nn.sigmoid(z)
    silu = z * sig
    gated = v * silu
    ug = ug_ref[...]
    level = lax.broadcasted_iota(jnp.int32, dot_ref.shape, 0)
    factor = jnp.zeros(dot_ref.shape, f32)
    for m in range(4):
        factor = jnp.where(level == m, -0.5 / (INNER >> m), factor)
    scale = scale_ref[...]
    upper, lower = split_two(dot_ref[...] * scale * scale * scale * factor)
    stat = t_mm(upper, level_ref[...]) + t_mm(lower, level_ref[...])
    gated_grad = ug * wide_ref[1:2, :] + 2.0 * gated * stat
    y_grad = gated_grad * silu
    yg_ref[...] = y_grad
    zg_ref[...] = (gated_grad * v * (sig * (1.0 + z * (1.0 - sig)))).astype(bf16)
    acc_ref[0:1, :] += jnp.sum(ug * gated, axis=0, keepdims=True)
    acc_ref[1:2, :] += jnp.sum(y_grad * x_ref[...].astype(f32), axis=0, keepdims=True)
    whole_entry = widen(col_ref[:, 2 * groups : 3 * groups], mask)
    lam_ref[...] += mm_two(stt_ref[STATE:, :], y_grad * whole_entry)


def within_back_kernel(groups, turn, x_ref, st_ref, col_ref, row_ref, yg_ref, dx_ref, dbc_ref, ds_ref):
    b_in = st_ref[:, :STATE]
    c_out = st_ref[:, STATE:]
    scores = mm_t(b_in, c_out)
    doc_col = col_ref[:, 3 * groups : 3 * groups + 1]
    doc_row = row_ref[2 * groups : 2 * groups + 1, :]
    row, col = rows_cols()
    same = doc_col == doc_row
    bias = jnp.where(same & (row <= col), 0.0, -1e30)
    masks = pair_masks()
    total = jnp.zeros((CHUNK, CHUNK), f32)
    head_lane = lax.broadcasted_iota(jnp.int32, (CHUNK, groups), 1)
    head_row = lax.broadcasted_iota(jnp.int32, (groups, CHUNK), 0)
    size_part = jnp.zeros((CHUNK, groups), f32)
    out_part = jnp.zeros((groups, CHUNK), f32)
    for pair in range(groups // 2):
        lanes = slice(pair * 2 * P_SIZE, (pair + 1) * 2 * P_SIZE)
        x_pair = x_ref[:, lanes]
        y_pair, y_rest = split_two(yg_ref[:, lanes])
        weights, values = [], []
        for side in range(2):
            h = 2 * pair + side
            step = col_ref[:, groups + h : groups + h + 1]
            spread = jnp.exp(row_ref[h : h + 1, :] - col_ref[:, h : h + 1] + bias)
            y_side = y_pair * masks[side]
            paired = spread * (mm_t(x_pair, y_side) + mm_t(x_pair, y_rest * masks[side]))
            total = total + step * paired
            product = scores * paired
            size_part = jnp.where(
                head_lane == h, jnp.sum(product, axis=1, keepdims=True), size_part
            )
            out_part = jnp.where(
                head_row == h, jnp.sum(step * product, axis=0, keepdims=True), out_part
            )
            weights.append((scores * spread).astype(bf16))
            values.append(y_side)
        dx_ref[:, lanes] = mm(jnp.concatenate(weights, axis=1), jnp.concatenate(values, axis=0))
    upper, lower = split_two(total)
    dbc_ref[:, :STATE] = mm(upper, c_out) + mm(lower, c_out)
    dbc_ref[:, STATE:] = t_mm(upper, b_in) + t_mm(lower, b_in)
    later = (same & (row <= col)).astype(f32)
    step_all = col_ref[:, groups : 2 * groups]
    ds_ref[:, :groups] = size_part
    ds_ref[:, groups:] = lax.dot_general(
        later, out_part, (((1,), (1,)), ((), ())), precision=high, preferred_element_type=f32
    ) - jnp.dot(later, step_all * size_part, precision=high, preferred_element_type=f32)


def conv_back_step(act_grad, pre, value, taps_ref, match, next_ref, sum_ref):
    sig = jax.nn.sigmoid(pre)
    slope = act_grad * (sig * (1.0 + pre * (1.0 - sig)))
    sum_ref[4:5, :] += jnp.sum(slope, axis=0, keepdims=True)
    sum_ref[3:4, :] += jnp.sum(slope * value, axis=0, keepdims=True)
    grad = taps_ref[3:4, :] * slope
    row = lax.broadcasted_iota(jnp.int32, (8, pre.shape[1]), 0)
    for k in range(KERNEL - 1):
        reach = KERNEL - 1 - k
        rolled = pltpu.roll(slope * match[k], CHUNK - reach, 0)
        last = rolled[CHUNK - 8 :]
        keep = row < 8 - reach
        after = next_ref[k * 8 : k * 8 + 8, :]
        moved = jnp.concatenate([rolled[: CHUNK - 8], jnp.where(keep, last, after)], axis=0)
        next_ref[k * 8 : k * 8 + 8, :] = jnp.where(keep, 0.0, last)
        grad = grad + taps_ref[k : k + 1, :] * moved
        sum_ref[k : k + 1, :] += jnp.sum(value * moved, axis=0, keepdims=True)
    return grad


def conv_back_edge(halo_ref, taps_ref, next_ref, sum_ref, edge_ref):
    value = halo_ref[...].astype(f32)[8:]
    edge = 0.0
    for k in range(KERNEL - 1):
        after = next_ref[k * 8 : k * 8 + 8, :]
        edge = edge + taps_ref[k : k + 1, :] * after
        sum_ref[k : k + 1, :] += jnp.sum(value * after, axis=0, keepdims=True)
    edge_ref[...] = edge


def carry_back_kernel(
    groups,
    turns,
    step_index,
    x_ref,
    st_ref,
    stt_ref,
    col_ref,
    row_ref,
    yg_ref,
    dxl_ref,
    dbcl_ref,
    dsl_ref,
    enter_ref,
    lam_ref,
    wide_ref,
    pre_ref,
    value_ref,
    halo_ref,
    taps_ref,
    pre_state_ref,
    value_state_ref,
    halo_state_ref,
    taps_state_ref,
    rate_ref,
    wide_sum_ref,
    grad_ref,
    tail_ref,
    edge_ref,
    sum_ref,
    grad_state_ref,
    grad_state_t_ref,
    step_grad_ref,
    adjoint,
    next_ref,
    next_state_ref,
):
    width = x_ref.shape[1]
    state_at = 2 * width
    step_at = state_at + 2 * STATE
    sum_inner_ref = sum_ref.at[:, :width]
    sum_state_ref = sum_ref.at[:, state_at:step_at]

    @pl.when(step_index == turns)
    def _():
        sum_ref[:, width:state_at] = wide_sum_ref[...]
        conv_back_edge(halo_ref, taps_ref, next_ref, sum_inner_ref, edge_ref.at[:, :width])
        edge_state_ref = edge_ref.at[:, width:]
        conv_back_edge(halo_state_ref, taps_state_ref, next_state_ref, sum_state_ref, edge_state_ref)
        edge = edge_state_ref[...]
        edge = jnp.concatenate([edge, jnp.zeros((CHUNK - 8, edge.shape[1]), f32)], axis=0)
        grad_state_t_ref[...] = jnp.transpose(edge)

    @pl.when(step_index == 0)
    def _():
        adjoint[...] = lam_ref[...]
        next_ref[...] = jnp.zeros_like(next_ref)
        next_state_ref[...] = jnp.zeros_like(next_state_ref)
        sum_ref[...] = jnp.zeros_like(sum_ref)

    @pl.when(step_index < turns)
    def _():
        mask = head_mask(groups, width)
        cum = col_ref[:, :groups]
        step = col_ref[:, groups : 2 * groups]
        from_start = col_ref[:, 3 * groups + 1 : 3 * groups + 2]
        to_end = col_ref[:, 3 * groups + 2 : 3 * groups + 3]
        inside = col_ref[:, 3 * groups + 3 : 3 * groups + 4]
        match = [col_ref[:, 3 * groups + 4 + k : 3 * groups + 5 + k] for k in range(KERNEL - 1)]
        cum_last = cum[CHUNK - 1 : CHUNK, :]
        entry = jnp.exp(cum) * from_start
        ending = jnp.exp(cum_last - cum) * to_end
        entry_wide = widen(entry, mask)
        ending_wide = widen(ending, mask)
        step_wide = widen(step, mask)
        y_grad = yg_ref[...]
        entered = enter_ref[...]
        held = adjoint[...]
        y_entry = y_grad * entry_wide
        out_grad = dbcl_ref[:, STATE:] + mm_three(y_entry, entered)
        out_carry = fold(y_entry * mm_two(st_ref[:, STATE:], entered), mask)
        x_wide = x_ref[...].astype(f32)
        back = ending_wide * mm_two(st_ref[:, :STATE], held)
        act_grad = step_wide * (dxl_ref[...] + back) + wide_ref[0:1, :] * y_grad
        in_grad = dbcl_ref[:, :STATE] + mm_three(x_wide * ending_wide * step_wide, held)
        size_carry = fold(x_wide * back, mask)
        both = jnp.sum(held * entered, axis=0, keepdims=True)
        crossing = fold(jnp.broadcast_to(both, (8, width)), mask)[0:1, :] * entry[CHUNK - 1 : CHUNK, :]
        doc_col = col_ref[:, 3 * groups : 3 * groups + 1]
        doc_row = row_ref[2 * groups : 2 * groups + 1, :]
        row, col = rows_cols()
        same = doc_col == doc_row
        later = (same & (row <= col)).astype(f32)
        earlier = (same & (row > col)).astype(f32)
        decayed = (
            dsl_ref[:, groups:]
            + jnp.dot(later, out_carry, precision=high, preferred_element_type=f32)
            + jnp.dot(earlier, step * size_carry, precision=high, preferred_element_type=f32)
            + crossing
        )
        decay_grad = decayed * inside
        size_grad = dsl_ref[:, :groups] + size_carry
        rate = rate_ref[1:2, :]
        step_grad = (size_grad - rate * decay_grad) * col_ref[:, 3 * groups + 7 :]
        step_grad_ref[...] = step_grad.astype(bf16)
        sum_ref[0:1, step_at : step_at + groups] += jnp.sum(step_grad, axis=0, keepdims=True)
        sum_ref[0:1, step_at + groups : step_at + 2 * groups] -= jnp.sum(
            decay_grad * step * rate, axis=0, keepdims=True
        )
        adjoint[...] = entry_wide[CHUNK - 1 : CHUNK, :] * held + mm_two(stt_ref[STATE:, :], y_entry)

        grad = conv_back_step(
            act_grad, pre_ref[...], value_ref[...].astype(f32), taps_ref, match, next_ref, sum_inner_ref
        )
        grad_ref[...] = grad.astype(bf16)
        grad_state = conv_back_step(
            jnp.concatenate([in_grad, out_grad], axis=1),
            pre_state_ref[...],
            value_state_ref[...].astype(f32),
            taps_state_ref,
            match,
            next_state_ref,
            sum_state_ref,
        )
        grad_state_ref[...] = grad_state.astype(bf16)
        grad_state_t_ref[...] = jnp.transpose(grad_state)

        @pl.when(step_index == 0)
        def _():
            tail_ref[:, :width] = grad[CHUNK - 16 :]
            tail_ref[:, width:] = grad_state[CHUNK - 16 :]


def norm_kernel(count, cols, planes_each, place_ref, gain_ref, wt_ref, ws_ref, ws_t_ref, *refs):
    pieces = refs[: PLANE * count]
    before_refs = refs[PLANE * count : (PLANE + 1) * count]
    out_ref, share_ref, value_ref, raw_ref, raw_row_ref, halo_ref, halo_value_ref = refs[
        (PLANE + 1) * count :
    ]
    place = place_ref[0]
    head = place_ref[1]
    share = pieces[0].shape[1]

    @pl.when(pl.program_id(0) == 0)
    def _():
        wide = [ref[...].astype(f32) for ref in before_refs]
        total = 0.0
        for q in range(count):
            total = total + jnp.sum(wide[q] * wide[q], axis=1, keepdims=True)
        inverse = lax.rsqrt(total / D + eps)
        for q in range(count):
            lanes = pl.ds(pl.multiple_of((head ^ q) * share, 128), share)
            halo_ref[:, lanes] = (wide[q] * inverse * gain_ref[:, lanes]).astype(bf16)
        halo_value_ref[...] = mm(halo_ref[...], wt_ref[...]).astype(bf16)

    for r in range(PLANE):

        @pl.when(pl.program_id(0) == r)
        def _():
            wide = [pieces[r * count + q][...].astype(f32) for q in range(count)]
            total = 0.0
            for q in range(count):
                total = total + jnp.sum(wide[q] * wide[q], axis=1, keepdims=True)
            inverse = lax.rsqrt(total / D + eps)
            for q in range(count):
                lanes = pl.ds(pl.multiple_of((head ^ q) * share, 128), share)
                out_ref[:, lanes] = (wide[q] * inverse * gain_ref[:, lanes]).astype(bf16)
            for t in range(PLANE):

                @pl.when(place == t)
                def _():
                    for z in range(planes_each):
                        share_ref[0, :, z * cols : (z + 1) * cols] = pieces[r * count][
                            :, (z * PLANE + t) * cols : (z * PLANE + t + 1) * cols
                        ]

    normed = out_ref[...]
    value_ref[...] = mm(normed, wt_ref[...]).astype(bf16)
    raw_ref[...] = mm(normed, ws_ref[...])
    raw_row_ref[...] = mm_t(ws_t_ref[...], normed)


def shift_in(value, last, reach, row):
    rolled = pltpu.roll(value, reach, 0)
    top = jnp.where(row < reach, pltpu.roll(last, reach, 0), rolled[:8])
    return jnp.concatenate([top, rolled[8:]], axis=0)


def conv_step(value, last_ref, taps_ref, match):
    row = lax.broadcasted_iota(jnp.int32, (8, value.shape[1]), 0)
    last = last_ref[...]
    pre = taps_ref[4:5, :] + taps_ref[3:4, :] * value
    for k in range(KERNEL - 1):
        moved = shift_in(value, last, KERNEL - 1 - k, row)
        pre = pre + taps_ref[k : k + 1, :] * moved * match[k]
    last_ref[...] = value[value.shape[0] - 8 :]
    return pre


def softplus(a):
    return jnp.maximum(a, 0.0) + jnp.log1p(jnp.exp(-jnp.abs(a)))


def vectors_kernel(
    groups, turn,
    base_ref,
    value_ref,
    halo_ref,
    raw_ref,
    raw_row_ref,
    taps_ref,
    starts_ref,
    starts_t_ref,
    head_row_ref,
    head_col_ref,
    pre_ref,
    act_ref,
    act_t_ref,
    col_ref,
    row_ref,
    decay_ref,
    last_ref,
    total_ref,
):
    chunk = turn

    @pl.when(chunk == 0)
    def _():
        last_ref[...] = halo_ref[...].astype(f32)[8:]
        total_ref[...] = jnp.zeros_like(total_ref)

    base = base_ref[0]
    first = base + chunk * CHUNK

    def doc_of(position):
        return jnp.sum((position >= starts_ref[...]).astype(f32), axis=1, keepdims=True)

    place = first + lax.broadcasted_iota(jnp.int32, (CHUNK, 1), 0)
    corner = jnp.zeros((1, 1), jnp.int32)
    doc = doc_of(place)
    match = [(doc_of(place - (KERNEL - 1) + k) == doc).astype(f32) for k in range(KERNEL - 1)]
    from_start = (doc == doc_of(corner + (first - 1))).astype(f32)
    to_end = (doc == doc_of(corner + (first + CHUNK - 1))).astype(f32)
    whole_start = (doc == doc_of(corner + (base - 1))).astype(f32)
    place_row = first + lax.broadcasted_iota(jnp.int32, (1, CHUNK), 1)
    row_ref[2 * groups : 2 * groups + 1, :] = jnp.sum(
        (place_row >= starts_t_ref[...]).astype(f32), axis=0, keepdims=True
    )

    pre = conv_step(value_ref[...].astype(f32), last_ref, taps_ref, match)
    pre_ref[...] = pre
    act = pre * jax.nn.sigmoid(pre)
    act_ref[...] = act.astype(bf16)
    act_t_ref[...] = jnp.transpose(act).astype(bf16)

    shifted_raw = raw_ref[...] + head_row_ref[0:1, :]
    step = softplus(shifted_raw)
    col_ref[:, 3 * groups + 7 :] = jax.nn.sigmoid(shifted_raw)
    row, col = rows_cols()
    lower = (row >= col).astype(f32)
    cum = jnp.dot(
        lower, -step * head_row_ref[1:2, :], precision=high, preferred_element_type=f32
    )
    whole = cum + total_ref[0:1, :]
    total_ref[...] = jnp.broadcast_to(whole[CHUNK - 1 : CHUNK, :], total_ref.shape)
    entry_whole = jnp.exp(whole) * whole_start
    col_ref[:, :groups] = cum
    col_ref[:, groups : 2 * groups] = step
    col_ref[:, 2 * groups : 3 * groups] = entry_whole
    for n, column in enumerate([doc, from_start, to_end, match[2]] + match):
        col_ref[:, 3 * groups + n : 3 * groups + n + 1] = column
    step_row = softplus(raw_row_ref[:groups, :] + head_col_ref[:, 0:1])
    row_ref[:groups, :] = lax.dot_general(
        -step_row * head_col_ref[:, 1:2],
        lower,
        (((1,), (1,)), ((), ())),
        precision=high,
        preferred_element_type=f32,
    )
    row_ref[groups : 2 * groups, :] = step_row
    decay_ref[...] = widen(
        jnp.broadcast_to(entry_whole[CHUNK - 1 : CHUNK, :], (8, groups)),
        head_mask(groups, decay_ref.shape[1]),
    )


def convolve_kernel(
    groups, turn, value_ref, halo_ref, stt_ref, col_ref, taps_ref, pre_ref, x_ref, state_ref, last_ref
):
    @pl.when(turn == 0)
    def _():
        last_ref[...] = halo_ref[...].astype(f32)[8:]
        state_ref[...] = jnp.zeros_like(state_ref)

    mask = head_mask(groups, x_ref.shape[1])
    match = [col_ref[:, 3 * groups + 4 + k : 3 * groups + 5 + k] for k in range(KERNEL - 1)]
    pre = conv_step(value_ref[...].astype(f32), last_ref, taps_ref, match)
    pre_ref[...] = pre
    x_low = (pre * jax.nn.sigmoid(pre)).astype(bf16)
    x_ref[...] = x_low
    cum = col_ref[:, :groups]
    cum_last = cum[CHUNK - 1 : CHUNK, :]
    from_start = col_ref[CHUNK - 1 : CHUNK, 3 * groups + 1 : 3 * groups + 2]
    to_end = col_ref[:, 3 * groups + 2 : 3 * groups + 3]
    ending = widen(jnp.exp(cum_last - cum) * to_end * col_ref[:, groups : 2 * groups], mask)
    kept = widen(jnp.broadcast_to(jnp.exp(cum_last) * from_start, (8, groups)), mask)
    state_ref[...] = kept[0:1, :] * state_ref[...] + mm_two(
        stt_ref[:STATE, :], x_low.astype(f32) * ending
    )


def weight_kernel(groups, *refs):
    refs = refs[1:]
    out_ref = refs[2 * PLANE]
    for r in range(PLANE):

        @pl.when(pl.program_id(0) == r)
        def _():
            for g in range(groups):
                lanes = slice(g * P_SIZE, (g + 1) * P_SIZE)
                both = [refs[r][:, lanes].astype(f32), refs[PLANE + r][:, lanes].astype(f32)]
                out_ref[:, g, :] = jnp.concatenate(both, axis=1)


def unpack_kernel(groups, state_rows, place_ref, *refs):
    small_refs = refs[:2]
    (
        state_ref,
        taps_ref,
        bias_ref,
        gated_ref,
        state_taps_ref,
        state_bias_ref,
        shift_ref,
        rate_ref,
        skip_ref,
        step_ref,
        total_ref,
    ) = refs[2:]
    head = place_ref[1]
    core = place_ref[0] & 1
    width = groups * P_SIZE
    sums = 8 + groups
    heads = small_refs[0].shape[1]
    state_at = 2 * width
    step_at = state_at + 2 * STATE
    total_ref[...] = jnp.zeros_like(total_ref)
    for side in range(2):
        for near in range(2):

            @pl.when(core == side ^ near)
            def _():
                for y in range(2):
                    for h in range(heads):
                        rows = small_refs[near]
                        state = rows[y, h, :state_rows, :].astype(f32)
                        at = (side * 2 + y) * (STATE // 2) + h * state_rows
                        state_ref[:, at : at + state_rows] = jnp.transpose(state)
                        value = (
                            rows[y, h, state_rows : state_rows + sums, :].astype(f32)
                            + rows[y, h, state_rows + sums :, :].astype(f32)
                        )
                        total_ref[...] += value[:8]
                        inner = y * 2 + side
                        for g in range(groups):
                            number = (inner * groups + g) * heads + h
                            here = slice(number * P_SIZE, (number + 1) * P_SIZE)
                            lanes = slice(g * P_SIZE, (g + 1) * P_SIZE)
                            taps_ref[:, here] = value[:KERNEL, lanes]
                            bias_ref[:, here] = value[KERNEL : KERNEL + 1, lanes]
                            lanes = slice(width + g * P_SIZE, width + (g + 1) * P_SIZE)
                            gated_ref[:, here] = value[0:1, lanes]
                            skip_ref[:, number : number + 1] = jnp.sum(
                                value[1:2, lanes], axis=1, keepdims=True
                            )
                            lane = step_at + g
                            shift_ref[:, number : number + 1] = value[0:1, lane : lane + 1]
                            lane = step_at + groups + g
                            rate_ref[:, number : number + 1] = value[0:1, lane : lane + 1]

                        @pl.when(head == h)
                        def _():
                            step_ref[inner * groups : (inner + 1) * groups, :] = value[8:]

    state_taps_ref[...] = total_ref[:KERNEL, state_at:step_at]
    state_bias_ref[...] = total_ref[KERNEL : KERNEL + 1, state_at:step_at]


def normed_back_kernel(
    place_ref,
    z_ref,
    inner_ref,
    step_ref,
    state_ref,
    normed_ref,
    wg_ref,
    wi_ref,
    ws_ref,
    wt_ref,
    own_ref,
    across_ref,
    core_ref,
    gain_ref,
    total_ref,
):
    total = (
        mm_t(z_ref[...], wg_ref[...])
        + mm_t(inner_ref[...], wi_ref[...])
        + mm_t(step_ref[...], ws_ref[...])
        + mm_t(state_ref[...], wt_ref[...])
    )
    total_ref[...] = total
    gain = jnp.sum(total * normed_ref[...].astype(f32), axis=0, keepdims=True)
    gain_ref[...] = jnp.broadcast_to(gain, gain_ref.shape)
    rows = own_ref.shape[0]
    place = place_ref[0]

    def block(r):
        return total_ref[pl.ds(pl.multiple_of((place ^ r) * rows, rows), rows), :]

    own_ref[...] = block(0)
    core_ref[0] = block(1).astype(bf16)
    across_ref[...] = block(2)
    core_ref[1] = block(3).astype(bf16)


def level_of(place, half):
    return jnp.where(place == 0, 3 - half, jnp.where(place == 1, 1, 0))


def split_kernel(count, cols, place_ref, whole_ref, *out_refs):
    place = place_ref[0]
    for r in range(PLANE):
        for t in range(PLANE):

            @pl.when(place == t ^ r)
            def _():
                for z in range(count):
                    out_refs[r][0, :, z * cols : (z + 1) * cols] = whole_ref[
                        0, :, (z * PLANE + t) * cols : (z * PLANE + t + 1) * cols
                    ]


def join_kernel(count, cols, place_ref, *refs):
    place = place_ref[0]
    out_ref = refs[PLANE]
    for r in range(PLANE):
        for t in range(PLANE):

            @pl.when(place == t ^ r)
            def _():
                for z in range(count):
                    out_ref[0, :, (z * PLANE + t) * cols : (z * PLANE + t + 1) * cols] = refs[r][
                        0, :, z * cols : (z + 1) * cols
                    ]


def pick_part(near_refs, first_refs, second_refs, cot_ref):
    step = pl.program_id(0)

    @pl.when(step < 2)
    def _():
        for q, near in enumerate(near_refs):
            cot_ref[q] = near[0]

    @pl.when(step == 2)
    def _():
        for q, first in enumerate(first_refs):
            cot_ref[q] = first[...]

    @pl.when(step == 3)
    def _():
        for q, second in enumerate(second_refs):
            cot_ref[q] = second[...]


def weight_rows_of(weight_ref, count, head, owner, span):
    each = weight_ref.shape[0] // count
    return jnp.concatenate(
        [weight_ref[(head ^ q) * each + z, owner, span, :] for q in range(count) for z in range(each)],
        axis=1,
    )


def scale_kernel(sum_ref, row_ref, col_ref):
    level = lax.broadcasted_iota(jnp.int32, sum_ref.shape, 0)
    width = jnp.zeros(sum_ref.shape, f32) + 1.0
    for m in range(4):
        width = jnp.where(level == m, float(INNER >> m), width)
    scale = lax.rsqrt(sum_ref[...] / width + eps)
    row_ref[...] = scale
    col_ref[...] = jnp.transpose(scale)


def out_back_kernel(count, place_ref, scale_ref, weight_ref, *refs):
    part_refs = refs[3 * count : 3 * count + PLANE]
    sum_ref, low_ref, cot_ref = refs[3 * count + PLANE :]
    pick_part(refs[:count], refs[count : 2 * count], refs[2 * count : 3 * count], cot_ref)
    place = place_ref[0]
    half = cot_ref.shape[3]
    for q in range(count):
        lanes = slice(q * half, (q + 1) * half)
        total = None
        for m in range(4):
            grad = (scale_ref[:, m : m + 1] * cot_ref[q, m].astype(f32)).astype(bf16)
            total = grad.astype(f32) if m == 0 else total + grad.astype(f32)
            upper, lower = split_two(total)
            sum_ref[m, :, lanes] = upper
            low_ref[m, :, lanes] = lower
    rows = weight_ref.shape[2] // 2
    for r in range(PLANE):
        owner = place ^ r
        for side in range(2):
            level = level_of(owner, side)
            span = slice(side * rows, (side + 1) * rows)
            weight = weight_rows_of(weight_ref, count, place_ref[1], owner, span)
            part = mm_t(sum_ref[level], weight)
            out_ref = part_refs[r]

            @pl.when(owner < 2)
            def _():
                out_ref[:, span] = (part + mm_t(low_ref[level], weight)).astype(out_ref.dtype)

            @pl.when(owner >= 2)
            def _():
                out_ref[:, span] = part.astype(out_ref.dtype)


def product_kernel(count, place_ref, weight_ref, *refs):
    u_refs = refs[:PLANE]
    cot_refs = refs[PLANE : PLANE + 3 * count]
    refs = refs[PLANE + 3 * count :]
    dot_ref, own_ref = refs[:2]
    send_refs = refs[2 : count + 1]
    block_ref, cot_ref = refs[count + 1 :]
    pick_part(cot_refs[:count], cot_refs[count : 2 * count], cot_refs[2 * count :], cot_ref)
    place = place_ref[0]
    half = cot_ref.shape[3]
    rows = weight_ref.shape[2] // 2
    block_ref[...] = jnp.zeros_like(block_ref)
    for r in range(PLANE):
        owner = place ^ r
        for side in range(2):
            span = slice(side * rows, (side + 1) * rows)
            weight = weight_rows_of(weight_ref, count, place_ref[1], owner, span)
            block_ref[level_of(owner, side)] += mm(u_refs[r][:, span], weight)
    running = None
    ones = jnp.ones((8, half), bf16)
    dot_ref[4:8, :] = jnp.zeros((4, dot_ref.shape[1]), f32)
    for m in (3, 2, 1, 0):
        running = block_ref[m] if running is None else running + block_ref[m]
        dots = 0.0
        for q in range(count):
            part = running[:, q * half : (q + 1) * half]
            dots = dots + cot_ref[q, m].astype(f32) * part
            if q == 0:
                own_ref[0, m] = part
            else:
                send_refs[q - 1][0, m] = part.astype(bf16)
        upper, lower = split_two(dots)
        dot_ref[m : m + 1, :] = (mm_t(ones, upper) + mm_t(ones, lower))[0:1, :]


def mix_kernel(count, scale_ref, tok_ref, own_ref, *refs):
    got_refs = refs[: count - 1]
    out_refs = refs[count - 1 :]
    for r in range(PLANE):

        @pl.when(pl.program_id(0) == r)
        def _():
            for m in range(4):
                total = own_ref[0, m]
                for got in got_refs:
                    total = total + got[0, m].astype(f32)
                out_refs[r][m] = (
                    tok_ref[0].astype(f32) + scale_ref[:, m : m + 1] * total
                ).astype(bf16)


def out_weight_kernel(count, planes_each, cols, place_ref, sum_ref, *refs):
    u_refs = refs[:PLANE]
    out_ref = refs[PLANE]
    place = place_ref[0]
    head = place_ref[1]
    rows = u_refs[0].shape[1] // 2
    for r in range(PLANE):

        @pl.when(pl.program_id(0) == r)
        def _():
            owner = place ^ r
            for side in range(2):
                span = slice(side * rows, (side + 1) * rows)
                grad = t_mm(u_refs[r][:, span], sum_ref[level_of(owner, side)])
                for q in range(count):
                    for z in range(planes_each):
                        lanes = slice((q * planes_each + z) * cols, (q * planes_each + z + 1) * cols)
                        out_ref[(head ^ q) * planes_each + z, span, :] = grad[:, lanes].astype(bf16)


def per_chunk(width):
    return "rows", pl.BlockSpec((SUB * CHUNK, width), lambda c, *rest: (c, 0))


def across(height):
    return "cols", pl.BlockSpec((height, SUB * CHUNK), lambda c, *rest: (0, c))


def fixed(*shape):
    return "fixed", pl.BlockSpec(shape, lambda c, *rest: (0,) * len(shape))


def spread(kernel, specs, reverse=False, ahead=0):
    def view(kind, ref, sub):
        part = pl.ds(sub * CHUNK, CHUNK)
        if kind == "rows":
            return ref.at[part, :]
        return ref.at[:, part] if kind == "cols" else ref

    def run(*refs):
        first, refs = refs[:ahead], refs[ahead:]
        for n in range(SUB):
            sub = SUB - 1 - n if reverse else n
            views = [view(kind, ref, sub) for (kind, _), ref in zip(specs, refs)]
            kernel(pl.program_id(0) * SUB + n, *first, *views, *refs[len(specs) :])

    return run


def shaped(shape, kind=f32):
    return jax.ShapeDtypeStruct(shape, kind)


def contract(left_side, right_side, left_dim, right_dim):
    return lax.dot_general(
        left_side,
        right_side,
        (((left_dim,), (right_dim,)), ((), ())),
        preferred_element_type=f32,
    )


def own_heads(values, heads):
    shape = values.shape[:-1]
    shaped_values = values.reshape(shape + (PLANE, -1, lax.axis_size("h"), heads))
    mine = take(shaped_values, lax.axis_index("i"), len(shape))
    mine = take(mine, lax.axis_index("h"), len(shape) + 1)
    return mine.reshape(shape + (-1,))


def shards(
    tokens,
    cotangent,
    doc_lengths,
    input_gain,
    input_weight,
    step_weight,
    state_weight,
    conv_inner,
    conv_inner_bias,
    conv_state,
    conv_state_bias,
    step_bias,
    decay_log,
    skip_gain,
    gated_gain,
    output_weight,
):
    planes = lax.axis_size("o")
    head_count = lax.axis_size("h")
    plane = lax.axis_index("o")
    inner = lax.axis_index("i")
    head = lax.axis_index("h")
    here = jnp.stack([inner, head]).astype(jnp.int32)
    tok_rows, share = tokens.shape
    span = tok_rows * PLANE
    steps = span // CHUNK
    weight_rows, groups_all = input_weight.shape[:2]
    groups = groups_all // PLANE
    width = groups * P_SIZE
    wide_rows = groups_all * P_SIZE
    cols = output_weight.shape[2]
    own_planes = planes // head_count
    half = own_planes * cols
    pad = KERNEL - 1
    halo = 16
    fence = lax.optimization_barrier

    def token_block(*rest):
        return pl.BlockSpec((tok_rows,) + rest, lambda r, place: (r ^ place[0],) + (0,) * len(rest))

    def part_block(*rest):
        return pl.BlockSpec((1,) + rest, lambda r, place: (r,) + (0,) * len(rest))

    def whole_block(*shape):
        return pl.BlockSpec(shape, lambda r, place: (0,) * len(shape))

    def placed_call(kernel, in_specs, out_specs, out_shape, scratch, name):
        return pl.pallas_call(
            kernel,
            grid_spec=pltpu.PrefetchScalarGridSpec(
                num_scalar_prefetch=1,
                grid=(PLANE,),
                in_specs=in_specs,
                out_specs=out_specs,
                scratch_shapes=scratch,
            ),
            out_shape=out_shape,
            compiler_params=PARAMS,
            name=name,
        )

    def placed_call_once(kernel, out_shape, scratch, name):
        return pl.pallas_call(
            kernel,
            grid_spec=pltpu.PrefetchScalarGridSpec(
                num_scalar_prefetch=1,
                grid=(1,),
                in_specs=[pl.BlockSpec(memory_space=pltpu.VMEM)] * 2,
                out_specs=[pl.BlockSpec(memory_space=pltpu.VMEM)] * len(out_shape),
                scratch_shapes=scratch,
            ),
            out_shape=out_shape,
            compiler_params=PARAMS,
            name=name,
        )

    def unplaced(kernel):
        return lambda place_ref, *refs: kernel(*refs)

    def chunk_call(kernel, in_specs, out_specs, out_shape, scratch, name, ahead=0):
        return pl.pallas_call(
            spread(kernel, in_specs + out_specs, ahead=ahead),
            grid_spec=pltpu.PrefetchScalarGridSpec(
                num_scalar_prefetch=ahead,
                grid=(steps // SUB,),
                in_specs=[spec for _, spec in in_specs],
                out_specs=[spec for _, spec in out_specs],
                scratch_shapes=scratch,
            ),
            out_shape=out_shape,
            compiler_params=PARAMS,
            name=name,
        )

    pieces = input_weight.reshape(weight_rows, PLANE, groups, 2, P_SIZE)

    def head_pieces(side):
        return jnp.transpose(pieces[:, :, :, side, :], (1, 0, 2, 3)).reshape(
            PLANE, weight_rows, width
        )

    inner_pieces = exchange_inner(head_pieces(1))
    near = [swap(tokens, "h", q) if q else tokens for q in range(head_count)]
    far = swap(tokens, "i", 2)
    step_planes = stack_planes(step_weight.reshape(weight_rows, groups_all))
    before = shifted(tokens[tok_rows - halo :], "o", 1)
    before = jnp.where(inner == PLANE - 1, before, jnp.zeros_like(before))
    near, far, inner_pieces, step_planes, before = fence(
        (near, far, inner_pieces, step_planes, before)
    )
    weight_inner = lax.all_gather(
        inner_pieces.reshape(PLANE * weight_rows, width), "o", axis=0, tiled=True
    )
    sibling = [swap(b, "i", 1) for b in near]
    before = before + swap(before, "i", 2)
    before = before + swap(before, "i", 1)
    before = [swap(before, "h", q) if q else before for q in range(head_count)]
    weight_step = jnp.transpose(stack_inner(step_planes), (1, 0, 2, 3)).reshape(D, groups_all)
    weight_step = lax.dynamic_slice_in_dim(weight_step, inner * groups, groups, 1)
    weight_step_t = jnp.pad(jnp.transpose(weight_step), ((0, 16 - groups), (0, 0)))
    far = [swap(far, "h", q) if q else far for q in range(head_count)]
    gate_pieces, before, far, sibling, weight_step, weight_step_t = fence(
        (
            exchange_inner(fence((head_pieces(0), near))[0]),
            before,
            far,
            sibling,
            weight_step,
            weight_step_t,
        )
    )
    weight_gate = lax.all_gather(
        gate_pieces.reshape(PLANE * weight_rows, width), "o", axis=0, tiled=True
    )
    blocks = [near, sibling, far, [swap(b, "i", 1) for b in far]]
    normed, tok_share, state_value, step_raw, step_row, normed_halo, state_halo = placed_call(
        partial(norm_kernel, head_count, cols, own_planes),
        [
            whole_block(1, D),
            whole_block(D, 2 * STATE),
            whole_block(D, groups),
            whole_block(16, D),
        ]
        + [whole_block(tok_rows, share)] * (PLANE * head_count)
        + [whole_block(halo, share)] * head_count,
        [
            token_block(D),
            part_block(tok_rows, half),
            token_block(2 * STATE),
            token_block(groups),
            pl.BlockSpec((16, tok_rows), lambda r, place: (0, r ^ place[0])),
            whole_block(halo, D),
            whole_block(halo, 2 * STATE),
        ],
        [
            shaped((span, D), bf16),
            shaped((PLANE, tok_rows, half), bf16),
            shaped((span, 2 * STATE), bf16),
            shaped((span, groups)),
            shaped((16, span)),
            shaped((halo, D), bf16),
            shaped((halo, 2 * STATE), bf16),
        ],
        [],
        "norm",
    )(
        here,
        input_gain[None],
        state_weight,
        weight_step,
        weight_step_t,
        *[b for row in blocks for b in row],
        *before,
    )

    weight_out = lax.all_gather(output_weight.reshape(wide_rows, cols), "o")
    weight_out = weight_out.reshape(planes, PLANE, width, cols)

    cotangent_later, normed = fence((cotangent, normed))
    largest = jnp.max(jnp.abs(cotangent_later)).astype(f32)
    cot_parts = pl.pallas_call(
        partial(split_kernel, own_planes, cols),
        grid_spec=pltpu.PrefetchScalarGridSpec(
            num_scalar_prefetch=1,
            grid=(4,),
            in_specs=[pl.BlockSpec((1, tok_rows, share), lambda m, place: (m, 0, 0))],
            out_specs=[pl.BlockSpec((1, tok_rows, half), lambda m, place: (m, 0, 0))] * PLANE,
        ),
        out_shape=[shaped((4, tok_rows, half), bf16)] * PLANE,
        compiler_params=PARAMS,
        name="split",
    )(here, cotangent_later)
    cot_near = jnp.stack([cot_parts[0], swap(cot_parts[1], "i", 1)])
    cot_sent = [swap(cot_parts[2], "i", 2), swap(cot_parts[3], "i", 3)]
    cot_near = [swap(cot_near, "h", q) if q else cot_near for q in range(head_count)]

    starts = (jnp.cumsum(doc_lengths) - doc_lengths).astype(jnp.int32)
    base = (plane * span).astype(jnp.int32).reshape(1)

    def taps_of(kernel, bias):
        return jnp.concatenate([kernel, bias[None], jnp.zeros((3, bias.shape[0]), f32)], axis=0)

    taps_inner = taps_of(own_heads(conv_inner, P_SIZE), own_heads(conv_inner_bias, P_SIZE))
    taps_state = taps_of(conv_state, conv_state_bias)
    gain_wide = own_heads(gated_gain, P_SIZE)
    step_shift = own_heads(step_bias, 1)
    rate_log = own_heads(decay_log, 1)
    skip_wide = jnp.repeat(own_heads(skip_gain, 1), P_SIZE)
    wide = jnp.concatenate([skip_wide[None], gain_wide[None], jnp.zeros((6, width), f32)], axis=0)
    group_number = inner * groups + jnp.arange(groups)
    level_limit = jnp.array([groups_all >> m for m in range(4)] + [0] * 4)
    level_mask = jnp.repeat(
        (group_number[None, :] < level_limit[:, None]).astype(bf16), P_SIZE, axis=1
    )

    rate = jnp.exp(rate_log)
    head_row = jnp.concatenate([step_shift[None], rate[None], jnp.zeros((6, groups), f32)], axis=0)
    head_col = jnp.stack([step_shift, rate], axis=1)
    col_width = 4 * groups + 7
    row_height = 2 * groups + 1

    pre_state, state_act, state_act_t, col_pack, row_pack, decay_wide = chunk_call(
        partial(vectors_kernel, groups),
        [
            per_chunk(2 * STATE),
            fixed(halo, 2 * STATE),
            per_chunk(groups),
            across(16),
            fixed(8, 2 * STATE),
            fixed(1, starts.shape[0]),
            fixed(starts.shape[0], 1),
            fixed(8, groups),
            fixed(groups, 2),
        ],
        [
            per_chunk(2 * STATE),
            per_chunk(2 * STATE),
            across(2 * STATE),
            per_chunk(col_width),
            across(row_height),
            fixed(8, width),
        ],
        [
            shaped((span, 2 * STATE)),
            shaped((span, 2 * STATE), bf16),
            shaped((2 * STATE, span), bf16),
            shaped((span, col_width)),
            shaped((row_height, span)),
            shaped((8, width)),
        ],
        [pltpu.VMEM((8, 2 * STATE), f32), pltpu.VMEM((8, groups), f32)],
        "vectors",
        ahead=1,
    )(
        base,
        state_value,
        state_halo,
        step_raw,
        step_row,
        taps_state,
        starts[None, :],
        starts[:, None],
        head_row,
        head_col,
    )
    decay_whole = decay_wide[0:1]

    wide_out = shaped((span, width))
    value = jnp.dot(normed, weight_inner, preferred_element_type=f32).astype(bf16)
    inner_halo = jnp.dot(normed_halo, weight_inner, preferred_element_type=f32).astype(bf16)
    pre_inner, x, own_state = chunk_call(
        partial(convolve_kernel, groups),
        [
            per_chunk(width),
            fixed(halo, width),
            across(2 * STATE),
            per_chunk(col_width),
            fixed(8, width),
        ],
        [per_chunk(width), per_chunk(width), fixed(STATE, width)],
        [wide_out, shaped((span, width), bf16), shaped((STATE, width))],
        [pltpu.VMEM((8, width), f32)],
        "convolve",
    )(value, inner_halo, state_act_t, col_pack, taps_inner)
    x, cot_near, cot_sent = fence((x, cot_near, cot_sent))
    cot_first = [swap(cot_sent[0], "h", q) if q else cot_sent[0] for q in range(head_count)]
    cot_second = [swap(cot_sent[1], "h", q) if q else cot_sent[1] for q in range(head_count)]
    incoming = chain(own_state, decay_whole, 1)
    (y_local,) = chunk_call(
        partial(within_kernel, groups),
        [per_chunk(width), per_chunk(2 * STATE), per_chunk(col_width), across(row_height)],
        [per_chunk(width)],
        [wide_out],
        [],
        "within",
    )(x, state_act, col_pack, row_pack)
    y_local, cot_first = fence((y_local, cot_first))
    gate_z = jnp.dot(normed, weight_gate, preferred_element_type=f32).astype(bf16)
    v, scaled_u, squares, entering = chunk_call(
        partial(carry_kernel, groups),
        [
            per_chunk(width),
            per_chunk(2 * STATE),
            across(2 * STATE),
            per_chunk(col_width),
            per_chunk(width),
            per_chunk(width),
            fixed(STATE, width),
            fixed(8, width),
            fixed(8, width),
        ],
        [per_chunk(width), per_chunk(width), across(8), per_chunk(width)],
        [
            wide_out,
            shaped((span, width), bf16),
            shaped((8, span)),
            shaped((steps * STATE, width)),
        ],
        [pltpu.VMEM((STATE, width), f32)],
        "carry",
    )(x, state_act, state_act_t, col_pack, y_local, gate_z, incoming, wide, level_mask)

    scaled_u, cot_second = fence((scaled_u, cot_second))
    cots = list(cot_near) + list(cot_first) + list(cot_second)

    squares = jnp.concatenate(
        [squares[:4], jnp.full((1, span), largest, f32), jnp.zeros((3, span), f32)], axis=0
    )
    squares = add_inner(add_all(add_inner(squares, 2), ("h",)), 1)
    scaled_u, squares = fence((scaled_u, squares))
    u_far = swap(scaled_u, "i", 2)
    u_parts = [scaled_u, swap(scaled_u, "i", 1), u_far, swap(u_far, "i", 1)]
    scales_row, scales = pl.pallas_call(
        scale_kernel,
        out_shape=[shaped((8, span)), shaped((span, 8))],
        compiler_params=pltpu.CompilerParams(vmem_limit_bytes=8 * 1024 * 1024),
        name="scales",
    )(squares)
    u_bound = squares[4, 0] * jnp.sum(jnp.max(scales_row[:4], axis=1))
    u_bound = u_bound * (0.1875 * 2.0 * head_count * half)
    scales, u_parts = fence((scales, u_parts))
    cot_block = part_block(4, tok_rows, half)
    weight_block = whole_block(planes, PLANE, width, cols)
    cot_near_block = pl.BlockSpec(
        (1, 4, tok_rows, half), lambda r, place: (jnp.minimum(r, 1), 0, 0, 0)
    )
    cot_blocks = [cot_near_block] * head_count
    cot_blocks += [whole_block(4, tok_rows, half)] * (2 * head_count)
    cot_scratch = pltpu.VMEM((head_count, 4, tok_rows, half), bf16)
    cot_shape = shaped((PLANE, 4, tok_rows, half), bf16)
    *parts, sums = placed_call(
        partial(out_back_kernel, head_count),
        [token_block(8), weight_block] + cot_blocks,
        [token_block(width)] * PLANE
        + [
            pl.BlockSpec((4, tok_rows, head_count * half), lambda r, place: (0, r ^ place[0], 0)),
        ],
        [wide_out] * PLANE + [shaped((4, span, head_count * half), bf16)],
        [pltpu.VMEM((4, tok_rows, head_count * half), bf16), cot_scratch],
        "out_back",
    )(here, scales, weight_out, *cots)
    u_scale = jnp.exp2(jnp.ceil(jnp.log2(jnp.clip(u_bound, 1e-30, 1e30))))
    out_grad = placed_call(
        partial(out_weight_kernel, head_count, own_planes, cols),
        [whole_block(4, span, head_count * half)] + [whole_block(span, width)] * PLANE,
        pl.BlockSpec((planes, width, cols), lambda r, place: (0, r ^ place[0], 0)),
        shaped((planes, wide_rows, cols), bf16),
        [],
        "out_weight_back",
    )(here, sums, *u_parts)

    parts_far = swap(parts[3], "i", 1)
    parts_far, out_grad_sent = fence((parts_far, out_grad))
    out_grad = lax.psum_scatter(out_grad_sent, "o", scatter_dimension=0, tiled=False)
    sent_across = ((parts[2] + parts_far) * (HALF_TOP / u_scale)).astype(jnp.float16)
    u_parts, sent_across = fence((u_parts, sent_across))
    got_across = swap(sent_across, "i", 2).astype(f32) * (u_scale / HALF_TOP)
    u_grad = parts[0] + swap(parts[1], "i", 1) + got_across
    dots, own_product, *sent_products = placed_call(
        partial(product_kernel, head_count),
        [weight_block]
        + [token_block(width)] * PLANE
        + cot_blocks,
        [pl.BlockSpec((8, tok_rows), lambda r, place: (0, r ^ place[0]))]
        + [cot_block] * head_count,
        [shaped((8, span)), shaped(cot_shape.shape)] + [cot_shape] * (head_count - 1),
        [pltpu.VMEM((4, tok_rows, head_count * half), f32), cot_scratch],
        "products",
    )(here, weight_out, *u_parts, *cots)
    dots = add_all(add_inner(dots, 1), ("h",))
    sent_products, dots = fence((sent_products, dots))
    dots = add_inner(dots, 2)
    y_grad, z_grad, wide_sums, leaving = chunk_call(
        partial(gate_back_kernel, groups),
        [
            per_chunk(width),
            per_chunk(width),
            per_chunk(width),
            per_chunk(width),
            across(2 * STATE),
            per_chunk(col_width),
            across(8),
            across(8),
            fixed(8, width),
            fixed(8, width),
        ],
        [per_chunk(width), per_chunk(width), fixed(8, width), fixed(STATE, width)],
        [wide_out, shaped((span, width), bf16), shaped((8, width)), shaped((STATE, width))],
        [],
        "gate_back",
    )(u_grad, v, gate_z, x, state_act_t, col_pack, dots, scales_row, wide, level_mask)
    lam = chain(leaving, decay_whole, -1)

    dx_local, dbc_local, ds_local = chunk_call(
        partial(within_back_kernel, groups),
        [
            per_chunk(width),
            per_chunk(2 * STATE),
            per_chunk(col_width),
            across(row_height),
            per_chunk(width),
        ],
        [per_chunk(width), per_chunk(2 * STATE), per_chunk(2 * groups)],
        [wide_out, shaped((span, 2 * STATE)), shaped((span, 2 * groups))],
        [],
        "within_back",
    )(x, state_act, col_pack, row_pack, y_grad)
    gate_z_grad, dx_local = fence((z_grad, dx_local))
    gate_part = contract(normed, gate_z_grad, 0, 0).astype(bf16)
    got_products = [swap(sent_products[q - 1], "h", q) for q in range(1, head_count)]
    lam, got_products, gate_part, out_grad = fence((lam, got_products, gate_part, out_grad))
    mixed_parts = placed_call(
        unplaced(partial(mix_kernel, head_count)),
        [token_block(8), part_block(tok_rows, half)] + [cot_block] * head_count,
        [whole_block(4, tok_rows, half)] * PLANE,
        [shaped((4, tok_rows, half), bf16)] * PLANE,
        [],
        "mix",
    )(here, scales, tok_share, own_product, *got_products)
    gate_grad = lax.psum_scatter(gate_part, "o", scatter_dimension=0, tiled=True)
    lam, mixed_parts = fence((lam, mixed_parts))
    mixed_parts = [mixed_parts[0]] + [swap(mixed_parts[r], "i", r) for r in range(1, PLANE)]
    turns = steps // SUB

    def back_rows(shape):
        return "rows", pl.BlockSpec(
            (SUB * CHUNK, shape), lambda c: (jnp.maximum(turns - 1 - c, 0), 0)
        )

    def back_cols(shape):
        return "cols", pl.BlockSpec(
            (shape, SUB * CHUNK), lambda c: (0, jnp.maximum(turns - 1 - c, 0))
        )

    back_wide = back_rows(width)
    back_state = back_rows(2 * STATE)
    both = width + 2 * STATE
    back_in = [
        back_wide,
        back_state,
        back_cols(2 * STATE),
        back_rows(col_width),
        back_cols(row_height),
        back_wide,
        back_wide,
        back_state,
        back_rows(2 * groups),
        back_wide,
        fixed(STATE, width),
        fixed(8, width),
        back_wide,
        back_wide,
        fixed(halo, width),
        fixed(8, width),
        back_state,
        back_state,
        fixed(halo, 2 * STATE),
        fixed(8, 2 * STATE),
        fixed(8, groups),
        fixed(8, width),
    ]
    back_out = [
        back_wide,
        fixed(16, both),
        fixed(8, both),
        fixed(8, D),
        back_state,
        ("cols", pl.BlockSpec((2 * STATE, SUB * CHUNK), lambda c: (0, turns - c))),
        back_rows(groups),
    ]
    inner_grad, tails, edges, narrow, state_grad, state_sum, step_grad_low = pl.pallas_call(
        spread(
            partial(carry_back_kernel, groups, steps), back_in + back_out, reverse=True
        ),
        grid=(turns + 1,),
        in_specs=[spec for _, spec in back_in],
        out_specs=[spec for _, spec in back_out],
        out_shape=[
            shaped((span, width), bf16),
            shaped((16, both)),
            shaped((8, both)),
            shaped((8, D)),
            shaped((span, 2 * STATE), bf16),
            shaped((2 * STATE, SUB * CHUNK + span)),
            shaped((span, groups), bf16),
        ],
        scratch_shapes=[
            pltpu.VMEM((STATE, width), f32),
            pltpu.VMEM((24, width), f32),
            pltpu.VMEM((24, 2 * STATE), f32),
        ],
        compiler_params=PARAMS,
        name="carry_back",
    )(
        x,
        state_act,
        state_act_t,
        col_pack,
        row_pack,
        y_grad,
        dx_local,
        dbc_local,
        ds_local,
        entering,
        lam,
        wide,
        pre_inner,
        value,
        inner_halo,
        taps_inner,
        pre_state,
        state_value,
        state_halo,
        taps_state,
        head_row,
        wide_sums,
    )
    edges, state_sum, narrow, mixed_parts = fence((edges, state_sum, narrow, mixed_parts))
    edges = shifted(edges, "o", -1)

    def state_half(values, axis, bit):
        halves = values.reshape((2, values.shape[0] // 2, values.shape[1]))
        side = jnp.where((lax.axis_index(axis) & bit) != 0, 1, 0)
        return take(halves, side) + swap(take(halves, 1 - side), axis, bit)

    for axis, bit in (("i", 1), ("i", 2)) + tuple(("h", b) for b in reversed(bits_of("h"))):
        state_sum = state_half(state_sum, axis, bit)
    edges, state_sum, gate_grad = fence((edges, state_sum, gate_grad))
    state_rows = state_sum.shape[0]
    state_low = state_sum.astype(bf16)
    edge_at = (SUB - 1) * CHUNK
    state_part = jnp.dot(
        state_low[:, SUB * CHUNK :], normed, preferred_element_type=f32
    ) + jnp.dot(
        state_low[:, edge_at : edge_at + 8], normed_halo[8:], preferred_element_type=f32
    )
    step_part = contract(step_grad_low, normed, 0, 0)
    sum_rows = 8 + groups

    def packed_rows(sums, state):
        return jnp.concatenate([state.astype(bf16), *split_rows(sums)], axis=0)

    def unpacked_rows(rows):
        upper = rows[..., state_rows : state_rows + sum_rows, :].astype(f32)
        return upper + rows[..., state_rows + sum_rows :, :].astype(f32), rows[..., :state_rows, :]

    def plus_plane(sums, state, bit):
        got, got_state = unpacked_rows(swap(packed_rows(sums, state), "o", bit))
        return sums + got, state + got_state.astype(f32)

    small = jnp.concatenate([narrow, step_part], axis=0)
    tails = (tails + jnp.pad(edges, ((8, 0), (0, 0)))).astype(bf16)
    inner_grad = lax.dynamic_update_slice_in_dim(inner_grad, tails[:, :width], span - 16, 0)
    state_grad = lax.dynamic_update_slice_in_dim(state_grad, tails[:, width:], span - 16, 0)

    small, state_part = plus_plane(small, state_part, 1)
    part = D // 8

    def columns_of(rows):
        return pl.BlockSpec((rows, part), lambda c, place: (0, c))

    def rows_of(width):
        return pl.BlockSpec((part, width), lambda c, place: (c, 0))

    normed_own, normed_across, normed_core, gain_part = pl.pallas_call(
        normed_back_kernel,
        grid_spec=pltpu.PrefetchScalarGridSpec(
            num_scalar_prefetch=1,
            grid=(8,),
            in_specs=[
                whole_block(span, width),
                whole_block(span, width),
                whole_block(span, groups),
                whole_block(span, 2 * STATE),
                columns_of(span),
                rows_of(width),
                rows_of(width),
                rows_of(groups),
                rows_of(2 * STATE),
            ],
            out_specs=[
                columns_of(tok_rows),
                columns_of(tok_rows),
                pl.BlockSpec((2, tok_rows, part), lambda c, place: (0, 0, c)),
                columns_of(8),
            ],
            scratch_shapes=[pltpu.VMEM((span, part), f32)],
        ),
        out_shape=[
            shaped((tok_rows, D)),
            shaped((tok_rows, D)),
            shaped((2, tok_rows, D), bf16),
            shaped((8, D)),
        ],
        compiler_params=PARAMS,
        name="normed_back",
    )(
        here,
        z_grad,
        inner_grad,
        step_grad_low,
        state_grad,
        normed,
        weight_gate,
        weight_inner,
        weight_step,
        state_weight,
    )
    inner_grad, normed_core, small, state_part = fence((inner_grad, normed_core, small, state_part))

    inner_part = contract(normed, inner_grad, 0, 0).astype(bf16)
    got_core = swap(normed_core, "i", 1)
    gain_sum = add_inner(gain_part[0].reshape(8, -1), 1)
    for bit in bits_of("o")[1:]:
        small, state_part = plus_plane(small, state_part, bit)
    gate_back = scattered_inner(gate_grad.reshape(PLANE, weight_rows, width))
    inner_part, got_core, gain_sum = fence((inner_part, got_core, gain_sum))
    got_core, small, state_part, gate_back = fence((got_core, small, state_part, gate_back))
    inner_part = lax.psum_scatter(inner_part, "o", scatter_dimension=0, tiled=True)

    got_across = swap((normed_across + got_core[1].astype(f32)).astype(bf16), "i", 2)
    small = packed_rows(small, state_part)
    shape = small.shape
    for bit in bits_of("h"):
        small = stack_over(small, "h", bit, 0)
        small = small.reshape((-1,) + shape)
    gain_sum = add_all(gain_sum, ("h",))
    output_weight_grad = out_grad.astype(f32).reshape(groups_all, P_SIZE, cols)
    mixed = placed_call(
        partial(join_kernel, own_planes, cols),
        [part_block(tok_rows, half)] * PLANE,
        part_block(tok_rows, share),
        shaped((4, tok_rows, share), bf16),
        [],
        "join",
    )(here, *mixed_parts)
    got_across, gain_sum, small, mixed, output_weight_grad = fence(
        (got_across, gain_sum, small, mixed, output_weight_grad)
    )

    full_grad = scatter_heads(
        normed_own + got_core[0].astype(f32) + got_across.astype(f32), 1
    )
    small = stack_over(small, "i", 2, 0)
    gain_sum = gain_sum + swap(gain_sum, "o", 1)
    full_grad, gain_sum, small, inner_part = fence((full_grad, gain_sum, small, inner_part))

    own_wide = [near[q].astype(f32) for q in range(head_count)]
    square = sum(jnp.sum(a * a, axis=1, keepdims=True) for a in own_wide)
    inverse = lax.rsqrt(square / D + eps)
    gain_share = lax.dynamic_slice_in_dim(input_gain, head * share, share, 0)
    unit = own_wide[0] * inverse
    resid = jnp.sum(cotangent.astype(f32), axis=0)

    def weighted_of(values):
        return values * gain_share[None, :]

    def norm_row_sum(values):
        sums = jnp.sum(weighted_of(values) * unit, axis=1).reshape(-1, CHUNK)
        return add_all(sums, ("h",)).reshape(-1, 1)

    inner_back = scattered_inner(inner_part.reshape(PLANE, weight_rows, width))
    small = small.reshape((2, head_count) + shape)
    small_core = swap(small, "i", 1)
    for bit in bits_of("o")[1:]:
        gain_sum = gain_sum + swap(gain_sum, "o", bit)
    row_sum = norm_row_sum(full_grad)
    small_core, gain_sum, row_sum = fence((small_core, gain_sum, row_sum))
    gain_sum = add_inner(gain_sum, 2)
    heads_all = groups_all * head_count
    row_of = [shaped((1, INNER)), shaped((1, 2 * STATE)), shaped((1, heads_all))]
    state_weight_grad, *rows, step_rows = placed_call_once(
        partial(unpack_kernel, groups, state_rows),
        [
            shaped((D, 2 * STATE)),
            shaped((KERNEL, INNER)),
            row_of[0],
            row_of[0],
            shaped((KERNEL, 2 * STATE)),
            row_of[1],
            row_of[2],
            row_of[2],
            row_of[2],
            shaped((groups_all, D)),
        ],
        [pltpu.VMEM((8, D), f32)],
        "unpack",
    )(here, small, small_core)
    inner_back, step_rows = fence((inner_back, step_rows))
    taps_grad, bias_grad, gated_grad, state_taps_grad, *rows = rows
    state_bias_grad, shift_grad, rate_grad, skip_grad = rows
    input_gain_grad = gain_sum.reshape(D) / input_gain
    step_weight_grad = lax.dynamic_slice_in_dim(
        step_rows, (plane * PLANE + inner) * weight_rows, weight_rows, 1
    )
    step_weight_grad = jnp.transpose(step_weight_grad)[:, None, :]
    if groups % 8 == 0:
        input_weight_grad = placed_call(
            partial(weight_kernel, groups),
            [whole_block(weight_rows, width)] * (2 * PLANE),
            pl.BlockSpec((weight_rows, groups, 2 * P_SIZE), lambda r, place: (0, r ^ place[0], 0)),
            shaped((weight_rows, groups_all, 2 * P_SIZE)),
            [],
            "weight_grad",
        )(here, *gate_back, *inner_back)
    else:
        sides = []
        for back in (gate_back, inner_back):
            whole = jnp.zeros((PLANE, weight_rows, groups, P_SIZE), bf16)
            for r in range(PLANE):
                whole = put(whole, back[r].reshape(weight_rows, groups, P_SIZE), inner ^ r)
            sides.append(jnp.transpose(whole, (1, 0, 2, 3)))
        input_weight_grad = jnp.concatenate(sides, axis=3).astype(f32)
        input_weight_grad = input_weight_grad.reshape(weight_rows, groups_all, 2 * P_SIZE)

    tokens_grad = resid + inverse * (weighted_of(full_grad) - unit * (row_sum / D))
    return (
        mixed,
        tokens_grad,
        input_gain_grad,
        input_weight_grad,
        step_weight_grad,
        state_weight_grad,
        taps_grad,
        bias_grad.reshape(INNER),
        state_taps_grad,
        state_bias_grad.reshape(2 * STATE),
        shift_grad.reshape(heads_all),
        rate_grad.reshape(heads_all),
        skip_grad.reshape(heads_all),
        gated_grad.reshape(INNER),
        output_weight_grad,
    )


def solution(mesh):
    rows, heads = mesh.devices.shape
    cut = Mesh(mesh.devices.reshape(rows // PLANE, PLANE, heads), ("o", "i", "h"))
    both = ("o", "i")
    placed = (
        P(both, "h"),
        P(None, both, "h"),
        P(),
        P(),
        P(both, None, "h"),
        P(both, "h", None),
        P(),
        P(),
        P(),
        P(),
        P(),
        P(),
        P(),
        P(),
        P(),
        P(None, "h", both),
    )
    return jax.shard_map(
        shards,
        mesh=cut,
        in_specs=placed,
        out_specs=(
            P(None, both, "h"),
            P(both, "h"),
            P(),
            P(both, None, "h"),
            P(both, "h", None),
            P(),
            P(),
            P(),
            P(),
            P(),
            P(),
            P(),
            P(),
            P(),
            P(None, "h", both),
        ),
        check_vma=False,
    )
```

time: 616 us -> 470 us (0.76)
  waiting for transfers between devices: 215 us -> 126 us
  local copies, waits for them, and re-layouts: 87.1 us -> 26.6 us
  Pallas kernels: 124 us -> 156 us
  other arithmetic: 53.5 us -> 34.5 us
  starting transfers between devices: 85.9 us -> 74.8 us
    ppermute x75 -> x65, waiting for transfers between devices: 184 us -> 122 us  [swap(): lax.ppermute(block, axis, [(a, a ^ bit) for a in range(lax.axis_size(axis...]
    ppermute x14 -> x8, waiting for transfers between devices: 31 us -> 4.09 us  [shifted(): return lax.ppermute(block, axis, route)]
    pallas_call x5 -> x9, Pallas kernels: 67.2 us -> 88.5 us  [the longest x1 20 us: shards(): placed_call(partial(out_back_kernel, head_count), [token_block(8), weight...]
    unnamed x184 -> x116, local copies, waits for them, and re-layouts: 27.1 us -> 9.46 us
    convert_element_type x13 -> x11, other arithmetic: 19.9 us -> 3.73 us  [the longest x1 2.13 us: shards(): ((parts[2] + parts_far) * (HALF_TOP / u_scale)).astype(jnp.float16)]
    concatenate x8 -> x4, local copies, waits for them, and re-layouts: 16.5 us -> 1.26 us  [the longest x1 0.72 us: shards(): jnp.concatenate([squares[:4], jnp.full((1, span), largest, f32), jnp.zero...]
    slice x23 -> x4, local copies, waits for them, and re-layouts: 10.6 us -> 2.23 us  [the longest x1 0.95 us: shards(): gain_sum = add_inner(gain_part[0].reshape(8, -1), 1)]
    ppermute x14 -> x8, starting transfers between devices: 24.3 us -> 17.3 us  [shifted(): return lax.ppermute(block, axis, route)]
  transfers between devices with their start and end apart: 95 -> 79, of which waited for: 41 -> 34; matrix products, arithmetic and copies ran while one was open for 22% -> 17% of each run, Pallas kernels for 18% -> 29%
where the time goes in v2:
time: 470 us; the launch traced here: 465 us
  Pallas kernels  156 us (33%)
  waiting for transfers between devices  126 us (27%)
  starting transfers between devices  74.8 us (16%)
  other arithmetic  34.5 us (7%)
  matrix products  29.3 us (6%)
  local copies, waits for them, and re-layouts  26.6 us (6%)
  between operations  17.1 us (4%)
    ppermute x65, waiting for transfers between devices, swap(): lax.ppermute(block, axis, [(a, a ^ bit) for a in range(lax.axis_size(axis...  122 us
    ppermute x65, starting transfers between devices, swap(): lax.ppermute(block, axis, [(a, a ^ bit) for a in range(lax.axis_size(axis...  56.3 us
    pallas_call x1, Pallas kernels, shards(): placed_call(partial(out_back_kernel, head_count), [token_block(8), weight...  20 us
    pallas_call x1, Pallas kernels, shards(): pl.pallas_call(spread(partial(carry_back_kernel, groups, steps), back_in...  17.7 us
    ppermute x8, starting transfers between devices, shifted(): return lax.ppermute(block, axis, route)  17.3 us
    pallas_call x1, Pallas kernels, shards(): pl.pallas_call(normed_back_kernel, grid_spec=pltpu.PrefetchScalarGridSpec...  13.9 us
    dot_general x3, matrix products, contract(): lax.dot_general(left_side, right_side, (((left_dim,), (right_dim,)), ((),...  12.6 us
    pallas_call x1, Pallas kernels, shards(): chunk_call(partial(within_back_kernel, groups), [per_chunk(width), per_ch...  12.2 us
  transfers between devices with their start and end apart: 79, of which 34 were waited for; matrix products, arithmetic and copies ran while one was open for 17% of the time, Pallas kernels for 29%

profile of v2, /device:TPU:0, one launch (start us, length us, event | category | flops | bytes accessed | tf_op | source)
XLA Modules:
  0.0 464.7 jit_solution(10569891106749572063)
XLA Ops:
  7.2 3.0 collective-permute-start
  18.4 2.7 collective-permute-start.6
  23.2 3.5 collective-permute-done.2
  28.5 4.0 collective-permute-done.3
  44.2 3.9 collective-permute-done.9
  49.6 5.0 %collective-permute-done.13.refs_9_ = bf16[16,1024]{1,0:T(8,128)(2,1)S(1)} collective-permute-done((bf16[16,1024]{1,0:T(8,128)(2,1)S(1)}, bf16[16,1024]{1,0:T(8,128)(2,1)S(1)}, u32[]{:S(2)}, u32[]{:S(2)}) %collective-permute-start.13) | collective-permute-done | bytes 32800 | tf_op jit(solution)/shard_map/ppermute | solution.py:32
  63.9 10.1 %norm.1 = (bf16[1024,2048]{1,0:T(8,128)(2,1)}, bf16[4,256,256]{2,1,0:T(8,128)(2,1)}, bf16[1024,256]{1,0:T(8,128)(2,1)}, f32[1024,8]{1,0:T(8,128)}, f32[16,1024]{...) custom-call(s32[2]{0:T(128)} %pad_add_fusion.place_ref.refs_0_, f32[1,2048]{1,0:T(1,128)} %bitcast.202, ...), custom_call_target="tpu_custom_call" | custom-call | tf_op jit(solution)/shard_map/norm/pallas_call | solution.py:1199
  74.0 4.8 %split.1 = (bf16[4,256,256]{2,1,0:T(8,128)(2,1)}, bf16[4,256,256]{2,1,0:T(8,128)(2,1)}, bf16[4,256,256]{2,1,0:T(8,128)(2,1)}, bf16[4,256,256]{2,1,0:T(8,128)(2,1)}) custom-call(s32[2]{0:T(128)} %pad_add_fusion.place_ref.refs_0_, bf16[4,256,1024]{2,1,0:T(8,128)(2,1)} %whole_ref), custom_call_target="tpu_custom_call" | custom-call | tf_op jit(solution)/shard_map/split/pallas_call | solution.py:1244
  83.9 5.6 %vectors.1 = (f32[1024,256]{1,0:T(8,128)}, bf16[1024,256]{1,0:T(8,128)(2,1)}, bf16[256,1024]{1,0:T(8,128)(2,1)}, f32[1024,39]{1,0:T(8,128)}, f32[17,1024]{1,0:T(8,128)}, /*index=5*/f32[8,512]{1,0:T(8,128)}) custom-call(s32[1]{0:T(128)} %bitcast.41.refs_0_, bf16[1024,256]{1,0:T(8,128)(2,1)} %get-tuple-element.196.refs_1_.refs_17_, ...), custom_call_target="tpu_custom_call" | custom-call | tf_op jit(solution)/shard_map/vectors/pallas_call | solution.py:1285
  91.9 6.3 %convolution_convert_fusion.3.refs_0_.refs_13_ = bf16[1024,512]{1,0:T(8,128)(2,1)} fusion(bf16[1024,2048]{1,0:T(8,128)(2,1)} %get-tuple-element.193.normed_ref, bf16[2048,512]{1,0:T(8,128)(2,1)} %all-gather.4.cloned.1.call-done.wi_ref), kind=kOutput, calls=%fused_computation.12 | convolution fusion | flops 2148007936 | bytes 7340032 | tf_op jit(solution)/shard_map/dot_general | solution.py:1332
  99.2 6.8 %convolve.1 = (f32[1024,512]{1,0:T(8,128)}, bf16[1024,512]{1,0:T(8,128)(2,1)}, f32[128,512]{1,0:T(8,128)}) custom-call(bf16[1024,512]{1,0:T(8,128)(2,1)} %convolution_convert_fusion.3.refs_0_.refs_13_, bf16[16,512]{1,0:T(8,128)(2,1)} %convolution_convert_fusion.4.refs_1_.refs_14_, bf16[256,1024]{1,0:T(8,128)(2,1)} %get-tuple-element.200.refs_2_.refs_4_, ...), custom_call_target="tpu_custom_call" | custom-call | tf_op jit(solution)/shard_map/convolve/pallas_call | solution.py:1334
  108.3 3.6 collective-permute-start.26
  113.7 4.5 collective-permute-start.27
  121.8 5.4 %within.1.refs_4_ = f32[1024,512]{1,0:T(8,128)} custom-call(bf16[1024,512]{1,0:T(8,128)(2,1)} %get-tuple-element.208.refs_0_.refs_3_, bf16[1024,256]{1,0:T(8,128)(2,1)} %get-tuple-element.209.refs_1_, f32[1024,39]{1,0:T(8,128)} %get-tuple-element.201.refs_3_.refs_2_.refs_5_, f32[17,1024]{1,0:T(8,128)} %get-tuple-element.210.refs_3_.refs_4_), custom_call_target="tpu_custom_call" | custom-call | tf_op jit(solution)/shard_map/within/pallas_call | solution.py:1352
  127.2 4.1 collective-permute-done.28
  132.1 2.8 collective-permute-done.25.refs_3_.refs_7_
  134.9 6.2 %convolution_convert_fusion.2.refs_5_.refs_2_ = bf16[1024,512]{1,0:T(8,128)(2,1)} fusion(bf16[1024,2048]{1,0:T(8,128)(2,1)} %get-tuple-element.193.normed_ref, bf16[2048,512]{1,0:T(8,128)(2,1)} %all-gather.6.cloned.1.call-done.wg_ref), kind=kOutput, calls=%fused_computation.11 | convolution fusion | flops 2148007936 | bytes 7340032 | tf_op jit(solution)/shard_map/dot_general | solution.py:1361
  141.1 8.4 %carry.1 = (f32[1024,512]{1,0:T(8,128)}, bf16[1024,512]{1,0:T(8,128)(2,1)}, f32[8,1024]{1,0:T(8,128)}, f32[1024,512]{1,0:T(8,128)}) custom-call(bf16[1024,512]{1,0:T(8,128)(2,1)} %get-tuple-element.208.refs_0_.refs_3_, bf16[1024,256]{1,0:T(8,128)(2,1)} %get-tuple-element.209.refs_1_, bf16[256,1024]{1,0:T(8,128)(2,1)} %get-tuple-element.200.refs_2_.refs_4_, ...), custom_call_target="tpu_custom_call" | custom-call | tf_op jit(solution)/shard_map/carry/pallas_call | solution.py:1362
  161.0 23.9 %collective-permute-done.34.refs_2_ = bf16[1024,512]{1,0:T(8,128)(2,1)S(1)} collective-permute-done((bf16[1024,512]{1,0:T(8,128)(2,1)}, bf16[1024,512]{1,0:T(8,128)(2,1)S(1)}, u32[]{:S(2)}, u32[]{:S(2)}) %collective-permute-start.34) | collective-permute-done | bytes 1048608 | tf_op jit(solution)/shard_map/ppermute | solution.py:32
  187.6 20.0 %out_back.1 = (f32[1024,512]{1,0:T(8,128)}, f32[1024,512]{1,0:T(8,128)}, f32[1024,512]{1,0:T(8,128)}, f32[1024,512]{1,0:T(8,128)}, bf16[4,1024,512]{2,1,0:T(8,128)(2,1)}) custom-call(s32[2]{0:T(128)} %pad_add_fusion.place_ref.refs_0_, f32[1024,8]{1,0:T(8,128)} %copy-done, bf16[4,4,512,128]{3,2,1,0:T(8,128)(2,1)} %bitcast.169, ...), custom_call_target="tpu_custom_call" | custom-call | tf_op jit(solution)/shard_map/out_back/pallas_call | solution.py:1414
  210.9 8.0 %out_weight_back.1 = bf16[4,2048,128]{2,1,0:T(8,128)(2,1)} custom-call(s32[2]{0:T(128)} %pad_add_fusion.place_ref.refs_0_, bf16[4,1024,512]{2,1,0:T(8,128)(2,1)} %get-tuple-element.238.sum_ref, bf16[1024,512]{1,0:T(8,128)(2,1)} %get-tuple-element.243.refs_0_, bf16[1024,512]{1,0:T(8,128)(2,1)} %copy-done.12, bf16[1024,512]{1,0:T(8,128)(2,1)} %copy-done.11, ...), custom_call_target="tpu_custom_call" | custom-call | tf_op jit(solution)/shard_map/out_weight_back/pallas_call | solution.py:1426
  223.8 11.2 %products.1 = (f32[8,1024]{1,0:T(8,128)}, f32[4,4,256,256]{3,2,1,0:T(8,128)}, bf16[4,4,256,256]{3,2,1,0:T(8,128)(2,1)}) custom-call(s32[2]{0:T(128)} %pad_add_fusion.place_ref.refs_0_, bf16[4,4,512,128]{3,2,1,0:T(8,128)(2,1)} %bitcast.170, bf16[1024,512]{1,0:T(8,128)(2,1)} %get-tuple-element.243.refs_0_, bf16[1024,512]{1,0:T(8,128)(2,1)} %copy-done.12, ...), custom_call_target="tpu_custom_call" | custom-call | tf_op jit(solution)/shard_map/products/pallas_call | solution.py:1442
  238.5 2.7 collective-permute-done.40
  243.4 5.2 %collective-permute-done.41 = f32[8,1024]{1,0:T(8,128)S(1)} collective-permute-done((f32[8,1024]{1,0:T(8,128)S(1)}, f32[8,1024]{1,0:T(8,128)S(1)}, u32[]{:S(2)}, u32[]{:S(2)}) %collective-permute-start.41) | collective-permute-done | bytes 32800 | tf_op jit(solution)/shard_map/ppermute | solution.py:32
  249.2 3.9 multiply_add_fusion.refs_0_
  253.1 7.7 %gate_back.1 = (f32[1024,512]{1,0:T(8,128)}, bf16[1024,512]{1,0:T(8,128)(2,1)}, f32[8,512]{1,0:T(8,128)}, f32[128,512]{1,0:T(8,128)}) custom-call(f32[1024,512]{1,0:T(8,128)} %multiply_add_fusion.refs_0_, f32[1024,512]{1,0:T(8,128)} %get-tuple-element.242.refs_1_, bf16[1024,512]{1,0:T(8,128)(2,1)} %convolution_convert_fusion.2.refs_5_.refs_2_, ...), custom_call_target="tpu_custom_call" | custom-call | tf_op jit(solution)/shard_map/gate_back/pallas_call | solution.py:1456
  267.1 12.2 %within_back.1 = (f32[1024,512]{1,0:T(8,128)}, f32[1024,256]{1,0:T(8,128)}, f32[1024,16]{1,0:T(8,128)}) custom-call(bf16[1024,512]{1,0:T(8,128)(2,1)} %get-tuple-element.208.refs_0_.refs_3_, bf16[1024,256]{1,0:T(8,128)(2,1)} %get-tuple-element.209.refs_1_, f32[1024,39]{1,0:T(8,128)} %get-tuple-element.201.refs_3_.refs_2_.refs_5_, ...), custom_call_target="tpu_custom_call" | custom-call | tf_op jit(solution)/shard_map/within_back/pallas_call | solution.py:1477
  279.3 3.7 convolution_convert_fusion.1
  283.9 5.0 %collective-permute-done.45.refs_3_ = bf16[4,4,256,256]{3,2,1,0:T(8,128)(2,1)} collective-permute-done((bf16[4,4,256,256]{3,2,1,0:T(8,128)(2,1)}, bf16[4,4,256,256]{3,2,1,0:T(8,128)(2,1)}, u32[]{:S(2)}, u32[]{:S(2)}) %collective-permute-start.45) | collective-permute-done | bytes 2097184 | tf_op jit(solution)/shard_map/ppermute | solution.py:32
  288.9 6.1 %mix.1 = (bf16[4,256,256]{2,1,0:T(8,128)(2,1)}, bf16[4,256,256]{2,1,0:T(8,128)(2,1)}, bf16[4,256,256]{2,1,0:T(8,128)(2,1)}, bf16[4,256,256]{2,1,0:T(8,128)(2,1)}) custom-call(s32[2]{0:T(128)} %pad_add_fusion.place_ref.refs_0_, f32[1024,8]{1,0:T(8,128)} %copy-done, bf16[4,256,256]{2,1,0:T(8,128)(2,1)} %get-tuple-element.262.refs_1_, ...), custom_call_target="tpu_custom_call" | custom-call | tf_op jit(solution)/shard_map/mix/pallas_call | solution.py:1495
  296.9 17.7 %carry_back.1 = (bf16[1024,512]{1,0:T(8,128)(2,1)}, f32[16,768]{1,0:T(8,128)}, f32[8,768]{1,0:T(8,128)}, f32[8,2048]{1,0:T(8,128)}, bf16[1024,256]{1,0:T(8,128)(...) custom-call(bf16[1024,512]{1,0:T(8,128)(2,1)} %get-tuple-element.208.refs_0_.refs_3_, ...), custom_call_target="tpu_custom_call" | custom-call | tf_op jit(solution)/shard_map/carry_back/pallas_call | solution.py:1554
  314.7 5.7 %collective-permute-done.48.refs_3_ = bf16[4,256,256]{2,1,0:T(8,128)(2,1)S(1)} collective-permute-done((bf16[4,256,256]{2,1,0:T(8,128)(2,1)}, bf16[4,256,256]{2,1,0:T(8,128)(2,1)S(1)}, u32[]{:S(2)}, u32[]{:S(2)}) %collective-permute-start.48) | collective-permute-done | bytes 524320 | tf_op jit(solution)/shard_map/ppermute | solution.py:32
  327.5 2.9 fusion.48
  331.8 4.2 collective-permute-done.51
  337.7 4.1 collective-permute-done.52
  341.9 3.0 fusion.12
  348.3 13.9 %normed_back.1 = (f32[256,2048]{1,0:T(8,128)}, f32[256,2048]{1,0:T(8,128)}, bf16[2,256,2048]{2,1,0:T(8,128)(2,1)}, f32[8,2048]{1,0:T(8,128)}) custom-call(s32[2]{0:T(128)} %pad_add_fusion.place_ref.refs_0_, bf16[1024,512]{1,0:T(8,128)(2,1)} %get-tuple-element.259.z_ref, bf16[1024,512]{1,0:T(8,128)(2,1)} %slice_dynamic-update-slice_fusion.inner_ref, ...), custom_call_target="tpu_custom_call" | custom-call | tf_op jit(solution)/shard_map/normed_back/pallas_call | solution.py:1648
  363.8 2.7 collective-permute-done.55
  366.6 3.8 collective-permute-start.56
  370.4 6.0 %convolution_convert_fusion = bf16[2048,512]{1,0:T(8,128)(2,1)} fusion(bf16[1024,2048]{1,0:T(8,128)(2,1)} %get-tuple-element.193.normed_ref, bf16[1024,512]{1,0:T(8,128)(2,1)S(1)} %copy-done.22), kind=kOutput, calls=%fused_computation.1 | convolution fusion | flops 2148532224 | bytes 7340032 | tf_op jit(solution)/shard_map/dot_general | solution.py:1047
  379.0 3.1 collective-permute-done.56
  393.1 4.9 %join.1 = bf16[4,256,1024]{2,1,0:T(8,128)(2,1)} custom-call(s32[2]{0:T(128)} %pad_add_fusion.place_ref.refs_0_, bf16[4,256,256]{2,1,0:T(8,128)(2,1)} %get-tuple-element.303.refs_0_, bf16[4,256,256]{2,1,0:T(8,128)(2,1)} %copy-done.24, bf16[4,256,256]{2,1,0:T(8,128)(2,1)} %copy-done.25, bf16[4,256,256]{2,1,0:T(8,128)(2,1)} %copy-done.26), custom_call_target="tpu_custom_call" | custom-call | tf_op jit(solution)/shard_map/join/pallas_call | solution.py:1712
  398.1 15.3 %collective-permute-done.60 = bf16[256,2048]{1,0:T(8,128)(2,1)S(1)} collective-permute-done((bf16[256,2048]{1,0:T(8,128)(2,1)S(1)}, bf16[256,2048]{1,0:T(8,128)(2,1)S(1)}, u32[]{:S(2)}, u32[]{:S(2)}) %collective-permute-start.60) | collective-permute-done | bytes 1048608 | tf_op jit(solution)/shard_map/ppermute | solution.py:32
  419.2 3.6 collective-permute-done.64
  422.8 4.3 collective-permute-done.65
  427.9 2.5 maximum_select_fusion.refs_0_
  440.4 8.2 %unpack.1 = (f32[2048,256]{1,0:T(8,128)}, f32[4,4096]{1,0:T(4,128)}, f32[1,4096]{1,0:T(1,128)}, f32[1,4096]{1,0:T(1,128)}, f32[4,256]{1,0:T(4,128)}, /*index=5*/...) custom-call(s32[2]{0:T(128)} %pad_add_fusion.place_ref.refs_0_, ...), custom_call_target="tpu_custom_call" | custom-call | tf_op jit(solution)/shard_map/unpack/pallas_call | solution.py:1755
  452.3 4.7 %weight_grad.1 = f32[128,32,128]{2,1,0:T(8,128)} custom-call(s32[2]{0:T(128)} %pad_add_fusion.place_ref.refs_0_, bf16[128,512]{1,0:T(8,128)(2,1)} %get-tuple-element.319.refs_1_, bf16[128,512]{1,0:T(8,128)(2,1)} %copy-done.36, bf16[128,512]{1,0:T(8,128)(2,1)} %copy-done.37, bf16[128,512]{1,0:T(8,128)(2,1)} %copy-done.38, ...), custom_call_target="tpu_custom_call" | custom-call | tf_op jit(solution)/shard_map/weight_grad/pallas_call | solution.py:1781
  (405 shorter events, 136.6 us)
Async XLA Ops:
  7.2 84.7 %all-gather.4.cloned.1.call-start = ((), (), s32[]{:S(2)}) async-start(), calls=%async_computation.3 | async-start | bytes 2621440 | tf_op jit(solution)/shard_map/all_gather | solution.py:1174
  7.2 25.3 %collective-permute-start = (bf16[256,1024]{1,0:T(8,128)(2,1)}, bf16[256,1024]{1,0:T(8,128)(2,1)S(1)}, u32[]{:S(2)}, u32[]{:S(2)}) collective-permute-start(bf16[256,1024]{1,0:T(8,128)(2,1)} %refs_0_), channel_id=1, source_target_pairs={{0,1},{1,0},{2,3},{3,2},{4,5},{5,4},{6,7},{7,6},{8,9},{9,8},{10,11... | collective-permute-start | bytes 1572872 | tf_op jit(solution)/shard_map/ppermute | solution.py:32
  10.2 22.3 %collective-permute-start.1 = (bf16[256,1024]{1,0:T(8,128)(2,1)}, bf16[256,1024]{1,0:T(8,128)(2,1)}, u32[]{:S(2)}, u32[]{:S(2)}) collective-permute-start(bf16[256,1024]{1,0:T(8,128)(2,1)} %refs_0_), channel_id=1, source_target_pairs={{0,4},{2,6},{4,0},{6,2},{1,5},{3,7},{5,1},{7,3},{8,12},{10,14},{12... | collective-permute-start | bytes 1572872 | tf_op jit(solution)/shard_map/ppermute | solution.py:32
  15.5 11.2 %collective-permute-start.2 = (bf16[128,512]{0,1:T(8,128)(2,1)S(1)}, bf16[128,512]{0,1:T(8,128)(2,1)S(1)}, u32[]{:S(2)}, u32[]{:S(2)}) collective-permute-start(bf16[128,512]{0,1:T(8,128)(2,1)S(1)} %dynamic-slice_bitcast_fusion.16), channel_id=1, source_target_pairs={{0,4},{2,6},{4,0},{6,2},{1,5},{3,7},{5,1},{7,3},{8,12},{10,14},{12... | collective-permute-start | bytes 393224 | tf_op jit(solution)/shard_map/ppermute | solution.py:32
  16.0 10.7 %collective-permute-start.7 = (bf16[16,1024]{1,0:T(8,128)(2,1)S(1)}, bf16[16,1024]{1,0:T(8,128)(2,1)S(1)}, u32[]{:S(2)}, u32[]{:S(2)}) collective-permute-start(bf16[16,1024]{1,0:T(8,128)(2,1)S(1)} %slice.147), channel_id=1, source_target_pairs={{0,8},{8,16},{16,24},{1,9},{9,17},{17,25},{2,10},{10,18},{18,26},{... | collective-permute-start | bytes 98312 | tf_op jit(solution)/shard_map/ppermute | solution.py:38
  33.6 101.3 %all-gather.6.cloned.1.call-start = ((), (), s32[]{:S(2)}) async-start(), calls=%async_computation.4 | async-start | bytes 2621440 | tf_op jit(solution)/shard_map/all_gather | solution.py:1195
  35.8 18.8 %collective-permute-start.15 = (bf16[256,1024]{1,0:T(8,128)(2,1)S(1)}, bf16[256,1024]{1,0:T(8,128)(2,1)S(1)}, u32[]{:S(2)}, u32[]{:S(2)}) collective-permute-start(bf16[256,1024]{1,0:T(8,128)(2,1)S(1)} %copy-done.6), channel_id=1, source_target_pairs={{0,2},{2,0},{4,6},{6,4},{1,3},{3,1},{5,7},{7,5},{8,10},{10,8},{12,... | collective-permute-start | bytes 1572872 | tf_op jit(solution)/shard_map/ppermute | solution.py:32
  35.8 18.8 %collective-permute-start.16 = (bf16[256,1024]{1,0:T(8,128)(2,1)S(1)}, bf16[256,1024]{1,0:T(8,128)(2,1)}, u32[]{:S(2)}, u32[]{:S(2)}) collective-permute-start(bf16[256,1024]{1,0:T(8,128)(2,1)S(1)} %collective-permute-done.refs_1_), channel_id=1, source_target_pairs={{0,2},{2,0},{4,6},{6,4},{1,3},{3,1},{5,7},{7,5},{8,10},{10,8},{12,... | collective-permute-start | bytes 1572872 | tf_op jit(solution)/shard_map/ppermute | solution.py:32
  39.6 14.9 %collective-permute-start.14 = (bf16[256,1024]{1,0:T(8,128)(2,1)}, bf16[256,1024]{1,0:T(8,128)(2,1)}, u32[]{:S(2)}, u32[]{:S(2)}) collective-permute-start(bf16[256,1024]{1,0:T(8,128)(2,1)} %collective-permute-done.1.refs_4_), channel_id=1, source_target_pairs={{0,1},{1,0},{2,3},{3,2},{4,5},{5,4},{6,7},{7,6},{8,9},{9,8},{10,11... | collective-permute-start | bytes 1572872 | tf_op jit(solution)/shard_map/ppermute | solution.py:32
  40.0 14.5 %collective-permute-start.13 = (bf16[16,1024]{1,0:T(8,128)(2,1)S(1)}, bf16[16,1024]{1,0:T(8,128)(2,1)S(1)}, u32[]{:S(2)}, u32[]{:S(2)}) collective-permute-start(bf16[16,1024]{1,0:T(8,128)(2,1)S(1)} %add.275.refs_8_), channel_id=1, source_target_pairs={{0,1},{1,0},{2,3},{3,2},{4,5},{5,4},{6,7},{7,6},{8,9},{9,8},{10,11... | collective-permute-start | bytes 98312 | tf_op jit(solution)/shard_map/ppermute | solution.py:32
  55.6 132.1 %all-gather.8.cloned.1.call-start = ((), (), s32[]{:S(2)}) async-start(), calls=%async_computation.5 | async-start | bytes 2621440 | tf_op jit(solution)/shard_map/all_gather | solution.py:1239
  56.3 232.5 %reduce-scatter.4.cloned.1.call-start = ((), (), s32[]{:S(2)}) async-start(), calls=%async_computation.6 | async-start | bytes 2621440 | tf_op jit(solution)/shard_map/reduce_scatter | solution.py:1437
  78.7 11.5 %collective-permute-start.21 = (bf16[4,256,256]{2,1,0:T(8,128)(2,1)}, bf16[4,256,256]{2,1,0:T(8,128)(2,1)S(1)}, u32[]{:S(2)}, u32[]{:S(2)}) collective-permute-start(bf16[4,256,256]{2,1,0:T(8,128)(2,1)} %get-tuple-element.205), channel_id=1, source_target_pairs={{0,2},{2,0},{4,6},{6,4},{1,3},{3,1},{5,7},{7,5},{8,10},{10,8},{12,... | collective-permute-start | bytes 1572872 | tf_op jit(solution)/shard_map/ppermute | solution.py:32
  82.1 36.1 %collective-permute-start.23 = (bf16[4,256,256]{2,1,0:T(8,128)(2,1)}, bf16[4,256,256]{2,1,0:T(8,128)(2,1)}, u32[]{:S(2)}, u32[]{:S(2)}) collective-permute-start(bf16[4,256,256]{2,1,0:T(8,128)(2,1)} %get-tuple-element.206), channel_id=1, source_target_pairs={{0,4},{2,6},{4,0},{6,2},{1,5},{3,7},{5,1},{7,3},{8,12},{10,14},{12... | collective-permute-start | bytes 1572872 | tf_op jit(solution)/shard_map/ppermute | solution.py:32
  83.4 36.2 %collective-permute-start.24 = (bf16[4,256,256]{2,1,0:T(8,128)(2,1)}, bf16[4,256,256]{2,1,0:T(8,128)(2,1)}, u32[]{:S(2)}, u32[]{:S(2)}) collective-permute-start(bf16[4,256,256]{2,1,0:T(8,128)(2,1)} %get-tuple-element.207), channel_id=1, source_target_pairs={{0,6},{2,4},{4,2},{6,0},{1,7},{3,5},{5,3},{7,1},{8,14},{10,12},{12... | collective-permute-start | bytes 1572872 | tf_op jit(solution)/shard_map/ppermute | solution.py:32
  91.4 28.2 %collective-permute-start.22 = (bf16[2,4,256,256]{3,2,1,0:T(8,128)(2,1)S(1)}, bf16[2,4,256,256]{3,2,1,0:T(8,128)(2,1)}, u32[]{:S(2)}, u32[]{:S(2)}) collective-permute-start(bf16[2,4,256,256]{3,2,1,0:T(8,128)(2,1)S(1)} %pad_maximum_fusion.refs_0_.refs_4_), channel_id=1, source_target_pairs={{0,1},{1,0},{2,3},{3,2},{4,5},{5,4},{6,7},{7,6},{8,9},{9,8},{10,11... | collective-permute-start | bytes 3145736 | tf_op jit(solution)/shard_map/ppermute | solution.py:32
  108.3 18.9 %collective-permute-start.26 = (f16[144,512]{1,0:T(8,128)(2,1)S(1)}, f16[144,512]{1,0:T(8,128)(2,1)S(1)}, u32[]{:S(2)}, u32[]{:S(2)}) collective-permute-start(f16[144,512]{1,0:T(8,128)(2,1)S(1)} %concatenate.66), channel_id=1, source_target_pairs={{0,8},{8,16},{16,24},{1,9},{9,17},{17,25},{2,10},{10,18},{18,26},{... | collective-permute-start | bytes 442376 | tf_op jit(solution)/shard_map/ppermute | solution.py:38
  113.7 13.5 %collective-permute-start.27 = (f16[144,512]{1,0:T(8,128)(2,1)S(1)}, f16[144,512]{1,0:T(8,128)(2,1)S(1)}, u32[]{:S(2)}, u32[]{:S(2)}) collective-permute-start(f16[144,512]{1,0:T(8,128)(2,1)S(1)} %concatenate.66), channel_id=1, source_target_pairs={{0,16},{8,24},{1,17},{9,25},{2,18},{10,26},{3,19},{11,27},{4,20},{... | collective-permute-start | bytes 442376 | tf_op jit(solution)/shard_map/ppermute | solution.py:38
  118.2 13.1 %collective-permute-start.28 = (f16[144,512]{1,0:T(8,128)(2,1)S(1)}, f16[144,512]{1,0:T(8,128)(2,1)S(1)}, u32[]{:S(2)}, u32[]{:S(2)}) collective-permute-start(f16[144,512]{1,0:T(8,128)(2,1)S(1)} %concatenate.66), channel_id=1, source_target_pairs={{0,24},{1,25},{2,26},{3,27},{4,28},{5,29},{6,30},{7,31}} | collective-permute-start | bytes 442376 | tf_op jit(solution)/shard_map/ppermute | solution.py:38
  119.7 15.2 %collective-permute-start.25 = (bf16[4,256,256]{2,1,0:T(8,128)(2,1)}, bf16[4,256,256]{2,1,0:T(8,128)(2,1)}, u32[]{:S(2)}, u32[]{:S(2)}) collective-permute-start(bf16[4,256,256]{2,1,0:T(8,128)(2,1)} %collective-permute-done.23.refs_2_.refs_6_), channel_id=1, source_target_pairs={{0,1},{1,0},{2,3},{3,2},{4,5},{5,4},{6,7},{7,6},{8,9},{9,8},{10,11... | collective-permute-start | bytes 1572872 | tf_op jit(solution)/shard_map/ppermute | solution.py:32
  121.2 37.0 %collective-permute-start.29 = (bf16[4,256,256]{2,1,0:T(8,128)(2,1)}, bf16[4,256,256]{2,1,0:T(8,128)(2,1)S(1)}, u32[]{:S(2)}, u32[]{:S(2)}) collective-permute-start(bf16[4,256,256]{2,1,0:T(8,128)(2,1)} %collective-permute-done.24.refs_4_.refs_8_), channel_id=1, source_target_pairs={{0,1},{1,0},{2,3},{3,2},{4,5},{5,4},{6,7},{7,6},{8,9},{9,8},{10,11... | collective-permute-start | bytes 1572872 | tf_op jit(solution)/shard_map/ppermute | solution.py:32
  159.5 25.5 %collective-permute-start.34 = (bf16[1024,512]{1,0:T(8,128)(2,1)}, bf16[1024,512]{1,0:T(8,128)(2,1)S(1)}, u32[]{:S(2)}, u32[]{:S(2)}) collective-permute-start(bf16[1024,512]{1,0:T(8,128)(2,1)} %get-tuple-element.243.refs_0_), channel_id=1, source_target_pairs={{0,4},{2,6},{4,0},{6,2},{1,5},{3,7},{5,1},{7,3},{8,12},{10,14},{12... | collective-permute-start | bytes 3145736 | tf_op jit(solution)/shard_map/ppermute | solution.py:32
  161.0 25.1 %collective-permute-start.33 = (bf16[1024,512]{1,0:T(8,128)(2,1)}, bf16[1024,512]{1,0:T(8,128)(2,1)S(1)}, u32[]{:S(2)}, u32[]{:S(2)}) collective-permute-start(bf16[1024,512]{1,0:T(8,128)(2,1)} %get-tuple-element.243.refs_0_), channel_id=1, source_target_pairs={{0,2},{2,0},{4,6},{6,4},{1,3},{3,1},{5,7},{7,5},{8,10},{10,8},{12,... | collective-permute-start | bytes 3145736 | tf_op jit(solution)/shard_map/ppermute | solution.py:32
  207.7 11.2 %collective-permute-start.37 = (f32[1024,512]{1,0:T(8,128)}, f32[1024,512]{1,0:T(8,128)}, u32[]{:S(2)}, u32[]{:S(2)}) collective-permute-start(f32[1024,512]{1,0:T(8,128)} %get-tuple-element.237), channel_id=1, source_target_pairs={{0,2},{2,0},{4,6},{6,4},{1,3},{3,1},{5,7},{7,5},{8,10},{10,8},{12,... | collective-permute-start | bytes 6291464 | tf_op jit(solution)/shard_map/ppermute | solution.py:32
  207.9 41.4 %collective-permute-start.36 = (f32[1024,512]{1,0:T(8,128)}, f32[1024,512]{1,0:T(8,128)}, u32[]{:S(2)}, u32[]{:S(2)}) collective-permute-start(f32[1024,512]{1,0:T(8,128)} %get-tuple-element.231), channel_id=1, source_target_pairs={{0,2},{2,0},{4,6},{6,4},{1,3},{3,1},{5,7},{7,5},{8,10},{10,8},{12,... | collective-permute-start | bytes 6291464 | tf_op jit(solution)/shard_map/ppermute | solution.py:32
  219.0 122.9 %reduce-scatter.6.cloned.1.call-start = ((), (), s32[]{:S(2)}) async-start(), calls=%async_computation.7 | async-start | bytes 2621440 | tf_op jit(solution)/shard_map/reduce_scatter | solution.py:1503
  222.7 26.6 %collective-permute-start.38 = (f16[1024,512]{1,0:T(8,128)(2,1)S(1)}, f16[1024,512]{1,0:T(8,128)(2,1)}, u32[]{:S(2)}, u32[]{:S(2)}) collective-permute-start(f16[1024,512]{1,0:T(8,128)(2,1)S(1)} %multiply_convert_fusion), channel_id=1, source_target_pairs={{0,4},{2,6},{4,0},{6,2},{1,5},{3,7},{5,1},{7,3},{8,12},{10,14},{12... | collective-permute-start | bytes 3145736 | tf_op jit(solution)/shard_map/ppermute | solution.py:32
  241.8 47.0 %collective-permute-start.45 = (bf16[4,4,256,256]{3,2,1,0:T(8,128)(2,1)}, bf16[4,4,256,256]{3,2,1,0:T(8,128)(2,1)}, u32[]{:S(2)}, u32[]{:S(2)}) collective-permute-start(bf16[4,4,256,256]{3,2,1,0:T(8,128)(2,1)} %get-tuple-element.258), channel_id=1, source_target_pairs={{0,1},{1,0},{2,3},{3,2},{4,5},{5,4},{6,7},{7,6},{8,9},{9,8},{10,11... | collective-permute-start | bytes 6291464 | tf_op jit(solution)/shard_map/ppermute | solution.py:32
  263.2 19.8 %collective-permute-start.42 = (f16[144,512]{1,0:T(8,128)(2,1)S(1)}, f16[144,512]{1,0:T(8,128)(2,1)S(1)}, u32[]{:S(2)}, u32[]{:S(2)}) collective-permute-start(f16[144,512]{1,0:T(8,128)(2,1)S(1)} %concatenate.69), channel_id=1, source_target_pairs={{8,0},{16,8},{24,16},{9,1},{17,9},{25,17},{10,2},{18,10},{26,18},{... | collective-permute-start | bytes 442376 | tf_op jit(solution)/shard_map/ppermute | solution.py:38
  264.5 18.6 %collective-permute-start.43 = (f16[144,512]{1,0:T(8,128)(2,1)S(1)}, f16[144,512]{1,0:T(8,128)(2,1)S(1)}, u32[]{:S(2)}, u32[]{:S(2)}) collective-permute-start(f16[144,512]{1,0:T(8,128)(2,1)S(1)} %concatenate.69), channel_id=1, source_target_pairs={{16,0},{24,8},{17,1},{25,9},{18,2},{26,10},{19,3},{27,11},{20,4},{... | collective-permute-start | bytes 442376 | tf_op jit(solution)/shard_map/ppermute | solution.py:38
  265.8 17.2 %collective-permute-start.44 = (f16[144,512]{1,0:T(8,128)(2,1)S(1)}, f16[144,512]{1,0:T(8,128)(2,1)S(1)}, u32[]{:S(2)}, u32[]{:S(2)}) collective-permute-start(f16[144,512]{1,0:T(8,128)(2,1)S(1)} %concatenate.69), channel_id=1, source_target_pairs={{24,0},{25,1},{26,2},{27,3},{28,4},{29,5},{30,6},{31,7}} | collective-permute-start | bytes 442376 | tf_op jit(solution)/shard_map/ppermute | solution.py:38
  288.9 143.6 %reduce-scatter.8.cloned.1.call-start = ((), (), s32[]{:S(2)}) async-start(), calls=%async_computation.8 | async-start | bytes 2621440 | tf_op jit(solution)/shard_map/reduce_scatter | solution.py:1702
  295.0 19.6 %collective-permute-start.46 = (bf16[4,256,256]{2,1,0:T(8,128)(2,1)}, bf16[4,256,256]{2,1,0:T(8,128)(2,1)S(1)}, u32[]{:S(2)}, u32[]{:S(2)}) collective-permute-start(bf16[4,256,256]{2,1,0:T(8,128)(2,1)} %get-tuple-element.279), channel_id=1, source_target_pairs={{0,2},{2,0},{4,6},{6,4},{1,3},{3,1},{5,7},{7,5},{8,10},{10,8},{12,... | collective-permute-start | bytes 1572872 | tf_op jit(solution)/shard_map/ppermute | solution.py:32
  295.0 19.6 %collective-permute-start.47 = (bf16[4,256,256]{2,1,0:T(8,128)(2,1)}, bf16[4,256,256]{2,1,0:T(8,128)(2,1)S(1)}, u32[]{:S(2)}, u32[]{:S(2)}) collective-permute-start(bf16[4,256,256]{2,1,0:T(8,128)(2,1)} %get-tuple-element.280), channel_id=1, source_target_pairs={{0,4},{2,6},{4,0},{6,2},{1,5},{3,7},{5,1},{7,3},{8,12},{10,14},{12... | collective-permute-start | bytes 1572872 | tf_op jit(solution)/shard_map/ppermute | solution.py:32
  296.5 24.0 %collective-permute-start.48 = (bf16[4,256,256]{2,1,0:T(8,128)(2,1)}, bf16[4,256,256]{2,1,0:T(8,128)(2,1)S(1)}, u32[]{:S(2)}, u32[]{:S(2)}) collective-permute-start(bf16[4,256,256]{2,1,0:T(8,128)(2,1)} %get-tuple-element.281), channel_id=1, source_target_pairs={{0,6},{2,4},{4,2},{6,0},{1,7},{3,5},{5,3},{7,1},{8,14},{10,12},{12... | collective-permute-start | bytes 1572872 | tf_op jit(solution)/shard_map/ppermute | solution.py:32
  326.0 10.1 %collective-permute-start.51 = (f32[64,1280]{1,0:T(8,128)S(1)}, f32[64,1280]{1,0:T(8,128)S(1)}, u32[]{:S(2)}, u32[]{:S(2)}) collective-permute-start(f32[64,1280]{1,0:T(8,128)S(1)} %dynamic-slice_bitcast_fusion.1), channel_id=1, source_target_pairs={{0,4},{2,6},{4,0},{6,2},{1,5},{3,7},{5,1},{7,3},{8,12},{10,14},{12... | collective-permute-start | bytes 983048 | tf_op jit(solution)/shard_map/ppermute | solution.py:32
  330.4 11.5 %collective-permute-start.49 = (f32[8,768]{1,0:T(8,128)S(1)}, f32[8,768]{1,0:T(8,128)S(1)}, u32[]{:S(2)}, u32[]{:S(2)}) collective-permute-start(f32[8,768]{1,0:T(8,128)S(1)} %copy-done.56), channel_id=1, source_target_pairs={{8,0},{16,8},{24,16},{9,1},{17,9},{25,17},{10,2},{18,10},{26,18},{... | collective-permute-start | bytes 73736 | tf_op jit(solution)/shard_map/ppermute | solution.py:38
  345.1 17.1 %collective-permute-start.53 = (bf16[64,2048]{1,0:T(8,128)(2,1)S(1)}, bf16[64,2048]{1,0:T(8,128)(2,1)S(1)}, u32[]{:S(2)}, u32[]{:S(2)}) collective-permute-start(bf16[64,2048]{1,0:T(8,128)(2,1)S(1)} %pad_maximum_fusion.1), channel_id=1, source_target_pairs={{0,8},{8,0},{16,24},{24,16},{1,9},{9,1},{17,25},{25,17},{2,10},{10... | collective-permute-start | bytes 786440 | tf_op jit(solution)/shard_map/ppermute | solution.py:32
  362.3 14.1 %collective-permute-start.54 = (bf16[2,256,2048]{2,1,0:T(8,128)(2,1)}, bf16[2,256,2048]{2,1,0:T(8,128)(2,1)}, u32[]{:S(2)}, u32[]{:S(2)}) collective-permute-start(bf16[2,256,2048]{2,1,0:T(8,128)(2,1)} %get-tuple-element.293), channel_id=1, source_target_pairs={{0,2},{2,0},{4,6},{6,4},{1,3},{3,1},{5,7},{7,5},{8,10},{10,8},{12,... | collective-permute-start | bytes 6291464 | tf_op jit(solution)/shard_map/ppermute | solution.py:32
  366.6 15.5 %collective-permute-start.56 = (bf16[64,2048]{1,0:T(8,128)(2,1)S(1)}, bf16[64,2048]{1,0:T(8,128)(2,1)S(1)}, u32[]{:S(2)}, u32[]{:S(2)}) collective-permute-start(bf16[64,2048]{1,0:T(8,128)(2,1)S(1)} %pad_maximum_fusion.2), channel_id=1, source_target_pairs={{0,16},{8,24},{16,0},{24,8},{1,17},{9,25},{17,1},{25,9},{2,18},{10... | collective-permute-start | bytes 786440 | tf_op jit(solution)/shard_map/ppermute | solution.py:32
  387.6 25.7 %collective-permute-start.60 = (bf16[256,2048]{1,0:T(8,128)(2,1)S(1)}, bf16[256,2048]{1,0:T(8,128)(2,1)S(1)}, u32[]{:S(2)}, u32[]{:S(2)}) collective-permute-start(bf16[256,2048]{1,0:T(8,128)(2,1)S(1)} %fusion.1), channel_id=1, source_target_pairs={{0,4},{2,6},{4,0},{6,2},{1,5},{3,7},{5,1},{7,3},{8,12},{10,14},{12... | collective-permute-start | bytes 3145736 | tf_op jit(solution)/shard_map/ppermute | solution.py:32
  388.9 9.1 %collective-permute-start.62 = (bf16[64,2048]{1,0:T(8,128)(2,1)S(1)}, bf16[64,2048]{1,0:T(8,128)(2,1)S(1)}, u32[]{:S(2)}, u32[]{:S(2)}) collective-permute-start(bf16[64,2048]{1,0:T(8,128)(2,1)S(1)} %get-tuple-element.357), channel_id=1, source_target_pairs={{0,1},{1,0},{2,3},{3,2},{4,5},{5,4},{6,7},{7,6},{8,9},{9,8},{10,11... | collective-permute-start | bytes 786440 | tf_op jit(solution)/shard_map/ppermute | solution.py:32
  413.4 13.8 %collective-permute-start.65 = (bf16[2,64,2048]{2,1,0:T(8,128)(2,1)S(1)}, bf16[2,64,2048]{2,1,0:T(8,128)(2,1)S(1)}, u32[]{:S(2)}, u32[]{:S(2)}) collective-permute-start(bf16[2,64,2048]{2,1,0:T(8,128)(2,1)S(1)} %maximum_select_fusion.1), channel_id=1, source_target_pairs={{0,4},{2,6},{4,0},{6,2},{1,5},{3,7},{5,1},{7,3},{8,12},{10,14},{12... | collective-permute-start | bytes 1572872 | tf_op jit(solution)/shard_map/ppermute | solution.py:32
  417.6 13.6 %collective-permute-start.63 = (bf16[256,1024]{1,0:T(8,128)(2,1)S(1)}, bf16[256,1024]{1,0:T(8,128)(2,1)}, u32[]{:S(2)}, u32[]{:S(2)}) collective-permute-start(bf16[256,1024]{1,0:T(8,128)(2,1)S(1)} %dynamic-slice_convert_fusion), channel_id=1, source_target_pairs={{0,1},{1,0},{2,3},{3,2},{4,5},{5,4},{6,7},{7,6},{8,9},{9,8},{10,11... | collective-permute-start | bytes 1572872 | tf_op jit(solution)/shard_map/ppermute | solution.py:32
  436.7 12.0 %collective-permute-start.70 = (bf16[128,512]{1,0:T(8,128)(2,1)S(1)}, bf16[128,512]{1,0:T(8,128)(2,1)S(1)}, u32[]{:S(2)}, u32[]{:S(2)}) collective-permute-start(bf16[128,512]{1,0:T(8,128)(2,1)S(1)} %get-tuple-element.345), channel_id=1, source_target_pairs={{0,2},{2,0},{4,6},{6,4},{1,3},{3,1},{5,7},{7,5},{8,10},{10,8},{12,... | collective-permute-start | bytes 393224 | tf_op jit(solution)/shard_map/ppermute | solution.py:32
  436.7 12.0 %collective-permute-start.71 = (bf16[128,512]{1,0:T(8,128)(2,1)S(1)}, bf16[128,512]{1,0:T(8,128)(2,1)S(1)}, u32[]{:S(2)}, u32[]{:S(2)}) collective-permute-start(bf16[128,512]{1,0:T(8,128)(2,1)S(1)} %get-tuple-element.344), channel_id=1, source_target_pairs={{0,4},{2,6},{4,0},{6,2},{1,5},{3,7},{5,1},{7,3},{8,12},{10,14},{12... | collective-permute-start | bytes 393224 | tf_op jit(solution)/shard_map/ppermute | solution.py:32
  437.9 10.7 %collective-permute-start.72 = (bf16[128,512]{1,0:T(8,128)(2,1)S(1)}, bf16[128,512]{1,0:T(8,128)(2,1)S(1)}, u32[]{:S(2)}, u32[]{:S(2)}) collective-permute-start(bf16[128,512]{1,0:T(8,128)(2,1)S(1)} %get-tuple-element.343), channel_id=1, source_target_pairs={{0,6},{2,4},{4,2},{6,0},{1,7},{3,5},{5,3},{7,1},{8,14},{10,12},{12... | collective-permute-start | bytes 393224 | tf_op jit(solution)/shard_map/ppermute | solution.py:32
  448.7 8.3 %collective-permute-start.69 = (f32[8,256]{1,0:T(8,128)S(1)}, f32[8,256]{1,0:T(8,128)S(1)}, u32[]{:S(2)}, u32[]{:S(2)}) collective-permute-start(f32[8,256]{1,0:T(8,128)S(1)} %add.324), channel_id=1, source_target_pairs={{0,4},{2,6},{4,0},{6,2},{1,5},{3,7},{5,1},{7,3},{8,12},{10,14},{12... | collective-permute-start | bytes 24584 | tf_op jit(solution)/shard_map/ppermute | solution.py:32
  (88 other events, 630.1 us)
Sparse Core Ops, SparseCore 0:
  33.7 45.3 all-gather.3
  80.7 50.5 all-gather.5
  132.9 50.3 all-gather.7
  219.1 45.8 reduce-scatter.3
  289.0 46.2 reduce-scatter.5
  376.5 41.7 reduce-scatter.7

commit v3 on v2

--- a/solution.py
+++ b/solution.py
@@ -869,7 +869,7 @@
 
 
 def pick_part(near_refs, first_refs, second_refs, cot_ref):
-    step = pl.program_id(0)
+    step = pl.program_id(0) % PLANE
 
     @pl.when(step < 2)
     def _():
@@ -907,36 +907,50 @@
 
 def out_back_kernel(count, place_ref, scale_ref, weight_ref, *refs):
     part_refs = refs[3 * count : 3 * count + PLANE]
-    sum_ref, low_ref, cot_ref = refs[3 * count + PLANE :]
-    pick_part(refs[:count], refs[count : 2 * count], refs[2 * count : 3 * count], cot_ref)
+    sum_ref, cot_ref, up_ref, low_ref, part_ref, sems = refs[3 * count + PLANE :]
+    step = pl.program_id(0)
     place = place_ref[0]
     half = cot_ref.shape[3]
-    for q in range(count):
-        lanes = slice(q * half, (q + 1) * half)
-        total = None
-        for m in range(4):
-            grad = (scale_ref[:, m : m + 1] * cot_ref[q, m].astype(f32)).astype(bf16)
-            total = grad.astype(f32) if m == 0 else total + grad.astype(f32)
-            upper, lower = split_two(total)
-            sum_ref[m, :, lanes] = upper
-            low_ref[m, :, lanes] = lower
     rows = weight_ref.shape[2] // 2
+    tokens = sum_ref.shape[1]
+
+    @pl.when(step < PLANE)
+    def _():
+        pick_part(refs[:count], refs[count : 2 * count], refs[2 * count : 3 * count], cot_ref)
+        here = pl.ds(pl.multiple_of((step ^ place) * tokens, tokens), tokens)
+        for q in range(count):
+            lanes = slice(q * half, (q + 1) * half)
+            total = None
+            for m in range(4):
+                grad = (scale_ref[:, m : m + 1] * cot_ref[q, m].astype(f32)).astype(bf16)
+                total = grad.astype(f32) if m == 0 else total + grad.astype(f32)
+                upper, lower = split_two(total)
+                sum_ref[m, :, lanes] = upper
+                up_ref[m, here, lanes] = upper
+                if m:
+                    low_ref[m - 1, here, lanes] = lower
+
     for r in range(PLANE):
-        owner = place ^ r
-        for side in range(2):
-            level = level_of(owner, side)
-            span = slice(side * rows, (side + 1) * rows)
-            weight = weight_rows_of(weight_ref, count, place_ref[1], owner, span)
-            part = mm_t(sum_ref[level], weight)
-            out_ref = part_refs[r]
-
-            @pl.when(owner < 2)
-            def _():
-                out_ref[:, span] = (part + mm_t(low_ref[level], weight)).astype(out_ref.dtype)
-
-            @pl.when(owner >= 2)
-            def _():
-                out_ref[:, span] = part.astype(out_ref.dtype)
+
+        @pl.when(step == PLANE + r)
+        def _():
+            owner = place ^ r
+            for side in range(2):
+                level = level_of(owner, side)
+                span = slice(side * rows, (side + 1) * rows)
+                weight = weight_rows_of(weight_ref, count, place_ref[1], owner, span)
+                part_ref[r, :, span] = mm_t(up_ref[level], weight)
+
+                @pl.when(owner < 2)
+                def _():
+                    part_ref[r, :, span] += mm_t(low_ref[level - 1], weight)
+
+            pltpu.make_async_copy(part_ref.at[r], part_refs[r], sems.at[r]).start()
+
+    @pl.when(step == 2 * PLANE - 1)
+    def _():
+        for r in range(PLANE):
+            pltpu.make_async_copy(part_ref.at[r], part_refs[r], sems.at[r]).wait()
 
 
 def product_kernel(count, place_ref, weight_ref, *refs):
@@ -1107,12 +1121,12 @@
     def whole_block(*shape):
         return pl.BlockSpec(shape, lambda r, place: (0,) * len(shape))
 
-    def placed_call(kernel, in_specs, out_specs, out_shape, scratch, name):
+    def placed_call(kernel, in_specs, out_specs, out_shape, scratch, name, turns=PLANE):
         return pl.pallas_call(
             kernel,
             grid_spec=pltpu.PrefetchScalarGridSpec(
                 num_scalar_prefetch=1,
-                grid=(PLANE,),
+                grid=(turns,),
                 in_specs=in_specs,
                 out_specs=out_specs,
                 scratch_shapes=scratch,
@@ -1407,20 +1421,31 @@
     cot_near_block = pl.BlockSpec(
         (1, 4, tok_rows, half), lambda r, place: (jnp.minimum(r, 1), 0, 0, 0)
     )
+    first_turns = pl.BlockSpec((tok_rows, 8), lambda r, place: (jnp.minimum(r, PLANE - 1) ^ place[0], 0))
     cot_blocks = [cot_near_block] * head_count
     cot_blocks += [whole_block(4, tok_rows, half)] * (2 * head_count)
     cot_scratch = pltpu.VMEM((head_count, 4, tok_rows, half), bf16)
     cot_shape = shaped((PLANE, 4, tok_rows, half), bf16)
     *parts, sums = placed_call(
         partial(out_back_kernel, head_count),
-        [token_block(8), weight_block] + cot_blocks,
-        [token_block(width)] * PLANE
+        [first_turns, weight_block] + cot_blocks,
+        [pl.BlockSpec(memory_space=pl.ANY)] * PLANE
         + [
-            pl.BlockSpec((4, tok_rows, head_count * half), lambda r, place: (0, r ^ place[0], 0)),
+            pl.BlockSpec(
+                (4, tok_rows, head_count * half),
+                lambda r, place: (0, jnp.minimum(r, PLANE - 1) ^ place[0], 0),
+            ),
         ],
         [wide_out] * PLANE + [shaped((4, span, head_count * half), bf16)],
-        [pltpu.VMEM((4, tok_rows, head_count * half), bf16), cot_scratch],
+        [
+            cot_scratch,
+            pltpu.VMEM((4, span, head_count * half), bf16),
+            pltpu.VMEM((3, span, head_count * half), bf16),
+            pltpu.VMEM((PLANE, span, width), f32),
+            pltpu.SemaphoreType.DMA((PLANE,)),
+        ],
         "out_back",
+        2 * PLANE,
     )(here, scales, weight_out, *cots)
     u_scale = jnp.exp2(jnp.ceil(jnp.log2(jnp.clip(u_bound, 1e-30, 1e30))))
     out_grad = placed_call(

time: 470 us -> 465 us (0.989)
  Pallas kernels: 156 us -> 151 us
    pallas_call x1, Pallas kernels: 20 us -> 14.9 us  [shards(): placed_call(partial(out_back_kernel, head_count), [first_turns, weight_bl...]
  transfers between devices with their start and end apart: 79 -> 79, of which waited for: 34 -> 34; matrix products, arithmetic and copies ran while one was open for 17% -> 17% of each run, Pallas kernels for 29% -> 30%
where the time goes in v3:
time: 465 us; the launch traced here: 460 us
  Pallas kernels  151 us (32%)
  waiting for transfers between devices  127 us (27%)
  starting transfers between devices  74 us (16%)
  other arithmetic  34.4 us (7%)
  matrix products  29.3 us (6%)
  local copies, waits for them, and re-layouts  27 us (6%)
  between operations  17.3 us (4%)
    ppermute x65, waiting for transfers between devices, swap(): lax.ppermute(block, axis, [(a, a ^ bit) for a in range(lax.axis_size(axis...  122 us
    ppermute x65, starting transfers between devices, swap(): lax.ppermute(block, axis, [(a, a ^ bit) for a in range(lax.axis_size(axis...  56.2 us
    pallas_call x1, Pallas kernels, shards(): pl.pallas_call(spread(partial(carry_back_kernel, groups, steps), back_in...  17.8 us
    ppermute x8, starting transfers between devices, shifted(): return lax.ppermute(block, axis, route)  17.4 us
    pallas_call x1, Pallas kernels, shards(): placed_call(partial(out_back_kernel, head_count), [first_turns, weight_bl...  14.9 us
    pallas_call x1, Pallas kernels, shards(): pl.pallas_call(normed_back_kernel, grid_spec=pltpu.PrefetchScalarGridSpec...  13.9 us
    dot_general x3, matrix products, contract(): lax.dot_general(left_side, right_side, (((left_dim,), (right_dim,)), ((),...  12.6 us
    pallas_call x1, Pallas kernels, shards(): chunk_call(partial(within_back_kernel, groups), [per_chunk(width), per_ch...  12.2 us
  transfers between devices with their start and end apart: 79, of which 34 were waited for; matrix products, arithmetic and copies ran while one was open for 17% of the time, Pallas kernels for 30%

profile of v3, /device:TPU:0, one launch (start us, length us, event | category | flops | bytes accessed | tf_op | source)
XLA Modules:
  0.0 459.9 jit_solution(1873700852548776844)
XLA Ops:
  7.2 3.0 collective-permute-start
  18.4 2.7 collective-permute-start.6
  23.2 3.5 collective-permute-done.2
  28.5 4.0 collective-permute-done.3
  44.2 3.9 collective-permute-done.9
  49.6 5.0 %collective-permute-done.13.refs_9_ = bf16[16,1024]{1,0:T(8,128)(2,1)S(1)} collective-permute-done((bf16[16,1024]{1,0:T(8,128)(2,1)S(1)}, bf16[16,1024]{1,0:T(8,128)(2,1)S(1)}, u32[]{:S(2)}, u32[]{:S(2)}) %collective-permute-start.13) | collective-permute-done | bytes 32800 | tf_op jit(solution)/shard_map/ppermute | solution.py:32
  63.6 10.0 %norm.1 = (bf16[1024,2048]{1,0:T(8,128)(2,1)}, bf16[4,256,256]{2,1,0:T(8,128)(2,1)}, bf16[1024,256]{1,0:T(8,128)(2,1)}, f32[1024,8]{1,0:T(8,128)}, f32[16,1024]{...) custom-call(s32[2]{0:T(128)} %pad_add_fusion.place_ref.refs_0_, f32[1,2048]{1,0:T(1,128)} %bitcast.202, ...), custom_call_target="tpu_custom_call" | custom-call | tf_op jit(solution)/shard_map/norm/pallas_call | solution.py:1213
  73.6 4.8 %split.1 = (bf16[4,256,256]{2,1,0:T(8,128)(2,1)}, bf16[4,256,256]{2,1,0:T(8,128)(2,1)}, bf16[4,256,256]{2,1,0:T(8,128)(2,1)}, bf16[4,256,256]{2,1,0:T(8,128)(2,1)}) custom-call(s32[2]{0:T(128)} %pad_add_fusion.place_ref.refs_0_, bf16[4,256,1024]{2,1,0:T(8,128)(2,1)} %whole_ref), custom_call_target="tpu_custom_call" | custom-call | tf_op jit(solution)/shard_map/split/pallas_call | solution.py:1258
  83.6 5.6 %vectors.1 = (f32[1024,256]{1,0:T(8,128)}, bf16[1024,256]{1,0:T(8,128)(2,1)}, bf16[256,1024]{1,0:T(8,128)(2,1)}, f32[1024,39]{1,0:T(8,128)}, f32[17,1024]{1,0:T(8,128)}, /*index=5*/f32[8,512]{1,0:T(8,128)}) custom-call(s32[1]{0:T(128)} %bitcast.41.refs_0_, bf16[1024,256]{1,0:T(8,128)(2,1)} %get-tuple-element.196.refs_1_.refs_17_, ...), custom_call_target="tpu_custom_call" | custom-call | tf_op jit(solution)/shard_map/vectors/pallas_call | solution.py:1299
  91.6 6.3 %convolution_convert_fusion.3.refs_0_.refs_13_ = bf16[1024,512]{1,0:T(8,128)(2,1)} fusion(bf16[1024,2048]{1,0:T(8,128)(2,1)} %get-tuple-element.193.normed_ref, bf16[2048,512]{1,0:T(8,128)(2,1)} %all-gather.4.cloned.1.call-done.wi_ref), kind=kOutput, calls=%fused_computation.12 | convolution fusion | flops 2148007936 | bytes 7340032 | tf_op jit(solution)/shard_map/dot_general | solution.py:1346
  98.9 6.8 %convolve.1 = (f32[1024,512]{1,0:T(8,128)}, bf16[1024,512]{1,0:T(8,128)(2,1)}, f32[128,512]{1,0:T(8,128)}) custom-call(bf16[1024,512]{1,0:T(8,128)(2,1)} %convolution_convert_fusion.3.refs_0_.refs_13_, bf16[16,512]{1,0:T(8,128)(2,1)} %convolution_convert_fusion.4.refs_1_.refs_14_, bf16[256,1024]{1,0:T(8,128)(2,1)} %get-tuple-element.200.refs_2_.refs_4_, ...), custom_call_target="tpu_custom_call" | custom-call | tf_op jit(solution)/shard_map/convolve/pallas_call | solution.py:1348
  107.9 3.7 collective-permute-start.26
  113.4 4.5 collective-permute-start.27
  121.7 5.4 %within.1.refs_4_ = f32[1024,512]{1,0:T(8,128)} custom-call(bf16[1024,512]{1,0:T(8,128)(2,1)} %get-tuple-element.208.refs_0_.refs_3_, bf16[1024,256]{1,0:T(8,128)(2,1)} %get-tuple-element.209.refs_1_, f32[1024,39]{1,0:T(8,128)} %get-tuple-element.201.refs_3_.refs_2_.refs_5_, f32[17,1024]{1,0:T(8,128)} %get-tuple-element.210.refs_3_.refs_4_), custom_call_target="tpu_custom_call" | custom-call | tf_op jit(solution)/shard_map/within/pallas_call | solution.py:1366
  127.1 4.1 collective-permute-done.28
  132.1 2.7 collective-permute-done.25.refs_3_.refs_7_
  134.8 6.2 %convolution_convert_fusion.2.refs_5_.refs_2_ = bf16[1024,512]{1,0:T(8,128)(2,1)} fusion(bf16[1024,2048]{1,0:T(8,128)(2,1)} %get-tuple-element.193.normed_ref, bf16[2048,512]{1,0:T(8,128)(2,1)} %all-gather.6.cloned.1.call-done.wg_ref), kind=kOutput, calls=%fused_computation.11 | convolution fusion | flops 2148007936 | bytes 7340032 | tf_op jit(solution)/shard_map/dot_general | solution.py:1375
  141.0 8.4 %carry.1 = (f32[1024,512]{1,0:T(8,128)}, bf16[1024,512]{1,0:T(8,128)(2,1)}, f32[8,1024]{1,0:T(8,128)}, f32[1024,512]{1,0:T(8,128)}) custom-call(bf16[1024,512]{1,0:T(8,128)(2,1)} %get-tuple-element.208.refs_0_.refs_3_, bf16[1024,256]{1,0:T(8,128)(2,1)} %get-tuple-element.209.refs_1_, bf16[256,1024]{1,0:T(8,128)(2,1)} %get-tuple-element.200.refs_2_.refs_4_, ...), custom_call_target="tpu_custom_call" | custom-call | tf_op jit(solution)/shard_map/carry/pallas_call | solution.py:1376
  160.9 24.0 %collective-permute-done.34.refs_2_ = bf16[1024,512]{1,0:T(8,128)(2,1)S(1)} collective-permute-done((bf16[1024,512]{1,0:T(8,128)(2,1)}, bf16[1024,512]{1,0:T(8,128)(2,1)S(1)}, u32[]{:S(2)}, u32[]{:S(2)}) %collective-permute-start.34) | collective-permute-done | bytes 1048608 | tf_op jit(solution)/shard_map/ppermute | solution.py:32
  187.6 14.9 %out_back.1 = (f32[1024,512]{1,0:T(8,128)}, f32[1024,512]{1,0:T(8,128)}, f32[1024,512]{1,0:T(8,128)}, f32[1024,512]{1,0:T(8,128)}, bf16[4,1024,512]{2,1,0:T(8,128)(2,1)}) custom-call(s32[2]{0:T(128)} %pad_add_fusion.place_ref.refs_0_, f32[1024,8]{1,0:T(8,128)} %copy-done, bf16[4,4,512,128]{3,2,1,0:T(8,128)(2,1)} %bitcast.169, ...), custom_call_target="tpu_custom_call" | custom-call | tf_op jit(solution)/shard_map/out_back/pallas_call | solution.py:1429
  205.7 8.2 %out_weight_back.1 = bf16[4,2048,128]{2,1,0:T(8,128)(2,1)} custom-call(s32[2]{0:T(128)} %pad_add_fusion.place_ref.refs_0_, bf16[4,1024,512]{2,1,0:T(8,128)(2,1)} %get-tuple-element.238.sum_ref, bf16[1024,512]{1,0:T(8,128)(2,1)} %get-tuple-element.243.refs_0_, bf16[1024,512]{1,0:T(8,128)(2,1)} %copy-done.12, bf16[1024,512]{1,0:T(8,128)(2,1)} %copy-done.11, ...), custom_call_target="tpu_custom_call" | custom-call | tf_op jit(solution)/shard_map/out_weight_back/pallas_call | solution.py:1451
  219.1 11.2 %products.1 = (f32[8,1024]{1,0:T(8,128)}, f32[4,4,256,256]{3,2,1,0:T(8,128)}, bf16[4,4,256,256]{3,2,1,0:T(8,128)(2,1)}) custom-call(s32[2]{0:T(128)} %pad_add_fusion.place_ref.refs_0_, bf16[4,4,512,128]{3,2,1,0:T(8,128)(2,1)} %bitcast.170, bf16[1024,512]{1,0:T(8,128)(2,1)} %get-tuple-element.243.refs_0_, bf16[1024,512]{1,0:T(8,128)(2,1)} %copy-done.12, ...), custom_call_target="tpu_custom_call" | custom-call | tf_op jit(solution)/shard_map/products/pallas_call | solution.py:1467
  233.9 2.7 collective-permute-done.40
  238.4 5.2 %collective-permute-done.41 = f32[8,1024]{1,0:T(8,128)S(1)} collective-permute-done((f32[8,1024]{1,0:T(8,128)S(1)}, f32[8,1024]{1,0:T(8,128)S(1)}, u32[]{:S(2)}, u32[]{:S(2)}) %collective-permute-start.41) | collective-permute-done | bytes 32800 | tf_op jit(solution)/shard_map/ppermute | solution.py:32
  244.3 3.8 multiply_add_fusion.refs_0_
  248.1 7.7 %gate_back.1 = (f32[1024,512]{1,0:T(8,128)}, bf16[1024,512]{1,0:T(8,128)(2,1)}, f32[8,512]{1,0:T(8,128)}, f32[128,512]{1,0:T(8,128)}) custom-call(f32[1024,512]{1,0:T(8,128)} %multiply_add_fusion.refs_0_, f32[1024,512]{1,0:T(8,128)} %get-tuple-element.242.refs_1_, bf16[1024,512]{1,0:T(8,128)(2,1)} %convolution_convert_fusion.2.refs_5_.refs_2_, ...), custom_call_target="tpu_custom_call" | custom-call | tf_op jit(solution)/shard_map/gate_back/pallas_call | solution.py:1481
  262.1 12.2 %within_back.1 = (f32[1024,512]{1,0:T(8,128)}, f32[1024,256]{1,0:T(8,128)}, f32[1024,16]{1,0:T(8,128)}) custom-call(bf16[1024,512]{1,0:T(8,128)(2,1)} %get-tuple-element.208.refs_0_.refs_3_, bf16[1024,256]{1,0:T(8,128)(2,1)} %get-tuple-element.209.refs_1_, f32[1024,39]{1,0:T(8,128)} %get-tuple-element.201.refs_3_.refs_2_.refs_5_, ...), custom_call_target="tpu_custom_call" | custom-call | tf_op jit(solution)/shard_map/within_back/pallas_call | solution.py:1502
  274.3 3.7 convolution_convert_fusion.1
  278.9 5.0 %collective-permute-done.45.refs_3_ = bf16[4,4,256,256]{3,2,1,0:T(8,128)(2,1)} collective-permute-done((bf16[4,4,256,256]{3,2,1,0:T(8,128)(2,1)}, bf16[4,4,256,256]{3,2,1,0:T(8,128)(2,1)}, u32[]{:S(2)}, u32[]{:S(2)}) %collective-permute-start.45) | collective-permute-done | bytes 2097184 | tf_op jit(solution)/shard_map/ppermute | solution.py:32
  283.9 6.3 %mix.1 = (bf16[4,256,256]{2,1,0:T(8,128)(2,1)}, bf16[4,256,256]{2,1,0:T(8,128)(2,1)}, bf16[4,256,256]{2,1,0:T(8,128)(2,1)}, bf16[4,256,256]{2,1,0:T(8,128)(2,1)}) custom-call(s32[2]{0:T(128)} %pad_add_fusion.place_ref.refs_0_, f32[1024,8]{1,0:T(8,128)} %copy-done, bf16[4,256,256]{2,1,0:T(8,128)(2,1)} %get-tuple-element.262.refs_1_, ...), custom_call_target="tpu_custom_call" | custom-call | tf_op jit(solution)/shard_map/mix/pallas_call | solution.py:1520
  292.1 17.8 %carry_back.1 = (bf16[1024,512]{1,0:T(8,128)(2,1)}, f32[16,768]{1,0:T(8,128)}, f32[8,768]{1,0:T(8,128)}, f32[8,2048]{1,0:T(8,128)}, bf16[1024,256]{1,0:T(8,128)(...) custom-call(bf16[1024,512]{1,0:T(8,128)(2,1)} %get-tuple-element.208.refs_0_.refs_3_, ...), custom_call_target="tpu_custom_call" | custom-call | tf_op jit(solution)/shard_map/carry_back/pallas_call | solution.py:1579
  310.0 5.7 %collective-permute-done.48.refs_3_ = bf16[4,256,256]{2,1,0:T(8,128)(2,1)S(1)} collective-permute-done((bf16[4,256,256]{2,1,0:T(8,128)(2,1)}, bf16[4,256,256]{2,1,0:T(8,128)(2,1)S(1)}, u32[]{:S(2)}, u32[]{:S(2)}) %collective-permute-start.48) | collective-permute-done | bytes 524320 | tf_op jit(solution)/shard_map/ppermute | solution.py:32
  323.0 2.9 fusion.48
  327.2 4.1 collective-permute-done.51
  332.9 4.1 collective-permute-done.52
  337.1 3.0 fusion.12
  343.7 13.9 %normed_back.1 = (f32[256,2048]{1,0:T(8,128)}, f32[256,2048]{1,0:T(8,128)}, bf16[2,256,2048]{2,1,0:T(8,128)(2,1)}, f32[8,2048]{1,0:T(8,128)}) custom-call(s32[2]{0:T(128)} %pad_add_fusion.place_ref.refs_0_, bf16[1024,512]{1,0:T(8,128)(2,1)} %get-tuple-element.259.z_ref, bf16[1024,512]{1,0:T(8,128)(2,1)} %slice_dynamic-update-slice_fusion.inner_ref, ...), custom_call_target="tpu_custom_call" | custom-call | tf_op jit(solution)/shard_map/normed_back/pallas_call | solution.py:1673
  359.2 2.7 collective-permute-done.55
  362.0 3.8 collective-permute-start.56
  365.8 6.0 %convolution_convert_fusion = bf16[2048,512]{1,0:T(8,128)(2,1)} fusion(bf16[1024,2048]{1,0:T(8,128)(2,1)} %get-tuple-element.193.normed_ref, bf16[1024,512]{1,0:T(8,128)(2,1)S(1)} %copy-done.22), kind=kOutput, calls=%fused_computation.1 | convolution fusion | flops 2148532224 | bytes 7340032 | tf_op jit(solution)/shard_map/dot_general | solution.py:1061
  374.4 3.1 collective-permute-done.56
  388.8 4.9 %join.1 = bf16[4,256,1024]{2,1,0:T(8,128)(2,1)} custom-call(s32[2]{0:T(128)} %pad_add_fusion.place_ref.refs_0_, bf16[4,256,256]{2,1,0:T(8,128)(2,1)} %get-tuple-element.303.refs_0_, bf16[4,256,256]{2,1,0:T(8,128)(2,1)} %copy-done.24, bf16[4,256,256]{2,1,0:T(8,128)(2,1)} %copy-done.25, bf16[4,256,256]{2,1,0:T(8,128)(2,1)} %copy-done.26), custom_call_target="tpu_custom_call" | custom-call | tf_op jit(solution)/shard_map/join/pallas_call | solution.py:1737
  393.8 15.0 %collective-permute-done.60 = bf16[256,2048]{1,0:T(8,128)(2,1)S(1)} collective-permute-done((bf16[256,2048]{1,0:T(8,128)(2,1)S(1)}, bf16[256,2048]{1,0:T(8,128)(2,1)S(1)}, u32[]{:S(2)}, u32[]{:S(2)}) %collective-permute-start.60) | collective-permute-done | bytes 1048608 | tf_op jit(solution)/shard_map/ppermute | solution.py:32
  414.8 3.6 collective-permute-done.64
  418.4 4.1 collective-permute-done.65
  423.3 2.5 maximum_select_fusion.refs_0_
  436.0 8.0 %unpack.1 = (f32[2048,256]{1,0:T(8,128)}, f32[4,4096]{1,0:T(4,128)}, f32[1,4096]{1,0:T(1,128)}, f32[1,4096]{1,0:T(1,128)}, f32[4,256]{1,0:T(4,128)}, /*index=5*/...) custom-call(s32[2]{0:T(128)} %pad_add_fusion.place_ref.refs_0_, ...), custom_call_target="tpu_custom_call" | custom-call | tf_op jit(solution)/shard_map/unpack/pallas_call | solution.py:1780
  447.3 4.7 %weight_grad.1 = f32[128,32,128]{2,1,0:T(8,128)} custom-call(s32[2]{0:T(128)} %pad_add_fusion.place_ref.refs_0_, bf16[128,512]{1,0:T(8,128)(2,1)} %get-tuple-element.319.refs_1_, bf16[128,512]{1,0:T(8,128)(2,1)} %copy-done.36, bf16[128,512]{1,0:T(8,128)(2,1)} %copy-done.37, bf16[128,512]{1,0:T(8,128)(2,1)} %copy-done.38, ...), custom_call_target="tpu_custom_call" | custom-call | tf_op jit(solution)/shard_map/weight_grad/pallas_call | solution.py:1806
  (405 shorter events, 137.0 us)
Async XLA Ops:
  7.2 84.4 %all-gather.4.cloned.1.call-start = ((), (), s32[]{:S(2)}) async-start(), calls=%async_computation.3 | async-start | bytes 2621440 | tf_op jit(solution)/shard_map/all_gather | solution.py:1188
  7.2 25.3 %collective-permute-start = (bf16[256,1024]{1,0:T(8,128)(2,1)}, bf16[256,1024]{1,0:T(8,128)(2,1)S(1)}, u32[]{:S(2)}, u32[]{:S(2)}) collective-permute-start(bf16[256,1024]{1,0:T(8,128)(2,1)} %refs_0_), channel_id=1, source_target_pairs={{0,1},{1,0},{2,3},{3,2},{4,5},{5,4},{6,7},{7,6},{8,9},{9,8},{10,11... | collective-permute-start | bytes 1572872 | tf_op jit(solution)/shard_map/ppermute | solution.py:32
  10.2 22.3 %collective-permute-start.1 = (bf16[256,1024]{1,0:T(8,128)(2,1)}, bf16[256,1024]{1,0:T(8,128)(2,1)}, u32[]{:S(2)}, u32[]{:S(2)}) collective-permute-start(bf16[256,1024]{1,0:T(8,128)(2,1)} %refs_0_), channel_id=1, source_target_pairs={{0,4},{2,6},{4,0},{6,2},{1,5},{3,7},{5,1},{7,3},{8,12},{10,14},{12... | collective-permute-start | bytes 1572872 | tf_op jit(solution)/shard_map/ppermute | solution.py:32
  15.5 11.2 %collective-permute-start.2 = (bf16[128,512]{0,1:T(8,128)(2,1)S(1)}, bf16[128,512]{0,1:T(8,128)(2,1)S(1)}, u32[]{:S(2)}, u32[]{:S(2)}) collective-permute-start(bf16[128,512]{0,1:T(8,128)(2,1)S(1)} %dynamic-slice_bitcast_fusion.16), channel_id=1, source_target_pairs={{0,4},{2,6},{4,0},{6,2},{1,5},{3,7},{5,1},{7,3},{8,12},{10,14},{12... | collective-permute-start | bytes 393224 | tf_op jit(solution)/shard_map/ppermute | solution.py:32
  16.0 10.7 %collective-permute-start.7 = (bf16[16,1024]{1,0:T(8,128)(2,1)S(1)}, bf16[16,1024]{1,0:T(8,128)(2,1)S(1)}, u32[]{:S(2)}, u32[]{:S(2)}) collective-permute-start(bf16[16,1024]{1,0:T(8,128)(2,1)S(1)} %slice.147), channel_id=1, source_target_pairs={{0,8},{8,16},{16,24},{1,9},{9,17},{17,25},{2,10},{10,18},{18,26},{... | collective-permute-start | bytes 98312 | tf_op jit(solution)/shard_map/ppermute | solution.py:38
  33.6 101.2 %all-gather.6.cloned.1.call-start = ((), (), s32[]{:S(2)}) async-start(), calls=%async_computation.4 | async-start | bytes 2621440 | tf_op jit(solution)/shard_map/all_gather | solution.py:1209
  35.8 18.8 %collective-permute-start.15 = (bf16[256,1024]{1,0:T(8,128)(2,1)S(1)}, bf16[256,1024]{1,0:T(8,128)(2,1)S(1)}, u32[]{:S(2)}, u32[]{:S(2)}) collective-permute-start(bf16[256,1024]{1,0:T(8,128)(2,1)S(1)} %copy-done.6), channel_id=1, source_target_pairs={{0,2},{2,0},{4,6},{6,4},{1,3},{3,1},{5,7},{7,5},{8,10},{10,8},{12,... | collective-permute-start | bytes 1572872 | tf_op jit(solution)/shard_map/ppermute | solution.py:32
  35.8 18.8 %collective-permute-start.16 = (bf16[256,1024]{1,0:T(8,128)(2,1)S(1)}, bf16[256,1024]{1,0:T(8,128)(2,1)}, u32[]{:S(2)}, u32[]{:S(2)}) collective-permute-start(bf16[256,1024]{1,0:T(8,128)(2,1)S(1)} %collective-permute-done.refs_1_), channel_id=1, source_target_pairs={{0,2},{2,0},{4,6},{6,4},{1,3},{3,1},{5,7},{7,5},{8,10},{10,8},{12,... | collective-permute-start | bytes 1572872 | tf_op jit(solution)/shard_map/ppermute | solution.py:32
  39.6 14.9 %collective-permute-start.14 = (bf16[256,1024]{1,0:T(8,128)(2,1)}, bf16[256,1024]{1,0:T(8,128)(2,1)}, u32[]{:S(2)}, u32[]{:S(2)}) collective-permute-start(bf16[256,1024]{1,0:T(8,128)(2,1)} %collective-permute-done.1.refs_4_), channel_id=1, source_target_pairs={{0,1},{1,0},{2,3},{3,2},{4,5},{5,4},{6,7},{7,6},{8,9},{9,8},{10,11... | collective-permute-start | bytes 1572872 | tf_op jit(solution)/shard_map/ppermute | solution.py:32
  40.0 14.5 %collective-permute-start.13 = (bf16[16,1024]{1,0:T(8,128)(2,1)S(1)}, bf16[16,1024]{1,0:T(8,128)(2,1)S(1)}, u32[]{:S(2)}, u32[]{:S(2)}) collective-permute-start(bf16[16,1024]{1,0:T(8,128)(2,1)S(1)} %add.275.refs_8_), channel_id=1, source_target_pairs={{0,1},{1,0},{2,3},{3,2},{4,5},{5,4},{6,7},{7,6},{8,9},{9,8},{10,11... | collective-permute-start | bytes 98312 | tf_op jit(solution)/shard_map/ppermute | solution.py:32
  55.6 132.0 %all-gather.8.cloned.1.call-start = ((), (), s32[]{:S(2)}) async-start(), calls=%async_computation.5 | async-start | bytes 2621440 | tf_op jit(solution)/shard_map/all_gather | solution.py:1253
  56.3 227.5 %reduce-scatter.4.cloned.1.call-start = ((), (), s32[]{:S(2)}) async-start(), calls=%async_computation.6 | async-start | bytes 2621440 | tf_op jit(solution)/shard_map/reduce_scatter | solution.py:1462
  78.4 11.5 %collective-permute-start.21 = (bf16[4,256,256]{2,1,0:T(8,128)(2,1)}, bf16[4,256,256]{2,1,0:T(8,128)(2,1)S(1)}, u32[]{:S(2)}, u32[]{:S(2)}) collective-permute-start(bf16[4,256,256]{2,1,0:T(8,128)(2,1)} %get-tuple-element.205), channel_id=1, source_target_pairs={{0,2},{2,0},{4,6},{6,4},{1,3},{3,1},{5,7},{7,5},{8,10},{10,8},{12,... | collective-permute-start | bytes 1572872 | tf_op jit(solution)/shard_map/ppermute | solution.py:32
  81.7 36.1 %collective-permute-start.23 = (bf16[4,256,256]{2,1,0:T(8,128)(2,1)}, bf16[4,256,256]{2,1,0:T(8,128)(2,1)}, u32[]{:S(2)}, u32[]{:S(2)}) collective-permute-start(bf16[4,256,256]{2,1,0:T(8,128)(2,1)} %get-tuple-element.206), channel_id=1, source_target_pairs={{0,4},{2,6},{4,0},{6,2},{1,5},{3,7},{5,1},{7,3},{8,12},{10,14},{12... | collective-permute-start | bytes 1572872 | tf_op jit(solution)/shard_map/ppermute | solution.py:32
  83.1 36.4 %collective-permute-start.24 = (bf16[4,256,256]{2,1,0:T(8,128)(2,1)}, bf16[4,256,256]{2,1,0:T(8,128)(2,1)}, u32[]{:S(2)}, u32[]{:S(2)}) collective-permute-start(bf16[4,256,256]{2,1,0:T(8,128)(2,1)} %get-tuple-element.207), channel_id=1, source_target_pairs={{0,6},{2,4},{4,2},{6,0},{1,7},{3,5},{5,3},{7,1},{8,14},{10,12},{12... | collective-permute-start | bytes 1572872 | tf_op jit(solution)/shard_map/ppermute | solution.py:32
  91.1 28.5 %collective-permute-start.22 = (bf16[2,4,256,256]{3,2,1,0:T(8,128)(2,1)S(1)}, bf16[2,4,256,256]{3,2,1,0:T(8,128)(2,1)}, u32[]{:S(2)}, u32[]{:S(2)}) collective-permute-start(bf16[2,4,256,256]{3,2,1,0:T(8,128)(2,1)S(1)} %pad_maximum_fusion.refs_0_.refs_4_), channel_id=1, source_target_pairs={{0,1},{1,0},{2,3},{3,2},{4,5},{5,4},{6,7},{7,6},{8,9},{9,8},{10,11... | collective-permute-start | bytes 3145736 | tf_op jit(solution)/shard_map/ppermute | solution.py:32
  107.9 19.2 %collective-permute-start.26 = (f16[144,512]{1,0:T(8,128)(2,1)S(1)}, f16[144,512]{1,0:T(8,128)(2,1)S(1)}, u32[]{:S(2)}, u32[]{:S(2)}) collective-permute-start(f16[144,512]{1,0:T(8,128)(2,1)S(1)} %concatenate.66), channel_id=1, source_target_pairs={{0,8},{8,16},{16,24},{1,9},{9,17},{17,25},{2,10},{10,18},{18,26},{... | collective-permute-start | bytes 442376 | tf_op jit(solution)/shard_map/ppermute | solution.py:38
  113.4 13.7 %collective-permute-start.27 = (f16[144,512]{1,0:T(8,128)(2,1)S(1)}, f16[144,512]{1,0:T(8,128)(2,1)S(1)}, u32[]{:S(2)}, u32[]{:S(2)}) collective-permute-start(f16[144,512]{1,0:T(8,128)(2,1)S(1)} %concatenate.66), channel_id=1, source_target_pairs={{0,16},{8,24},{1,17},{9,25},{2,18},{10,26},{3,19},{11,27},{4,20},{... | collective-permute-start | bytes 442376 | tf_op jit(solution)/shard_map/ppermute | solution.py:38
  117.9 13.4 %collective-permute-start.28 = (f16[144,512]{1,0:T(8,128)(2,1)S(1)}, f16[144,512]{1,0:T(8,128)(2,1)S(1)}, u32[]{:S(2)}, u32[]{:S(2)}) collective-permute-start(f16[144,512]{1,0:T(8,128)(2,1)S(1)} %concatenate.66), channel_id=1, source_target_pairs={{0,24},{1,25},{2,26},{3,27},{4,28},{5,29},{6,30},{7,31}} | collective-permute-start | bytes 442376 | tf_op jit(solution)/shard_map/ppermute | solution.py:38
  119.6 15.2 %collective-permute-start.25 = (bf16[4,256,256]{2,1,0:T(8,128)(2,1)}, bf16[4,256,256]{2,1,0:T(8,128)(2,1)}, u32[]{:S(2)}, u32[]{:S(2)}) collective-permute-start(bf16[4,256,256]{2,1,0:T(8,128)(2,1)} %collective-permute-done.23.refs_2_.refs_6_), channel_id=1, source_target_pairs={{0,1},{1,0},{2,3},{3,2},{4,5},{5,4},{6,7},{7,6},{8,9},{9,8},{10,11... | collective-permute-start | bytes 1572872 | tf_op jit(solution)/shard_map/ppermute | solution.py:32
  121.2 37.1 %collective-permute-start.29 = (bf16[4,256,256]{2,1,0:T(8,128)(2,1)}, bf16[4,256,256]{2,1,0:T(8,128)(2,1)S(1)}, u32[]{:S(2)}, u32[]{:S(2)}) collective-permute-start(bf16[4,256,256]{2,1,0:T(8,128)(2,1)} %collective-permute-done.24.refs_4_.refs_8_), channel_id=1, source_target_pairs={{0,1},{1,0},{2,3},{3,2},{4,5},{5,4},{6,7},{7,6},{8,9},{9,8},{10,11... | collective-permute-start | bytes 1572872 | tf_op jit(solution)/shard_map/ppermute | solution.py:32
  159.4 25.5 %collective-permute-start.34 = (bf16[1024,512]{1,0:T(8,128)(2,1)}, bf16[1024,512]{1,0:T(8,128)(2,1)S(1)}, u32[]{:S(2)}, u32[]{:S(2)}) collective-permute-start(bf16[1024,512]{1,0:T(8,128)(2,1)} %get-tuple-element.243.refs_0_), channel_id=1, source_target_pairs={{0,4},{2,6},{4,0},{6,2},{1,5},{3,7},{5,1},{7,3},{8,12},{10,14},{12... | collective-permute-start | bytes 3145736 | tf_op jit(solution)/shard_map/ppermute | solution.py:32
  160.9 25.2 %collective-permute-start.33 = (bf16[1024,512]{1,0:T(8,128)(2,1)}, bf16[1024,512]{1,0:T(8,128)(2,1)S(1)}, u32[]{:S(2)}, u32[]{:S(2)}) collective-permute-start(bf16[1024,512]{1,0:T(8,128)(2,1)} %get-tuple-element.243.refs_0_), channel_id=1, source_target_pairs={{0,2},{2,0},{4,6},{6,4},{1,3},{3,1},{5,7},{7,5},{8,10},{10,8},{12,... | collective-permute-start | bytes 3145736 | tf_op jit(solution)/shard_map/ppermute | solution.py:32
  202.5 11.4 %collective-permute-start.37 = (f32[1024,512]{1,0:T(8,128)}, f32[1024,512]{1,0:T(8,128)}, u32[]{:S(2)}, u32[]{:S(2)}) collective-permute-start(f32[1024,512]{1,0:T(8,128)} %get-tuple-element.237), channel_id=1, source_target_pairs={{0,2},{2,0},{4,6},{6,4},{1,3},{3,1},{5,7},{7,5},{8,10},{10,8},{12,... | collective-permute-start | bytes 6291464 | tf_op jit(solution)/shard_map/ppermute | solution.py:32
  202.7 41.5 %collective-permute-start.36 = (f32[1024,512]{1,0:T(8,128)}, f32[1024,512]{1,0:T(8,128)}, u32[]{:S(2)}, u32[]{:S(2)}) collective-permute-start(f32[1024,512]{1,0:T(8,128)} %get-tuple-element.231), channel_id=1, source_target_pairs={{0,2},{2,0},{4,6},{6,4},{1,3},{3,1},{5,7},{7,5},{8,10},{10,8},{12,... | collective-permute-start | bytes 6291464 | tf_op jit(solution)/shard_map/ppermute | solution.py:32
  213.9 123.2 %reduce-scatter.6.cloned.1.call-start = ((), (), s32[]{:S(2)}) async-start(), calls=%async_computation.7 | async-start | bytes 2621440 | tf_op jit(solution)/shard_map/reduce_scatter | solution.py:1528
  217.6 26.6 %collective-permute-start.38 = (f16[1024,512]{1,0:T(8,128)(2,1)S(1)}, f16[1024,512]{1,0:T(8,128)(2,1)}, u32[]{:S(2)}, u32[]{:S(2)}) collective-permute-start(f16[1024,512]{1,0:T(8,128)(2,1)S(1)} %multiply_convert_fusion), channel_id=1, source_target_pairs={{0,4},{2,6},{4,0},{6,2},{1,5},{3,7},{5,1},{7,3},{8,12},{10,14},{12... | collective-permute-start | bytes 3145736 | tf_op jit(solution)/shard_map/ppermute | solution.py:32
  236.8 47.0 %collective-permute-start.45 = (bf16[4,4,256,256]{3,2,1,0:T(8,128)(2,1)}, bf16[4,4,256,256]{3,2,1,0:T(8,128)(2,1)}, u32[]{:S(2)}, u32[]{:S(2)}) collective-permute-start(bf16[4,4,256,256]{3,2,1,0:T(8,128)(2,1)} %get-tuple-element.258), channel_id=1, source_target_pairs={{0,1},{1,0},{2,3},{3,2},{4,5},{5,4},{6,7},{7,6},{8,9},{9,8},{10,11... | collective-permute-start | bytes 6291464 | tf_op jit(solution)/shard_map/ppermute | solution.py:32
  258.2 19.8 %collective-permute-start.42 = (f16[144,512]{1,0:T(8,128)(2,1)S(1)}, f16[144,512]{1,0:T(8,128)(2,1)S(1)}, u32[]{:S(2)}, u32[]{:S(2)}) collective-permute-start(f16[144,512]{1,0:T(8,128)(2,1)S(1)} %concatenate.69), channel_id=1, source_target_pairs={{8,0},{16,8},{24,16},{9,1},{17,9},{25,17},{10,2},{18,10},{26,18},{... | collective-permute-start | bytes 442376 | tf_op jit(solution)/shard_map/ppermute | solution.py:38
  259.5 18.6 %collective-permute-start.43 = (f16[144,512]{1,0:T(8,128)(2,1)S(1)}, f16[144,512]{1,0:T(8,128)(2,1)S(1)}, u32[]{:S(2)}, u32[]{:S(2)}) collective-permute-start(f16[144,512]{1,0:T(8,128)(2,1)S(1)} %concatenate.69), channel_id=1, source_target_pairs={{16,0},{24,8},{17,1},{25,9},{18,2},{26,10},{19,3},{27,11},{20,4},{... | collective-permute-start | bytes 442376 | tf_op jit(solution)/shard_map/ppermute | solution.py:38
  260.8 17.2 %collective-permute-start.44 = (f16[144,512]{1,0:T(8,128)(2,1)S(1)}, f16[144,512]{1,0:T(8,128)(2,1)S(1)}, u32[]{:S(2)}, u32[]{:S(2)}) collective-permute-start(f16[144,512]{1,0:T(8,128)(2,1)S(1)} %concatenate.69), channel_id=1, source_target_pairs={{24,0},{25,1},{26,2},{27,3},{28,4},{29,5},{30,6},{31,7}} | collective-permute-start | bytes 442376 | tf_op jit(solution)/shard_map/ppermute | solution.py:38
  283.9 144.2 %reduce-scatter.8.cloned.1.call-start = ((), (), s32[]{:S(2)}) async-start(), calls=%async_computation.8 | async-start | bytes 2621440 | tf_op jit(solution)/shard_map/reduce_scatter | solution.py:1727
  290.3 19.6 %collective-permute-start.46 = (bf16[4,256,256]{2,1,0:T(8,128)(2,1)}, bf16[4,256,256]{2,1,0:T(8,128)(2,1)S(1)}, u32[]{:S(2)}, u32[]{:S(2)}) collective-permute-start(bf16[4,256,256]{2,1,0:T(8,128)(2,1)} %get-tuple-element.279), channel_id=1, source_target_pairs={{0,2},{2,0},{4,6},{6,4},{1,3},{3,1},{5,7},{7,5},{8,10},{10,8},{12,... | collective-permute-start | bytes 1572872 | tf_op jit(solution)/shard_map/ppermute | solution.py:32
  290.3 19.7 %collective-permute-start.47 = (bf16[4,256,256]{2,1,0:T(8,128)(2,1)}, bf16[4,256,256]{2,1,0:T(8,128)(2,1)S(1)}, u32[]{:S(2)}, u32[]{:S(2)}) collective-permute-start(bf16[4,256,256]{2,1,0:T(8,128)(2,1)} %get-tuple-element.280), channel_id=1, source_target_pairs={{0,4},{2,6},{4,0},{6,2},{1,5},{3,7},{5,1},{7,3},{8,12},{10,14},{12... | collective-permute-start | bytes 1572872 | tf_op jit(solution)/shard_map/ppermute | solution.py:32
  292.0 23.7 %collective-permute-start.48 = (bf16[4,256,256]{2,1,0:T(8,128)(2,1)}, bf16[4,256,256]{2,1,0:T(8,128)(2,1)S(1)}, u32[]{:S(2)}, u32[]{:S(2)}) collective-permute-start(bf16[4,256,256]{2,1,0:T(8,128)(2,1)} %get-tuple-element.281), channel_id=1, source_target_pairs={{0,6},{2,4},{4,2},{6,0},{1,7},{3,5},{5,3},{7,1},{8,14},{10,12},{12... | collective-permute-start | bytes 1572872 | tf_op jit(solution)/shard_map/ppermute | solution.py:32
  321.2 10.1 %collective-permute-start.51 = (f32[64,1280]{1,0:T(8,128)S(1)}, f32[64,1280]{1,0:T(8,128)S(1)}, u32[]{:S(2)}, u32[]{:S(2)}) collective-permute-start(f32[64,1280]{1,0:T(8,128)S(1)} %dynamic-slice_bitcast_fusion.1), channel_id=1, source_target_pairs={{0,4},{2,6},{4,0},{6,2},{1,5},{3,7},{5,1},{7,3},{8,12},{10,14},{12... | collective-permute-start | bytes 983048 | tf_op jit(solution)/shard_map/ppermute | solution.py:32
  325.9 11.2 %collective-permute-start.49 = (f32[8,768]{1,0:T(8,128)S(1)}, f32[8,768]{1,0:T(8,128)S(1)}, u32[]{:S(2)}, u32[]{:S(2)}) collective-permute-start(f32[8,768]{1,0:T(8,128)S(1)} %copy-done.56), channel_id=1, source_target_pairs={{8,0},{16,8},{24,16},{9,1},{17,9},{25,17},{10,2},{18,10},{26,18},{... | collective-permute-start | bytes 73736 | tf_op jit(solution)/shard_map/ppermute | solution.py:38
  340.4 17.2 %collective-permute-start.53 = (bf16[64,2048]{1,0:T(8,128)(2,1)S(1)}, bf16[64,2048]{1,0:T(8,128)(2,1)S(1)}, u32[]{:S(2)}, u32[]{:S(2)}) collective-permute-start(bf16[64,2048]{1,0:T(8,128)(2,1)S(1)} %pad_maximum_fusion.1), channel_id=1, source_target_pairs={{0,8},{8,0},{16,24},{24,16},{1,9},{9,1},{17,25},{25,17},{2,10},{10... | collective-permute-start | bytes 786440 | tf_op jit(solution)/shard_map/ppermute | solution.py:32
  357.7 14.1 %collective-permute-start.54 = (bf16[2,256,2048]{2,1,0:T(8,128)(2,1)}, bf16[2,256,2048]{2,1,0:T(8,128)(2,1)}, u32[]{:S(2)}, u32[]{:S(2)}) collective-permute-start(bf16[2,256,2048]{2,1,0:T(8,128)(2,1)} %get-tuple-element.293), channel_id=1, source_target_pairs={{0,2},{2,0},{4,6},{6,4},{1,3},{3,1},{5,7},{7,5},{8,10},{10,8},{12,... | collective-permute-start | bytes 6291464 | tf_op jit(solution)/shard_map/ppermute | solution.py:32
  362.0 15.5 %collective-permute-start.56 = (bf16[64,2048]{1,0:T(8,128)(2,1)S(1)}, bf16[64,2048]{1,0:T(8,128)(2,1)S(1)}, u32[]{:S(2)}, u32[]{:S(2)}) collective-permute-start(bf16[64,2048]{1,0:T(8,128)(2,1)S(1)} %pad_maximum_fusion.2), channel_id=1, source_target_pairs={{0,16},{8,24},{16,0},{24,8},{1,17},{9,25},{17,1},{25,9},{2,18},{10... | collective-permute-start | bytes 786440 | tf_op jit(solution)/shard_map/ppermute | solution.py:32
  383.0 25.8 %collective-permute-start.60 = (bf16[256,2048]{1,0:T(8,128)(2,1)S(1)}, bf16[256,2048]{1,0:T(8,128)(2,1)S(1)}, u32[]{:S(2)}, u32[]{:S(2)}) collective-permute-start(bf16[256,2048]{1,0:T(8,128)(2,1)S(1)} %fusion.1), channel_id=1, source_target_pairs={{0,4},{2,6},{4,0},{6,2},{1,5},{3,7},{5,1},{7,3},{8,12},{10,14},{12... | collective-permute-start | bytes 3145736 | tf_op jit(solution)/shard_map/ppermute | solution.py:32
  384.5 9.1 %collective-permute-start.62 = (bf16[64,2048]{1,0:T(8,128)(2,1)S(1)}, bf16[64,2048]{1,0:T(8,128)(2,1)S(1)}, u32[]{:S(2)}, u32[]{:S(2)}) collective-permute-start(bf16[64,2048]{1,0:T(8,128)(2,1)S(1)} %get-tuple-element.357), channel_id=1, source_target_pairs={{0,1},{1,0},{2,3},{3,2},{4,5},{5,4},{6,7},{7,6},{8,9},{9,8},{10,11... | collective-permute-start | bytes 786440 | tf_op jit(solution)/shard_map/ppermute | solution.py:32
  408.8 13.7 %collective-permute-start.65 = (bf16[2,64,2048]{2,1,0:T(8,128)(2,1)S(1)}, bf16[2,64,2048]{2,1,0:T(8,128)(2,1)S(1)}, u32[]{:S(2)}, u32[]{:S(2)}) collective-permute-start(bf16[2,64,2048]{2,1,0:T(8,128)(2,1)S(1)} %maximum_select_fusion.1), channel_id=1, source_target_pairs={{0,4},{2,6},{4,0},{6,2},{1,5},{3,7},{5,1},{7,3},{8,12},{10,14},{12... | collective-permute-start | bytes 1572872 | tf_op jit(solution)/shard_map/ppermute | solution.py:32
  413.3 13.6 %collective-permute-start.63 = (bf16[256,1024]{1,0:T(8,128)(2,1)S(1)}, bf16[256,1024]{1,0:T(8,128)(2,1)}, u32[]{:S(2)}, u32[]{:S(2)}) collective-permute-start(bf16[256,1024]{1,0:T(8,128)(2,1)S(1)} %dynamic-slice_convert_fusion), channel_id=1, source_target_pairs={{0,1},{1,0},{2,3},{3,2},{4,5},{5,4},{6,7},{7,6},{8,9},{9,8},{10,11... | collective-permute-start | bytes 1572872 | tf_op jit(solution)/shard_map/ppermute | solution.py:32
  432.3 11.8 %collective-permute-start.70 = (bf16[128,512]{1,0:T(8,128)(2,1)S(1)}, bf16[128,512]{1,0:T(8,128)(2,1)S(1)}, u32[]{:S(2)}, u32[]{:S(2)}) collective-permute-start(bf16[128,512]{1,0:T(8,128)(2,1)S(1)} %get-tuple-element.345), channel_id=1, source_target_pairs={{0,2},{2,0},{4,6},{6,4},{1,3},{3,1},{5,7},{7,5},{8,10},{10,8},{12,... | collective-permute-start | bytes 393224 | tf_op jit(solution)/shard_map/ppermute | solution.py:32
  432.3 11.8 %collective-permute-start.71 = (bf16[128,512]{1,0:T(8,128)(2,1)S(1)}, bf16[128,512]{1,0:T(8,128)(2,1)S(1)}, u32[]{:S(2)}, u32[]{:S(2)}) collective-permute-start(bf16[128,512]{1,0:T(8,128)(2,1)S(1)} %get-tuple-element.344), channel_id=1, source_target_pairs={{0,4},{2,6},{4,0},{6,2},{1,5},{3,7},{5,1},{7,3},{8,12},{10,14},{12... | collective-permute-start | bytes 393224 | tf_op jit(solution)/shard_map/ppermute | solution.py:32
  433.6 10.5 %collective-permute-start.72 = (bf16[128,512]{1,0:T(8,128)(2,1)S(1)}, bf16[128,512]{1,0:T(8,128)(2,1)S(1)}, u32[]{:S(2)}, u32[]{:S(2)}) collective-permute-start(bf16[128,512]{1,0:T(8,128)(2,1)S(1)} %get-tuple-element.343), channel_id=1, source_target_pairs={{0,6},{2,4},{4,2},{6,0},{1,7},{3,5},{5,3},{7,1},{8,14},{10,12},{12... | collective-permute-start | bytes 393224 | tf_op jit(solution)/shard_map/ppermute | solution.py:32
  444.1 7.9 %collective-permute-start.69 = (f32[8,256]{1,0:T(8,128)S(1)}, f32[8,256]{1,0:T(8,128)S(1)}, u32[]{:S(2)}, u32[]{:S(2)}) collective-permute-start(f32[8,256]{1,0:T(8,128)S(1)} %add.324), channel_id=1, source_target_pairs={{0,4},{2,6},{4,0},{6,2},{1,5},{3,7},{5,1},{7,3},{8,12},{10,14},{12... | collective-permute-start | bytes 24584 | tf_op jit(solution)/shard_map/ppermute | solution.py:32
  (88 other events, 604.7 us)
Sparse Core Ops, SparseCore 0:
  33.7 45.3 all-gather.3
  80.7 50.6 all-gather.5
  133.0 50.3 all-gather.7
  214.0 46.2 reduce-scatter.3
  284.0 46.5 reduce-scatter.5
  371.9 41.9 reduce-scatter.7
